TPU v7x, 256 devices: a whole 4x4x8 slice. The times are simulated.
256 devices in a mesh: row: 16 (over x, z_lo, core), col: 16 (over y, z_hi).
Axes of the slice: x: 4, y: 4, z: 8 (z_hi: 4, z_lo: 2; z = z_hi * 2 + z_lo), core: 2. Of those that a mesh axis runs over, the one named last changes fastest.
Arguments:
- points: float32 [3, 65536], P(None, ('row', 'col')), may hold values from -1 to 1, as said below
- self_term: float32 [65536], P(('row', 'col')), may hold values from 1 to 2
- solution: float32 [128, 65536], P(None, ('row', 'col')), may hold values from -6 to 6
- residual: float32 [128, 65536], P(None, ('row', 'col')), may hold values from -45 to 45
- direction: float32 [128, 65536], P(None, ('row', 'col')), may hold values from -45 to 45
Outputs:
- solution_next: float32 [128, 65536], P(None, ('row', 'col'))
- residual_next: float32 [128, 65536], P(None, ('row', 'col'))
- direction_next: float32 [128, 65536], P(None, ('row', 'col'))
Inputs may be any that keep to these rules, and one draw needn't show every extreme that they name: Every column of points is a unit vector.
All inputs are finite; a program needn't handle non-finite values.
Results may differ from a plain program's by a relative error of at most 0.00011.
Values sent between devices are 32-bit elements; how exact they have to be, the bound alone decides.
No kernel may reach another device: no remote copies, remote signals or barrier semaphores. Data moves between devices by JAX's collectives and lax.ppermute only.
A program may use at most 128 MiB of HBM per device.

v0:
```python
import math

import jax
import jax.numpy as jnp
from jax import lax
from jax.sharding import PartitionSpec as P


def tile_kernel(source_pts, target_pts, smoothing):
    squared = (source_pts[0][:, None] - target_pts[0][None, :]) ** 2
    squared = squared + (source_pts[1][:, None] - target_pts[1][None, :]) ** 2
    squared = squared + (source_pts[2][:, None] - target_pts[2][None, :]) ** 2
    return 1.0 / jnp.sqrt(squared + smoothing * smoothing)


def make_accumulate(targets, smoothing, shard_len, totals, pieces):
    values, coords = pieces
    shards = values.shape[1] // shard_len
    values_split = values.reshape(values.shape[0], shards, shard_len).transpose(1, 0, 2)
    coords_split = coords.reshape(3, shards, shard_len).transpose(1, 0, 2)

    def one_shard(running, shard_pair):
        shard_vals, shard_pts = shard_pair
        kernel = tile_kernel(shard_pts, targets, smoothing)
        running = running + jnp.dot(
            shard_vals, kernel, precision=lax.Precision.HIGHEST, preferred_element_type=jnp.float32
        )
        return (running, None)

    totals, unused = lax.scan(one_shard, totals, (values_split, coords_split))
    return totals


def on_device(points, self_term, solution, residual, direction):
    shard_len = direction.shape[1]
    systems = direction.shape[0]
    row_count = lax.axis_size("row")
    total = shard_len * row_count * lax.axis_size("col")
    smoothing = 1.0 / math.sqrt(total)
    norm_now = lax.psum(jnp.sum(residual * residual, axis=1), ("row", "col"))
    targets = lax.all_gather(points, "col", axis=1, tiled=True)
    start_totals = jnp.zeros((systems, targets.shape[1]), jnp.float32)
    totals = make_accumulate(
        targets,
        smoothing,
        shard_len,
        start_totals,
        (
            lax.all_gather(direction, "row", axis=1, tiled=True),
            lax.all_gather(points, "row", axis=1, tiled=True),
        ),
    )
    summed = lax.psum_scatter(totals, "col", scatter_dimension=1, tiled=True)
    applied = self_term[None, :] * direction + summed / math.sqrt(total)
    curvature = lax.psum(jnp.sum(direction * applied, axis=1), ("row", "col"))
    step_len = norm_now / (curvature + 1e-06)
    solution_next = solution + step_len[:, None] * direction
    residual_next = residual - step_len[:, None] * applied
    norm_next = lax.psum(jnp.sum(residual_next * residual_next, axis=1), ("row", "col"))
    factor = norm_next / (norm_now + 1e-06)
    direction_next = residual_next + factor[:, None] * direction
    return (solution_next, residual_next, direction_next)


def solution(mesh):
    placed = (
        P(None, ("row", "col")),
        P(("row", "col")),
        P(None, ("row", "col")),
        P(None, ("row", "col")),
        P(None, ("row", "col")),
    )
    return jax.shard_map(
        on_device,
        mesh=mesh,
        in_specs=placed,
        out_specs=(P(None, ("row", "col")), P(None, ("row", "col")), P(None, ("row", "col"))),
        check_vma=False,
    )
```

profile of v0, /device:TPU:1, one launch (start us, length us, event | category | flops | bytes accessed | tf_op | source)
XLA Modules:
  0.0 403.3 jit_solution(5702970183478999386)
XLA Ops:
  7.2 1.7 copy.8
  9.0 41.2 %all_gather.11 = f32[3,4096]{1,0:T(4,128)S(1)} all-gather(f32[3,256]{1,0:T(4,128)} %param.7), channel_id=1, replica_groups=mesh['row'=16,'col'=16] {'col'}, dimensions={1}, use_global_device_ids=true | all-gather | bytes 52224 | tf_op jit(solution)/shard_map/all_gather | solution.py:41
  50.2 27.1 %all_gather.10 = f32[3,4096]{1,0:T(4,128)S(1)} all-gather(f32[3,256]{1,0:T(4,128)} %param.7), channel_id=1, replica_groups=mesh['row'=16,'col'=16] {'row'}, dimensions={1}, use_global_device_ids=true | all-gather | bytes 52224 | tf_op jit(solution)/shard_map/all_gather | solution.py:50
  77.2 88.0 %while.11 = (s32[]{:T(128)}, f32[128,4096]{1,0:T(8,128)S(1)}, f32[16,128,256]{1,2,0:T(8,128)}, f32[16,3,256]{2,1,0:T(4,128)S(1)}, f32[3,4096]{1,0:T(4,128)S(1)}, /*index=5*/s32[]{:T(128)}, s32[]{:T(128)}, s32[]{}, s32[]{}) while((s32[]{:T(128)}, f32[128,4096]{1,0:T(8,128)S(1)}, f32[16,128,256]{1,2,0:T(8,128)}, ...), condition=%wide.region_3.4_spmd.clone, body=%wide.region_2.3_spmd.clone.sunk | while | flops 1621098496 | bytes 4482699 | solution.py:30
  77.3 5.4 %convolution_add_fusion.2 = f32[128,4096]{1,0:T(8,128)S(1)} fusion(f32[128,4096]{1,0:T(8,128)S(1)} %get-tuple-element.128, f32[4096]{0:T(1024)S(1)} %bitcast.31, f32[256]{0:T(256)S(1)} %bitcast.36, f32[4096]{0:T(1024)S(1)} %bitcast.32, f32[256]{0:T(256)S(1)} %bitcast.35, f32[4096]{0:T(1024)S(1)} %bitcast.30, f32[256]{0:T(256)S(1)} %bitcast.34, ...), kind=kOutput, calls=%fused_computation.clone.1 | convolution fusion | flops 1621098496 | bytes 4378113 | tf_op jit(solution)/shard_map/while/body/eval_jaxpr/dot_general | solution.py:25
  82.8 5.4 %convolution_add_fusion.2 = f32[128,4096]{1,0:T(8,128)S(1)} fusion(f32[128,4096]{1,0:T(8,128)S(1)} %get-tuple-element.128, f32[4096]{0:T(1024)S(1)} %bitcast.31, f32[256]{0:T(256)S(1)} %bitcast.36, f32[4096]{0:T(1024)S(1)} %bitcast.32, f32[256]{0:T(256)S(1)} %bitcast.35, f32[4096]{0:T(1024)S(1)} %bitcast.30, f32[256]{0:T(256)S(1)} %bitcast.34, ...), kind=kOutput, calls=%fused_computation.clone.1 | convolution fusion | flops 1621098496 | bytes 4378113 | tf_op jit(solution)/shard_map/while/body/eval_jaxpr/dot_general | solution.py:25
  88.3 5.4 %convolution_add_fusion.2 = f32[128,4096]{1,0:T(8,128)S(1)} fusion(f32[128,4096]{1,0:T(8,128)S(1)} %get-tuple-element.128, f32[4096]{0:T(1024)S(1)} %bitcast.31, f32[256]{0:T(256)S(1)} %bitcast.36, f32[4096]{0:T(1024)S(1)} %bitcast.32, f32[256]{0:T(256)S(1)} %bitcast.35, f32[4096]{0:T(1024)S(1)} %bitcast.30, f32[256]{0:T(256)S(1)} %bitcast.34, ...), kind=kOutput, calls=%fused_computation.clone.1 | convolution fusion | flops 1621098496 | bytes 4378113 | tf_op jit(solution)/shard_map/while/body/eval_jaxpr/dot_general | solution.py:25
  93.8 5.4 %convolution_add_fusion.2 = f32[128,4096]{1,0:T(8,128)S(1)} fusion(f32[128,4096]{1,0:T(8,128)S(1)} %get-tuple-element.128, f32[4096]{0:T(1024)S(1)} %bitcast.31, f32[256]{0:T(256)S(1)} %bitcast.36, f32[4096]{0:T(1024)S(1)} %bitcast.32, f32[256]{0:T(256)S(1)} %bitcast.35, f32[4096]{0:T(1024)S(1)} %bitcast.30, f32[256]{0:T(256)S(1)} %bitcast.34, ...), kind=kOutput, calls=%fused_computation.clone.1 | convolution fusion | flops 1621098496 | bytes 4378113 | tf_op jit(solution)/shard_map/while/body/eval_jaxpr/dot_general | solution.py:25
  99.3 5.4 %convolution_add_fusion.2 = f32[128,4096]{1,0:T(8,128)S(1)} fusion(f32[128,4096]{1,0:T(8,128)S(1)} %get-tuple-element.128, f32[4096]{0:T(1024)S(1)} %bitcast.31, f32[256]{0:T(256)S(1)} %bitcast.36, f32[4096]{0:T(1024)S(1)} %bitcast.32, f32[256]{0:T(256)S(1)} %bitcast.35, f32[4096]{0:T(1024)S(1)} %bitcast.30, f32[256]{0:T(256)S(1)} %bitcast.34, ...), kind=kOutput, calls=%fused_computation.clone.1 | convolution fusion | flops 1621098496 | bytes 4378113 | tf_op jit(solution)/shard_map/while/body/eval_jaxpr/dot_general | solution.py:25
  104.8 5.4 %convolution_add_fusion.2 = f32[128,4096]{1,0:T(8,128)S(1)} fusion(f32[128,4096]{1,0:T(8,128)S(1)} %get-tuple-element.128, f32[4096]{0:T(1024)S(1)} %bitcast.31, f32[256]{0:T(256)S(1)} %bitcast.36, f32[4096]{0:T(1024)S(1)} %bitcast.32, f32[256]{0:T(256)S(1)} %bitcast.35, f32[4096]{0:T(1024)S(1)} %bitcast.30, f32[256]{0:T(256)S(1)} %bitcast.34, ...), kind=kOutput, calls=%fused_computation.clone.1 | convolution fusion | flops 1621098496 | bytes 4378113 | tf_op jit(solution)/shard_map/while/body/eval_jaxpr/dot_general | solution.py:25
  110.3 5.4 %convolution_add_fusion.2 = f32[128,4096]{1,0:T(8,128)S(1)} fusion(f32[128,4096]{1,0:T(8,128)S(1)} %get-tuple-element.128, f32[4096]{0:T(1024)S(1)} %bitcast.31, f32[256]{0:T(256)S(1)} %bitcast.36, f32[4096]{0:T(1024)S(1)} %bitcast.32, f32[256]{0:T(256)S(1)} %bitcast.35, f32[4096]{0:T(1024)S(1)} %bitcast.30, f32[256]{0:T(256)S(1)} %bitcast.34, ...), kind=kOutput, calls=%fused_computation.clone.1 | convolution fusion | flops 1621098496 | bytes 4378113 | tf_op jit(solution)/shard_map/while/body/eval_jaxpr/dot_general | solution.py:25
  115.8 5.4 %convolution_add_fusion.2 = f32[128,4096]{1,0:T(8,128)S(1)} fusion(f32[128,4096]{1,0:T(8,128)S(1)} %get-tuple-element.128, f32[4096]{0:T(1024)S(1)} %bitcast.31, f32[256]{0:T(256)S(1)} %bitcast.36, f32[4096]{0:T(1024)S(1)} %bitcast.32, f32[256]{0:T(256)S(1)} %bitcast.35, f32[4096]{0:T(1024)S(1)} %bitcast.30, f32[256]{0:T(256)S(1)} %bitcast.34, ...), kind=kOutput, calls=%fused_computation.clone.1 | convolution fusion | flops 1621098496 | bytes 4378113 | tf_op jit(solution)/shard_map/while/body/eval_jaxpr/dot_general | solution.py:25
  121.3 5.4 %convolution_add_fusion.2 = f32[128,4096]{1,0:T(8,128)S(1)} fusion(f32[128,4096]{1,0:T(8,128)S(1)} %get-tuple-element.128, f32[4096]{0:T(1024)S(1)} %bitcast.31, f32[256]{0:T(256)S(1)} %bitcast.36, f32[4096]{0:T(1024)S(1)} %bitcast.32, f32[256]{0:T(256)S(1)} %bitcast.35, f32[4096]{0:T(1024)S(1)} %bitcast.30, f32[256]{0:T(256)S(1)} %bitcast.34, ...), kind=kOutput, calls=%fused_computation.clone.1 | convolution fusion | flops 1621098496 | bytes 4378113 | tf_op jit(solution)/shard_map/while/body/eval_jaxpr/dot_general | solution.py:25
  126.8 5.4 %convolution_add_fusion.2 = f32[128,4096]{1,0:T(8,128)S(1)} fusion(f32[128,4096]{1,0:T(8,128)S(1)} %get-tuple-element.128, f32[4096]{0:T(1024)S(1)} %bitcast.31, f32[256]{0:T(256)S(1)} %bitcast.36, f32[4096]{0:T(1024)S(1)} %bitcast.32, f32[256]{0:T(256)S(1)} %bitcast.35, f32[4096]{0:T(1024)S(1)} %bitcast.30, f32[256]{0:T(256)S(1)} %bitcast.34, ...), kind=kOutput, calls=%fused_computation.clone.1 | convolution fusion | flops 1621098496 | bytes 4378113 | tf_op jit(solution)/shard_map/while/body/eval_jaxpr/dot_general | solution.py:25
  132.3 5.4 %convolution_add_fusion.2 = f32[128,4096]{1,0:T(8,128)S(1)} fusion(f32[128,4096]{1,0:T(8,128)S(1)} %get-tuple-element.128, f32[4096]{0:T(1024)S(1)} %bitcast.31, f32[256]{0:T(256)S(1)} %bitcast.36, f32[4096]{0:T(1024)S(1)} %bitcast.32, f32[256]{0:T(256)S(1)} %bitcast.35, f32[4096]{0:T(1024)S(1)} %bitcast.30, f32[256]{0:T(256)S(1)} %bitcast.34, ...), kind=kOutput, calls=%fused_computation.clone.1 | convolution fusion | flops 1621098496 | bytes 4378113 | tf_op jit(solution)/shard_map/while/body/eval_jaxpr/dot_general | solution.py:25
  137.8 5.4 %convolution_add_fusion.2 = f32[128,4096]{1,0:T(8,128)S(1)} fusion(f32[128,4096]{1,0:T(8,128)S(1)} %get-tuple-element.128, f32[4096]{0:T(1024)S(1)} %bitcast.31, f32[256]{0:T(256)S(1)} %bitcast.36, f32[4096]{0:T(1024)S(1)} %bitcast.32, f32[256]{0:T(256)S(1)} %bitcast.35, f32[4096]{0:T(1024)S(1)} %bitcast.30, f32[256]{0:T(256)S(1)} %bitcast.34, ...), kind=kOutput, calls=%fused_computation.clone.1 | convolution fusion | flops 1621098496 | bytes 4378113 | tf_op jit(solution)/shard_map/while/body/eval_jaxpr/dot_general | solution.py:25
  143.3 5.4 %convolution_add_fusion.2 = f32[128,4096]{1,0:T(8,128)S(1)} fusion(f32[128,4096]{1,0:T(8,128)S(1)} %get-tuple-element.128, f32[4096]{0:T(1024)S(1)} %bitcast.31, f32[256]{0:T(256)S(1)} %bitcast.36, f32[4096]{0:T(1024)S(1)} %bitcast.32, f32[256]{0:T(256)S(1)} %bitcast.35, f32[4096]{0:T(1024)S(1)} %bitcast.30, f32[256]{0:T(256)S(1)} %bitcast.34, ...), kind=kOutput, calls=%fused_computation.clone.1 | convolution fusion | flops 1621098496 | bytes 4378113 | tf_op jit(solution)/shard_map/while/body/eval_jaxpr/dot_general | solution.py:25
  148.8 5.4 %convolution_add_fusion.2 = f32[128,4096]{1,0:T(8,128)S(1)} fusion(f32[128,4096]{1,0:T(8,128)S(1)} %get-tuple-element.128, f32[4096]{0:T(1024)S(1)} %bitcast.31, f32[256]{0:T(256)S(1)} %bitcast.36, f32[4096]{0:T(1024)S(1)} %bitcast.32, f32[256]{0:T(256)S(1)} %bitcast.35, f32[4096]{0:T(1024)S(1)} %bitcast.30, f32[256]{0:T(256)S(1)} %bitcast.34, ...), kind=kOutput, calls=%fused_computation.clone.1 | convolution fusion | flops 1621098496 | bytes 4378113 | tf_op jit(solution)/shard_map/while/body/eval_jaxpr/dot_general | solution.py:25
  154.3 5.4 %convolution_add_fusion.2 = f32[128,4096]{1,0:T(8,128)S(1)} fusion(f32[128,4096]{1,0:T(8,128)S(1)} %get-tuple-element.128, f32[4096]{0:T(1024)S(1)} %bitcast.31, f32[256]{0:T(256)S(1)} %bitcast.36, f32[4096]{0:T(1024)S(1)} %bitcast.32, f32[256]{0:T(256)S(1)} %bitcast.35, f32[4096]{0:T(1024)S(1)} %bitcast.30, f32[256]{0:T(256)S(1)} %bitcast.34, ...), kind=kOutput, calls=%fused_computation.clone.1 | convolution fusion | flops 1621098496 | bytes 4378113 | tf_op jit(solution)/shard_map/while/body/eval_jaxpr/dot_general | solution.py:25
  159.8 5.4 %convolution_add_fusion.2 = f32[128,4096]{1,0:T(8,128)S(1)} fusion(f32[128,4096]{1,0:T(8,128)S(1)} %get-tuple-element.128, f32[4096]{0:T(1024)S(1)} %bitcast.31, f32[256]{0:T(256)S(1)} %bitcast.36, f32[4096]{0:T(1024)S(1)} %bitcast.32, f32[256]{0:T(256)S(1)} %bitcast.35, f32[4096]{0:T(1024)S(1)} %bitcast.30, f32[256]{0:T(256)S(1)} %bitcast.34, ...), kind=kOutput, calls=%fused_computation.clone.1 | convolution fusion | flops 1621098496 | bytes 4378113 | tf_op jit(solution)/shard_map/while/body/eval_jaxpr/dot_general | solution.py:25
  166.7 77.4 %reduce-scatter.2.cloned.1.call-done = f32[128,256]{1,0:T(8,128)} async-done(((f32[128,4096]{1,0:T(8,128)}), f32[128,256]{1,0:T(8,128)}) %reduce-scatter.2.cloned.1.call-update) | async-done | bytes 131088 | tf_op jit(solution)/shard_map/reduce_scatter | solution.py:53
  245.2 75.6 %all-reduce = (f32[128]{0:T(128)S(1)}, f32[128]{0:T(128)S(1)}) all-reduce(f32[128]{0:T(128)S(1)} %multiply_reduce_fusion.2, f32[128]{0:T(128)S(1)} %multiply_reduce_fusion.1), channel_id=1, replica_groups=mesh['row'=16,'col'=16] {'row','col'}, use_global_device_ids=true, to_apply=%region_1.0 | all-reduce | flops 256 | bytes 2048 | tf_op jit(solution)/shard_map/psum | solution.py:40
  320.8 1.7 multiply_reduce_fusion
  322.4 73.2 %psum.23 = f32[128]{0:T(128)S(1)} all-reduce(f32[128]{0:T(128)S(1)} %get-tuple-element.66), channel_id=1, replica_groups=mesh['row'=16,'col'=16] {'row','col'}, use_global_device_ids=true, to_apply=%region_8.9 | all-reduce | flops 128 | bytes 1024 | tf_op jit(solution)/shard_map/psum | solution.py:59
  (55 shorter events, 4.1 us)
Async XLA Ops:
  7.2 70.1 %all-gather.2.cloned.1.call-start = ((), (), s32[]{:S(2)}) async-start(), calls=%async_computation.1 | async-start | bytes 2228224 | tf_op jit(solution)/shard_map/all_gather | solution.py:49
  8.9 235.3 %reduce-scatter.2.cloned.1.call-start = ((), (), s32[]{:S(2)}) async-start(), calls=%async_computation.2 | async-start | bytes 2228224 | tf_op jit(solution)/shard_map/reduce_scatter | solution.py:53
  165.2 1.4 copy-start
  165.2 1.4 copy-start.2
  165.2 78.9 %copy-start.1 = (f32[128,256]{1,0:T(8,128)S(1)}, f32[128,256]{1,0:T(8,128)}, u32[]{:S(2)}) copy-start(f32[128,256]{1,0:T(8,128)} %param.11) | copy-start | bytes 393220
  165.3 78.9 %copy-start.5 = (f32[256]{0:T(256)S(1)}, f32[256]{0:T(256)}, u32[]{:S(2)}) copy-start(f32[256]{0:T(256)} %param.8) | copy-start | bytes 3076
  165.3 155.5 %copy-start.4 = (f32[128,256]{1,0:T(8,128)S(1)}, f32[128,256]{1,0:T(8,128)}, u32[]{:S(2)}) copy-start(f32[128,256]{1,0:T(8,128)} %param.9) | copy-start | bytes 393220
  322.4 74.0 %copy-start.3 = (f32[128,256]{1,0:T(8,128)}, f32[128,256]{1,0:T(8,128)S(1)}, u32[]{:S(2)}) copy-start(f32[128,256]{1,0:T(8,128)S(1)} %get-tuple-element.67) | copy-start | bytes 393220
Sparse Core Ops, SparseCore 0:
  10.4 40.7 all-gather.1
  166.7 77.3 reduce-scatter.1
where the time goes:
time: 404 us; the launch traced here: 403 us
  blocking collectives  217 us (54%)
  matrix products  86.5 us (21%)
  waiting for transfers between devices  77.5 us (19%)
  between operations  14.1 us (3%)
    dot_general x16, matrix products, one_shard(): jnp.dot(shard_vals, kernel, precision=lax.Precision.HIGHEST, preferred_el...  86.5 us
    reduce_scatter x1, waiting for transfers between devices, on_device(): summed = lax.psum_scatter(totals, 'col', scatter_dimension=1, tiled=True)  77.4 us
    psum x1, blocking collectives, on_device(): norm_now = lax.psum(jnp.sum(residual * residual, axis=1), ('row', 'col'))  75.6 us
    psum x1, blocking collectives, on_device(): lax.psum(jnp.sum(residual_next * residual_next, axis=1), ('row', 'col'))  73.2 us
    all_gather x1, blocking collectives, on_device(): targets = lax.all_gather(points, 'col', axis=1, tiled=True)  41.2 us
    all_gather x1, blocking collectives, on_device(): lax.all_gather(points, 'row', axis=1, tiled=True)  27.1 us
  transfers between devices with their start and end apart: 2, of which 1 were waited for; matrix products, arithmetic and copies ran while one was open for 0% of the time, Pallas kernels for 0%

commit v1 on v0

v1 whole, which is shorter than its diff:
```python
import functools
import math

import jax
import jax.numpy as jnp
from jax import lax
from jax.experimental import pallas as pl
from jax.experimental.pallas import tpu as pltpu
from jax.sharding import Mesh, PartitionSpec as P

FINE = ("x", "zl", "c", "y", "zh")
SIZES = (4, 2, 2, 4, 4)
SOURCES = ("x", "y")
RING = ("zl", "zh")
PART = 256
WIDE = 1024
LANES = 256


def operator_kernel(smoothing, target_ref, source_ref, out_ref, target_cols, source_rows, weights, tile_a, tile_b):
    target_blocks, _, block = target_ref.shape
    source_blocks = source_ref.shape[0]
    systems = weights.shape[1] // 2
    for b in range(target_blocks):
        target_cols[b * block : (b + 1) * block, :] = jnp.transpose(target_ref[b])
    for b in range(source_blocks):
        rows = slice(b * block, (b + 1) * block)
        values = jnp.transpose(source_ref[b, :systems, :])
        high = values.astype(jnp.bfloat16)
        weights[rows, :systems] = high
        weights[rows, systems:] = (values - high.astype(jnp.float32)).astype(jnp.bfloat16)
        source_rows[:, rows] = source_ref[b, systems:, :]
    targets = target_blocks * block
    across = source_blocks * block // WIDE
    steps = (targets // PART) * across
    tiles = (tile_a, tile_b)

    def make(step, tile):
        first = pl.multiple_of((step // across) * PART, PART)
        column = pl.multiple_of((step % across) * WIDE, WIDE)
        for r in range(0, PART, 16):
            place = [
                jnp.broadcast_to(target_cols[pl.ds(first + r, 16), i : i + 1], (16, LANES)) for i in range(3)
            ]
            for c in range(0, WIDE, LANES):
                lanes = pl.ds(column + c, LANES)
                dx = source_rows[0:1, lanes] - place[0]
                dy = source_rows[1:2, lanes] - place[1]
                dz = source_rows[2:3, lanes] - place[2]
                kernel = lax.rsqrt(dx * dx + dy * dy + (dz * dz + smoothing * smoothing))
                high = kernel.astype(jnp.bfloat16)
                tile[r : r + 16, c : c + LANES] = high
                tile[PART + r : PART + r + 16, c : c + LANES] = (kernel - high.astype(jnp.float32)).astype(
                    jnp.bfloat16
                )

    def multiply(step, tile):
        rows = pl.ds(pl.multiple_of((step // across) * PART, PART), PART)
        column = pl.multiple_of((step % across) * WIDE, WIDE)
        product = jnp.dot(tile[...], weights[pl.ds(column, WIDE), :], preferred_element_type=jnp.float32)
        out_ref[rows, :] += (product[:PART, :systems] + product[PART:, systems:]) + (
            product[:PART, systems:] + product[PART:, :systems]
        )

    out_ref[...] = jnp.zeros_like(out_ref)
    make(0, tile_a)

    def two_steps(pair, carry):
        for half in range(2):
            step = pair * 2 + half
            make(jnp.minimum(step + 1, steps - 1), tiles[1 - half])
            multiply(step, tiles[half])
        return carry

    lax.fori_loop(0, steps // 2, two_steps, 0)


def apply_operator(targets, sources, smoothing):
    target_blocks, coords, block = targets.shape
    source_blocks, rows, _ = sources.shape
    systems = rows - coords
    return pl.pallas_call(
        functools.partial(operator_kernel, smoothing),
        out_shape=jax.ShapeDtypeStruct((target_blocks * block, systems), jnp.float32),
        in_specs=[pl.BlockSpec(memory_space=pltpu.VMEM)] * 2,
        out_specs=pl.BlockSpec(memory_space=pltpu.VMEM),
        scratch_shapes=[
            pltpu.VMEM((target_blocks * block, coords), jnp.float32),
            pltpu.VMEM((coords, source_blocks * block), jnp.float32),
            pltpu.VMEM((source_blocks * block, 2 * systems), jnp.bfloat16),
            pltpu.VMEM((2 * PART, WIDE), jnp.bfloat16),
            pltpu.VMEM((2 * PART, WIDE), jnp.bfloat16),
        ],
        compiler_params=pltpu.CompilerParams(vmem_limit_bytes=40 * 2**20),
        name="operator",
    )(targets, sources)


def column_sums(values):
    half = values.shape[1] // 2
    return jnp.sum(jnp.transpose(values[:, :half] + values[:, half:]), axis=0, keepdims=True)


def products_kernel(scale, parts_ref, self_ref, residual_ref, direction_ref, applied_ref, sums_ref):
    total = parts_ref[0]
    for part in range(1, parts_ref.shape[0]):
        total = total + parts_ref[part]
    direction = direction_ref[...]
    residual = residual_ref[...]
    applied = self_ref[...] * direction + jnp.transpose(total) * scale
    applied_ref[...] = applied
    sums = jnp.concatenate(
        [
            column_sums(residual * residual),
            column_sums(direction * applied),
            column_sums(residual * applied),
            column_sums(applied * applied),
        ],
        axis=1,
    )
    sums_ref[...] = jnp.broadcast_to(sums[None], sums_ref.shape)


def update_kernel(
    sums_ref, solution_ref, residual_ref, direction_ref, applied_ref, solution_out, residual_out, direction_out
):
    systems = solution_ref.shape[0]
    sums = jnp.sum(sums_ref[...], axis=0)
    norm_now, curvature, cross, image = (sums[:, i * systems : (i + 1) * systems] for i in range(4))
    step_len = norm_now / (curvature + 1e-06)
    norm_next = jnp.maximum(norm_now + step_len * (step_len * image - 2.0 * cross), 0.0)
    factor = norm_next / (norm_now + 1e-06)
    step_len = jnp.transpose(jnp.broadcast_to(step_len, (systems, systems)))
    factor = jnp.transpose(jnp.broadcast_to(factor, (systems, systems)))
    for c in range(0, solution_ref.shape[1], systems):
        cols = slice(c, c + systems)
        direction = direction_ref[:, cols]
        residual_next = residual_ref[:, cols] - step_len * applied_ref[:, cols]
        solution_out[:, cols] = solution_ref[:, cols] + step_len * direction
        residual_out[:, cols] = residual_next
        direction_out[:, cols] = residual_next + factor * direction


def on_device(points, self_term, solution, residual, direction):
    systems, block = direction.shape
    total = block * math.prod(SIZES)
    smoothing = 1.0 / math.sqrt(total)
    vmem = pl.BlockSpec(memory_space=pltpu.VMEM)
    coords = jnp.concatenate([points, jnp.zeros((5, block), jnp.float32)], axis=0)
    cores = ("c",) + RING
    group = lax.axis_size(cores)
    targets = lax.all_to_all(jnp.broadcast_to(coords[None], (group,) + coords.shape), cores, 0, 0)
    mine = jnp.concatenate([direction, coords], axis=0)
    planes = lax.axis_size(SOURCES)
    sources = lax.all_to_all(jnp.broadcast_to(mine[None], (planes,) + mine.shape), SOURCES, 0, 0)
    partial = apply_operator(targets, sources, smoothing)
    halves = partial.reshape(2, group // 2, block, systems)
    core = lax.axis_index("c")
    keep = lax.dynamic_index_in_dim(halves, core, 0, keepdims=False)
    give = lax.dynamic_index_in_dim(halves, 1 - core, 0, keepdims=False)
    keep = keep + lax.ppermute(give, "c", [(0, 1), (1, 0)])
    parts = lax.all_to_all(keep, RING, 0, 0)
    devices = math.prod(SIZES)
    applied, sums = pl.pallas_call(
        functools.partial(products_kernel, 1.0 / math.sqrt(total)),
        out_shape=(
            jax.ShapeDtypeStruct((systems, block), jnp.float32),
            jax.ShapeDtypeStruct((devices, 1, 4 * systems), jnp.float32),
        ),
        in_specs=[vmem] * 4,
        out_specs=(vmem, vmem),
        name="products",
    )(parts, self_term[None, :], residual, direction)
    sums = lax.all_to_all(sums, FINE, 0, 0)
    return pl.pallas_call(
        update_kernel,
        out_shape=(jax.ShapeDtypeStruct((systems, block), jnp.float32),) * 3,
        in_specs=[vmem] * 5,
        out_specs=(vmem,) * 3,
        name="update",
    )(sums, solution, residual, direction, applied)


def solution(mesh):
    fine = Mesh(mesh.devices.reshape(SIZES), FINE)
    matrix = P(None, FINE)
    return jax.shard_map(
        on_device,
        mesh=fine,
        in_specs=(matrix, P(FINE), matrix, matrix, matrix),
        out_specs=(matrix, matrix, matrix),
        check_vma=False,
    )
```

time: 404 us -> 168 us (0.42)
  blocking collectives: 217 us -> 59.2 us
  matrix products: 86.5 us -> 0 us
  Pallas kernels: 0 us -> 42.8 us
  waiting for transfers between devices: 77.5 us -> 35.9 us
  starting transfers between devices: 0.08 us -> 22.4 us
  between operations: 14.1 us -> 0.68 us
    psum x2 -> x0, blocking collectives: 149 us -> none  [the longest x1 75.6 us: on_device(): norm_now = lax.psum(jnp.sum(residual * residual, axis=1), ('row', 'col'))]
    dot_general x16 -> x0, matrix products: 86.5 us -> none  [one_shard(): jnp.dot(shard_vals, kernel, precision=lax.Precision.HIGHEST, preferred_el...]
    reduce_scatter x1 -> x0, waiting for transfers between devices: 77.4 us -> none  [on_device(): summed = lax.psum_scatter(totals, 'col', scatter_dimension=1, tiled=True)]
    all_gather x2 -> x0, blocking collectives: 68.3 us -> none  [the longest x1 41.2 us: on_device(): targets = lax.all_gather(points, 'col', axis=1, tiled=True)]
    all_to_all x0 -> x2, blocking collectives: none -> 59.2 us  [the longest x1 31.3 us: on_device(): sums = lax.all_to_all(sums, FINE, 0, 0)]
    pallas_call x0 -> x3, Pallas kernels: none -> 42.8 us  [the longest x1 37.9 us: apply_operator(): pl.pallas_call(functools.partial(operator_kernel, smoothing), out_shape=j...]
    all_to_all x0 -> x2, waiting for transfers between devices: none -> 33.6 us  [the longest x1 27 us: on_device(): lax.all_to_all(jnp.broadcast_to(mine[None], (planes,) + mine.shape), SOUR...]
    all_to_all x0 -> x2, starting transfers between devices: none -> 16.7 us  [the longest x1 9.99 us: on_device(): lax.all_to_all(jnp.broadcast_to(coords[None], (group,) + coords.shape), c...]
  transfers between devices with their start and end apart: 2 -> 3, of which waited for: 1 -> 3; matrix products, arithmetic and copies ran while one was open for 0% -> 1% of each run, Pallas kernels for 0% -> 0%
where the time goes in v1:
time: 168 us
  blocking collectives  59.2 us (35%)
  Pallas kernels  42.8 us (25%)
  waiting for transfers between devices  35.9 us (21%)
  starting transfers between devices  22.4 us (13%)
  local copies, waits for them, and re-layouts  4.37 us (3%)
  other arithmetic  2.33 us (1%)
    pallas_call x1, Pallas kernels, apply_operator(): pl.pallas_call(functools.partial(operator_kernel, smoothing), out_shape=j...  37.9 us
    all_to_all x1, blocking collectives, on_device(): sums = lax.all_to_all(sums, FINE, 0, 0)  31.3 us
    all_to_all x1, blocking collectives, on_device(): parts = lax.all_to_all(keep, RING, 0, 0)  27.9 us
    all_to_all x1, waiting for transfers between devices, on_device(): lax.all_to_all(jnp.broadcast_to(mine[None], (planes,) + mine.shape), SOUR...  27 us
    all_to_all x1, starting transfers between devices, on_device(): lax.all_to_all(jnp.broadcast_to(coords[None], (group,) + coords.shape), c...  9.99 us
    all_to_all x1, starting transfers between devices, on_device(): lax.all_to_all(jnp.broadcast_to(mine[None], (planes,) + mine.shape), SOUR...  6.75 us
    all_to_all x1, waiting for transfers between devices, on_device(): lax.all_to_all(jnp.broadcast_to(coords[None], (group,) + coords.shape), c...  6.67 us
    ppermute x1, starting transfers between devices, on_device(): keep = keep + lax.ppermute(give, 'c', [(0, 1), (1, 0)])  5.61 us
  transfers between devices with their start and end apart: 3, of which 3 were waited for; matrix products, arithmetic and copies ran while one was open for 1% of the time, Pallas kernels for 0%

profile of v1, /device:TPU:1, one launch (start us, length us, event | category | flops | bytes accessed | tf_op | source)
XLA Modules:
  0.0 167.6 jit_solution(11567292379393352399)
XLA Ops:
  0.6 0.7 concatenate.7
  1.3 0.7 broadcast_in_dim.8
  2.0 10.0 %all-to-all-start = ((f32[16,8,256]{2,1,0:T(8,128)}), f32[16,8,256]{2,1,0:T(8,128)S(1)}, u32[]{:S(2)}, u32[]{:S(2)}) async-start(f32[16,8,256]{2,1,0:T(8,128)} %broadcast_in_dim.8), calls=%async_computation | async-start | bytes 262144 | tf_op jit(solution)/shard_map/all_to_all | solution.py:152
  12.0 0.1 pad.3.clone
  12.1 1.0 maximum_maximum_fusion
  13.1 6.7 %all-to-all-done.target_ref = f32[16,8,256]{2,1,0:T(8,128)S(1)} async-done(((f32[16,8,256]{2,1,0:T(8,128)}), f32[16,8,256]{2,1,0:T(8,128)S(1)}, u32[]{:S(2)}, u32[]{:S(2)}) %all-to-all-start) | async-done | bytes 131104 | tf_op jit(solution)/shard_map/all_to_all | solution.py:152
  19.7 1.5 broadcast_in_dim.20
  21.3 6.8 %all-to-all-start.1 = ((f32[16,136,256]{2,1,0:T(8,128)}), f32[16,136,256]{2,1,0:T(8,128)S(1)}, u32[]{:S(2)}, u32[]{:S(2)}) async-start(f32[16,136,256]{2,1,0:T(8,128)} %broadcast_in_dim.20), calls=%async_computation.1 | async-start | bytes 4456448 | tf_op jit(solution)/shard_map/all_to_all | solution.py:155
  28.0 27.0 %all-to-all-done.1.source_ref = f32[16,136,256]{2,1,0:T(8,128)S(1)} async-done(((f32[16,136,256]{2,1,0:T(8,128)}), f32[16,136,256]{2,1,0:T(8,128)S(1)}, u32[]{:S(2)}, u32[]{:S(2)}) %all-to-all-start.1) | async-done | bytes 2228256 | tf_op jit(solution)/shard_map/all_to_all | solution.py:155
  55.0 37.9 %operator.1 = f32[4096,128]{1,0:T(8,128)S(1)} custom-call(f32[16,8,256]{2,1,0:T(8,128)S(1)} %all-to-all-done.target_ref, f32[16,136,256]{2,1,0:T(8,128)S(1)} %all-to-all-done.1.source_ref), custom_call_target="tpu_custom_call" | custom-call | tf_op jit(solution)/shard_map/operator/pallas_call | solution.py:82
  92.9 0.0 copy-start
  92.9 1.3 copy-done
  94.2 0.1 dynamic-slice_bitcast_fusion
  94.3 5.6 %collective-permute-start = (f32[8,256,128]{2,1,0:T(8,128)S(1)}, f32[8,256,128]{2,1,0:T(8,128)S(1)}, u32[]{:S(2)}, u32[]{:S(2)}) collective-permute-start(f32[8,256,128]{2,1,0:T(8,128)S(1)} %dynamic-slice_bitcast_fusion), channel_id=1, source_target_pairs={{0,16},{16,0},{1,17},{17,1},{2,18},{18,2},{3,19},{19,3},{4,20},{20... | collective-permute-start | bytes 3145736 | tf_op jit(solution)/shard_map/ppermute | solution.py:161
  99.9 2.3 %collective-permute-done = f32[8,256,128]{2,1,0:T(8,128)S(1)} collective-permute-done((f32[8,256,128]{2,1,0:T(8,128)S(1)}, f32[8,256,128]{2,1,0:T(8,128)S(1)}, u32[]{:S(2)}, u32[]{:S(2)}) %collective-permute-start) | collective-permute-done | bytes 1048608 | tf_op jit(solution)/shard_map/ppermute | solution.py:161
  102.2 1.3 bitcast_add_fusion
  103.5 27.9 %all_to_all.20.parts_ref = f32[8,256,128]{2,1,0:T(8,128)} all-to-all(f32[8,256,128]{2,1,0:T(8,128)S(1)} %bitcast_add_fusion), channel_id=1, replica_groups=mesh['x'=4,'zl'=2,'c'=2,'y'=4,'zh'=4] {'zl','zh'}, dimensions={0} | all-to-all | bytes 2097152 | tf_op jit(solution)/shard_map/all_to_all | solution.py:162
  131.4 2.4 %products.1 = (f32[128,256]{1,0:T(8,128)}, f32[256,1,512]{2,1,0:T(1,128)}) custom-call(f32[8,256,128]{2,1,0:T(8,128)} %all_to_all.20.parts_ref, f32[1,256]{1,0:T(1,128)} %bitcast.8, f32[128,256]{1,0:T(8,128)} %residual_ref.3, f32[128,256]{1,0:T(8,128)} %direction_ref.3), custom_call_target="tpu_custom_call" | custom-call | tf_op jit(solution)/shard_map/products/pallas_call | solution.py:164
  133.8 31.3 %all_to_all.21.sums_ref = f32[256,1,512]{2,1,0:T(1,128)} all-to-all(f32[256,1,512]{2,1,0:T(1,128)} %get-tuple-element.5), channel_id=1, replica_groups=mesh['x'=4,'zl'=2,'c'=2,'y'=4,'zh'=4] {'x','zl','c','y','zh'}, dimensions={0} | all-to-all | bytes 1048576 | tf_op jit(solution)/shard_map/all_to_all | solution.py:174
  165.1 2.5 %update.1 = (f32[128,256]{1,0:T(8,128)}, f32[128,256]{1,0:T(8,128)}, f32[128,256]{1,0:T(8,128)}) custom-call(f32[256,1,512]{2,1,0:T(1,128)} %all_to_all.21.sums_ref, f32[128,256]{1,0:T(8,128)} %solution_ref.1, f32[128,256]{1,0:T(8,128)} %residual_ref.3, f32[128,256]{1,0:T(8,128)} %direction_ref.3, f32[128,256]{1,0:T(8,128)} %get-tuple-element.6.applied_ref), custom_call_target="tpu_custom_call" | custom-call | tf_op jit(solution)/shard_map/update/pallas_call | solution.py:175
  (1 shorter events, 0.0 us)
Async XLA Ops:
  2.0 17.7 %all-to-all-start = ((f32[16,8,256]{2,1,0:T(8,128)}), f32[16,8,256]{2,1,0:T(8,128)S(1)}, u32[]{:S(2)}, u32[]{:S(2)}) async-start(f32[16,8,256]{2,1,0:T(8,128)} %broadcast_in_dim.8), calls=%async_computation | async-start | bytes 262144 | tf_op jit(solution)/shard_map/all_to_all | solution.py:152
  21.3 33.7 %all-to-all-start.1 = ((f32[16,136,256]{2,1,0:T(8,128)}), f32[16,136,256]{2,1,0:T(8,128)S(1)}, u32[]{:S(2)}, u32[]{:S(2)}) async-start(f32[16,136,256]{2,1,0:T(8,128)} %broadcast_in_dim.20), calls=%async_computation.1 | async-start | bytes 4456448 | tf_op jit(solution)/shard_map/all_to_all | solution.py:155
  92.9 1.4 copy-start
  94.3 7.9 %collective-permute-start = (f32[8,256,128]{2,1,0:T(8,128)S(1)}, f32[8,256,128]{2,1,0:T(8,128)S(1)}, u32[]{:S(2)}, u32[]{:S(2)}) collective-permute-start(f32[8,256,128]{2,1,0:T(8,128)S(1)} %dynamic-slice_bitcast_fusion), channel_id=1, source_target_pairs={{0,16},{16,0},{1,17},{17,1},{2,18},{18,2},{3,19},{19,3},{4,20},{20... | collective-permute-start | bytes 3145736 | tf_op jit(solution)/shard_map/ppermute | solution.py:161

commit v2 on v1

v2 whole, which is shorter than its diff:
```python
import functools
import math

import jax
import jax.numpy as jnp
from jax import lax
from jax.experimental import pallas as pl
from jax.experimental.pallas import tpu as pltpu
from jax.sharding import Mesh, PartitionSpec as P

FINE = ("x", "zl", "c", "y", "zh")
SIZES = (4, 2, 2, 4, 4)
RING = ("zl", "zh")
PLANE = ("x", "c", "y")
PART = 256
LANES = 256
COORDS = 8
VMEM = pl.BlockSpec(memory_space=pltpu.VMEM)
SMEM = pl.BlockSpec(memory_space=pltpu.SMEM)


def shift(value, axes, by):
    size = lax.axis_size(axes)
    return lax.ppermute(value, axes, [(i, (i + by) % size) for i in range(size)])


def ring_index(z):
    return (z % 2) * SIZES[4] + z // 2


def ring_shift(value, by):
    size = lax.axis_size(RING)
    return lax.ppermute(value, RING, [(ring_index(z), ring_index((z + by) % size)) for z in range(size)])


def prepare(groups, weights, rows):
    systems = weights.shape[0] // 2
    at = 0
    for group in groups:
        for b in range(group.shape[0]):
            block = group.shape[2]
            cols = slice(at, at + block)
            values = group[b, :systems, :]
            high = values.astype(jnp.bfloat16)
            weights[:systems, cols] = high
            weights[systems:, cols] = (values - high.astype(jnp.float32)).astype(jnp.bfloat16)
            for i in range(3):
                rows[8 * i : 8 * i + 8, cols] = jnp.broadcast_to(group[b, systems + i : systems + i + 1, :], (8, block))
            at += block


def accumulate(smoothing, wide, weights, rows, columns, out, tile_a, tile_b):
    systems = out.shape[1]
    across = weights.shape[1] // wide
    steps = (out.shape[0] // PART) * across
    tiles = (tile_a, tile_b)

    def make(step, tile):
        first = pl.multiple_of((step // across) * PART, PART)
        column = pl.multiple_of((step % across) * wide, wide)
        for r in range(0, PART, 16):
            place = [jnp.broadcast_to(columns[pl.ds(first + r, 16), i : i + 1], (16, LANES)) for i in range(3)]
            for c in range(0, wide, LANES):
                lanes = pl.ds(column + c, LANES)
                far = [jnp.concatenate([rows[8 * i : 8 * i + 8, lanes]] * 2, axis=0) for i in range(3)]
                dx, dy, dz = (far[i] - place[i] for i in range(3))
                kernel = lax.rsqrt(dx * dx + dy * dy + (dz * dz + smoothing * smoothing))
                high = kernel.astype(jnp.bfloat16)
                low = (kernel - high.astype(jnp.float32)).astype(jnp.bfloat16)
                tile[r : r + 16, c : c + LANES] = high
                tile[PART + r : PART + r + 16, c : c + LANES] = low

    def multiply(step, tile):
        at = pl.ds(pl.multiple_of((step // across) * PART, PART), PART)
        column = pl.multiple_of((step % across) * wide, wide)
        product = lax.dot_general(
            tile[...],
            weights[:, pl.ds(column, wide)],
            (((1,), (1,)), ((), ())),
            preferred_element_type=jnp.float32,
        )
        out[at, :] += (product[:PART, :systems] + product[PART:, systems:]) + (
            product[:PART, systems:] + product[PART:, :systems]
        )

    make(0, tile_a)

    def two_steps(pair, carry):
        for half in range(2):
            step = pair * 2 + half
            make(jnp.minimum(step + 1, steps - 1), tiles[1 - half])
            multiply(step, tiles[half])
        return carry

    lax.fori_loop(0, steps // 2, two_steps, 0)


def bulk_kernel(smoothing, wide, count, started, *refs):
    groups, refs = refs[:count], refs[count:]
    target, refs = refs[0], refs[1:]
    before, refs = (refs[0], refs[1:]) if started else (None, refs)
    out, weights, rows, columns, tile_a, tile_b = refs
    block = target.shape[2]
    for b in range(target.shape[0]):
        columns[b * block : (b + 1) * block, :] = jnp.transpose(target[b])
    prepare(groups, weights, rows)
    out[...] = before[...] if started else jnp.zeros_like(out)
    accumulate(smoothing, wide, weights, rows, columns, out, tile_a, tile_b)


def step_kernel(smoothing, wide, offset, count, arrived, *refs):
    here, refs = refs[0], refs[1:]
    groups, refs = refs[:count], refs[count:]
    if not count:
        weights, rows, refs = refs[0], refs[1], refs[2:]
    target, before, refs = refs[0], refs[1], refs[2:]
    came, refs = (refs[0], refs[1:]) if arrived else (None, refs)
    out, refs = refs[0], refs[1:]
    if count:
        weights, rows, refs = refs[0], refs[1], refs[2:]
        prepare(groups, weights, rows)
    columns, tile_a, tile_b = refs
    length = target.shape[0]
    z = lax.rem(here[0] + offset, length)
    which = lax.rem(z, 2) * (length // 2) + lax.div(z, 2)
    columns[...] = jnp.transpose(target[which])
    block = out.shape[0]
    earlier = before[pl.ds(pl.multiple_of(which * block, block), block), :]
    out[...] = earlier + came[...] if arrived else earlier
    accumulate(smoothing, wide, weights, rows, columns, out, tile_a, tile_b)


def cost(targets, sources, systems):
    return pl.CostEstimate(
        flops=16 * targets * sources * systems, bytes_accessed=4 * targets * systems, transcendentals=targets * sources
    )


def bulk(groups, targets, before, smoothing, wide=1024):
    ring, coords, block = targets.shape
    systems = groups[0].shape[1] - coords
    sources = sum(g.shape[0] for g in groups) * block
    started = before is not None
    return pl.pallas_call(
        functools.partial(bulk_kernel, smoothing, wide, len(groups), started),
        out_shape=jax.ShapeDtypeStruct((ring * block, systems), jnp.float32),
        in_specs=[VMEM] * (len(groups) + 1 + started),
        out_specs=VMEM,
        scratch_shapes=[
            pltpu.VMEM((2 * systems, sources), jnp.bfloat16),
            pltpu.VMEM((24, sources), jnp.float32),
            pltpu.VMEM((ring * block, coords), jnp.float32),
            pltpu.VMEM((2 * PART, wide), jnp.bfloat16),
            pltpu.VMEM((2 * PART, wide), jnp.bfloat16),
        ],
        compiler_params=pltpu.CompilerParams(vmem_limit_bytes=24 * 2**20),
        cost_estimate=cost(ring * block, sources, systems),
        name="bulk",
    )(*groups, targets, *([before] if started else []))


def ring_step(here, offset, groups, prepared, targets, before, arrived, smoothing, wide=512):
    ring, coords, block = targets.shape
    systems = before.shape[1]
    sources = prepared[0].shape[1] if prepared else sum(g.shape[0] for g in groups) * block
    came = [] if arrived is None else [arrived]
    outs = [jax.ShapeDtypeStruct((block, systems), jnp.float32)]
    if groups:
        outs += [
            jax.ShapeDtypeStruct((2 * systems, sources), jnp.bfloat16),
            jax.ShapeDtypeStruct((24, sources), jnp.float32),
        ]
    operands = [*groups, *prepared, targets, before, *came]
    return pl.pallas_call(
        functools.partial(step_kernel, smoothing, wide, offset % ring, len(groups), bool(came)),
        out_shape=outs,
        in_specs=[SMEM] + [VMEM] * len(operands),
        out_specs=[VMEM] * len(outs),
        scratch_shapes=[
            pltpu.VMEM((block, coords), jnp.float32),
            pltpu.VMEM((2 * PART, wide), jnp.bfloat16),
            pltpu.VMEM((2 * PART, wide), jnp.bfloat16),
        ],
        compiler_params=pltpu.CompilerParams(vmem_limit_bytes=24 * 2**20),
        cost_estimate=cost(block, sources, systems),
        name="ring_step",
    )(here, *operands)


def column_sums(values):
    half = values.shape[1] // 2
    return jnp.sum(jnp.transpose(values[:, :half] + values[:, half:]), axis=0, keepdims=True)


def products_kernel(scale, own, up, down, self_term, residual_ref, direction_ref, applied_ref, sums_ref):
    total = (own[...] + up[...]) + down[...]
    direction = direction_ref[...]
    residual = residual_ref[...]
    applied = self_term[...] * direction + jnp.transpose(total) * scale
    applied_ref[...] = applied
    sums = jnp.concatenate(
        [
            column_sums(residual * residual),
            column_sums(direction * applied),
            column_sums(residual * applied),
            column_sums(applied * applied),
        ],
        axis=1,
    )
    sums_ref[...] = jnp.broadcast_to(sums[None], sums_ref.shape)


def spread_kernel(parts, out):
    out[...] = jnp.broadcast_to(jnp.sum(parts[...], axis=0, keepdims=True), out.shape)


def update_kernel(
    sums_ref, solution_ref, residual_ref, direction_ref, applied_ref, solution_out, residual_out, direction_out
):
    systems = solution_ref.shape[0]
    sums = jnp.sum(sums_ref[...], axis=0)
    norm_now, curvature, cross, image = (sums[:, i * systems : (i + 1) * systems] for i in range(4))
    step_len = norm_now / (curvature + 1e-06)
    norm_next = jnp.maximum(norm_now + step_len * (step_len * image - 2.0 * cross), 0.0)
    factor = norm_next / (norm_now + 1e-06)
    step_len = jnp.transpose(jnp.broadcast_to(step_len, (systems, systems)))
    factor = jnp.transpose(jnp.broadcast_to(factor, (systems, systems)))
    for c in range(0, solution_ref.shape[1], systems):
        cols = slice(c, c + systems)
        direction = direction_ref[:, cols]
        residual_next = residual_ref[:, cols] - step_len * applied_ref[:, cols]
        solution_out[:, cols] = solution_ref[:, cols] + step_len * direction
        residual_out[:, cols] = residual_next
        direction_out[:, cols] = residual_next + factor * direction


def on_device(points, self_term, solution, residual, direction):
    systems, block = direction.shape
    total = block * math.prod(SIZES)
    smoothing = 1.0 / math.sqrt(total)
    ring = lax.axis_size(RING)
    here = jnp.reshape(lax.axis_index("zh") * 2 + lax.axis_index("zl"), (1,))
    small = pltpu.CompilerParams(vmem_limit_bytes=16 * 2**20)

    mine = jnp.concatenate([direction, points, jnp.zeros((COORDS - 3, block), jnp.float32)], axis=0)
    coords = jnp.concatenate([points, jnp.zeros((COORDS - 3, block), jnp.float32)], axis=0)
    line = jnp.stack([mine, shift(mine, "x", 1), shift(mine, "x", -1), shift(mine, "x", 2)])
    targets = lax.all_to_all(jnp.broadcast_to(coords[None], (ring,) + coords.shape), RING, 0, 0)
    above, below = shift(line, "y", 1), shift(line, "y", -1)
    sums = bulk([line, shift(line, "c", 1)], targets, None, smoothing)
    sums, above, below = lax.optimization_barrier((sums, above, below))
    far = [shift(above[:2], "y", 1), shift(below[2:], "y", -1)]
    sums = bulk([above, shift(above, "c", 1)], targets, sums, smoothing)
    last = [below, *far]
    last += [shift(part, "c", 1) for part in last]

    up, *prepared = ring_step(here, 4, last, [], targets, sums, None, smoothing)
    up = ring_shift(up, 1)
    (down,) = ring_step(here, -3, [], prepared, targets, sums, None, smoothing)
    down = ring_shift(down, -1)
    for away in (3, 2, 1):
        (up,) = ring_step(here, away, [], prepared, targets, sums, up, smoothing)
        up = ring_shift(up, 1)
        if away > 1:
            (down,) = ring_step(here, 1 - away, [], prepared, targets, sums, down, smoothing)
            down = ring_shift(down, -1)
    (own,) = ring_step(here, 0, [], prepared, targets, sums, None, smoothing)

    applied, shares = pl.pallas_call(
        functools.partial(products_kernel, 1.0 / math.sqrt(total)),
        out_shape=(
            jax.ShapeDtypeStruct((systems, block), jnp.float32),
            jax.ShapeDtypeStruct((lax.axis_size(PLANE), 1, 4 * systems), jnp.float32),
        ),
        in_specs=[VMEM] * 6,
        out_specs=(VMEM, VMEM),
        compiler_params=small,
        name="products",
    )(own, up, down, self_term[None, :], residual, direction)
    shares = pl.pallas_call(
        spread_kernel,
        out_shape=jax.ShapeDtypeStruct((ring, 1, 4 * systems), jnp.float32),
        in_specs=[VMEM],
        out_specs=VMEM,
        compiler_params=small,
        name="spread",
    )(lax.all_to_all(shares, PLANE, 0, 0))
    return pl.pallas_call(
        update_kernel,
        out_shape=(jax.ShapeDtypeStruct((systems, block), jnp.float32),) * 3,
        in_specs=[VMEM] * 5,
        out_specs=(VMEM,) * 3,
        compiler_params=small,
        name="update",
    )(lax.all_to_all(shares, RING, 0, 0), solution, residual, direction, applied)


def solution(mesh):
    fine = Mesh(mesh.devices.reshape(SIZES), FINE)
    matrix = P(None, FINE)
    return jax.shard_map(
        on_device,
        mesh=fine,
        in_specs=(matrix, P(FINE), matrix, matrix, matrix),
        out_specs=(matrix, matrix, matrix),
        check_vma=False,
    )
```

time: 168 us -> 131 us (0.78)
  blocking collectives: 59.2 us -> 28.1 us
  waiting for transfers between devices: 35.9 us -> 18.3 us
  starting transfers between devices: 22.4 us -> 33.5 us
  Pallas kernels: 42.8 us -> 46.5 us
    all_to_all x2, blocking collectives: 59.2 us -> 28.1 us  [the longest x1 15.1 us: on_device(): lax.all_to_all(shares, PLANE, 0, 0)]
    all_to_all x2 -> x1, waiting for transfers between devices: 33.6 us -> 4.02 us  [on_device(): lax.all_to_all(jnp.broadcast_to(coords[None], (ring,) + coords.shape), RI...]
    ppermute x1 -> x19, starting transfers between devices: 5.61 us -> 25.3 us  [the longest x12 16.6 us: shift(): lax.ppermute(value, axes, [(i, (i + by) % size) for i in range(size)])]
    ppermute x1 -> x19, waiting for transfers between devices: 2.29 us -> 14.3 us  [the longest x12 11.9 us: shift(): lax.ppermute(value, axes, [(i, (i + by) % size) for i in range(size)])]
    all_to_all x2 -> x1, starting transfers between devices: 16.7 us -> 8.19 us  [on_device(): lax.all_to_all(jnp.broadcast_to(coords[None], (ring,) + coords.shape), RI...]
    pallas_call x1 -> x11, Pallas kernels: 37.9 us -> 45.4 us  [the longest x8 24.6 us: ring_step(): pl.pallas_call(functools.partial(step_kernel, smoothing, wide, offset % r...]
    pallas_call x1, Pallas kernels: 2.38 us -> 0.23 us  [on_device(): pl.pallas_call(functools.partial(products_kernel, 1.0 / math.sqrt(total))...]
  transfers between devices with their start and end apart: 3 -> 20, of which waited for: 3 -> 8; matrix products, arithmetic and copies ran while one was open for 1% -> 2% of each run, Pallas kernels for 0% -> 32%
where the time goes in v2:
time: 131 us
  Pallas kernels  46.5 us (35%)
  starting transfers between devices  33.5 us (26%)
  blocking collectives  28.1 us (21%)
  waiting for transfers between devices  18.3 us (14%)
  local copies, waits for them, and re-layouts  2.88 us (2%)
    pallas_call x8, Pallas kernels, ring_step(): pl.pallas_call(functools.partial(step_kernel, smoothing, wide, offset % r...  24.6 us
    pallas_call x2, Pallas kernels, bulk(): pl.pallas_call(functools.partial(bulk_kernel, smoothing, wide, len(groups...  20.8 us
    ppermute x12, starting transfers between devices, shift(): lax.ppermute(value, axes, [(i, (i + by) % size) for i in range(size)])  16.6 us
    all_to_all x1, blocking collectives, on_device(): lax.all_to_all(shares, PLANE, 0, 0)  15.1 us
    all_to_all x1, blocking collectives, on_device(): lax.all_to_all(shares, RING, 0, 0)  13 us
    ppermute x12, waiting for transfers between devices, shift(): lax.ppermute(value, axes, [(i, (i + by) % size) for i in range(size)])  11.9 us
    ppermute x7, starting transfers between devices, ring_shift(): lax.ppermute(value, RING, [(ring_index(z), ring_index((z + by) % size)) f...  8.76 us
    all_to_all x1, starting transfers between devices, on_device(): lax.all_to_all(jnp.broadcast_to(coords[None], (ring,) + coords.shape), RI...  8.19 us
  transfers between devices with their start and end apart: 20, of which 8 were waited for; matrix products, arithmetic and copies ran while one was open for 2% of the time, Pallas kernels for 32%

profile of v2, /device:TPU:1, one launch (start us, length us, event | category | flops | bytes accessed | tf_op | source)
XLA Modules:
  0.0 131.2 jit_solution(12678146600838904095)
XLA Ops:
  1.7 3.4 %collective-permute-start.1 = (f32[136,256]{1,0:T(8,128)S(1)}, f32[136,256]{1,0:T(8,128)S(1)}, u32[]{:S(2)}, u32[]{:S(2)}) collective-permute-start(f32[136,256]{1,0:T(8,128)S(1)} %get-tuple-element.20), channel_id=1, source_target_pairs={{0,192},{64,0},{128,64},{192,128},{1,193},{65,1},{129,65},{193,129... | collective-permute-start | bytes 417800 | tf_op jit(solution)/shard_map/ppermute | solution.py:24
  5.1 1.7 %collective-permute-start.2 = (f32[136,256]{1,0:T(8,128)S(1)}, f32[136,256]{1,0:T(8,128)S(1)}, u32[]{:S(2)}, u32[]{:S(2)}) collective-permute-start(f32[136,256]{1,0:T(8,128)S(1)} %get-tuple-element.20), channel_id=1, source_target_pairs={{0,128},{64,192},{128,0},{192,64},{1,129},{65,193},{129,1},{193,65... | collective-permute-start | bytes 417800 | tf_op jit(solution)/shard_map/ppermute | solution.py:24
  7.5 4.9 %collective-permute-done = f32[136,256]{1,0:T(8,128)S(1)} collective-permute-done((f32[136,256]{1,0:T(8,128)S(1)}, f32[136,256]{1,0:T(8,128)S(1)}, u32[]{:S(2)}, u32[]{:S(2)}) %collective-permute-start) | collective-permute-done | bytes 139296 | tf_op jit(solution)/shard_map/ppermute | solution.py:24
  12.6 2.9 %collective-permute-start.3 = (f32[4,136,256]{2,1,0:T(8,128)S(1)}, f32[4,136,256]{2,1,0:T(8,128)S(1)}, u32[]{:S(2)}, u32[]{:S(2)}) collective-permute-start(f32[4,136,256]{2,1,0:T(8,128)S(1)} %pad_maximum_fusion.refs_0_), channel_id=1, source_target_pairs={{0,16},{16,0},{1,17},{17,1},{2,18},{18,2},{3,19},{19,3},{4,20},{20... | collective-permute-start | bytes 1671176 | tf_op jit(solution)/shard_map/ppermute | solution.py:24
  16.9 8.2 %all-to-all-start = ((f32[8,8,256]{2,1,0:T(8,128)}), f32[8,8,256]{2,1,0:T(8,128)S(1)}, u32[]{:S(2)}, u32[]{:S(2)}) async-start(f32[8,8,256]{2,1,0:T(8,128)} %broadcast_in_dim.4), calls=%async_computation | async-start | bytes 131072 | tf_op jit(solution)/shard_map/all_to_all | solution.py:248
  25.0 2.7 %collective-permute-start.5 = (f32[4,136,256]{2,1,0:T(8,128)S(1)}, f32[4,136,256]{2,1,0:T(8,128)S(1)}, u32[]{:S(2)}, u32[]{:S(2)}) collective-permute-start(f32[4,136,256]{2,1,0:T(8,128)S(1)} %pad_maximum_fusion.refs_0_), channel_id=1, source_target_pairs={{0,12},{4,0},{8,4},{12,8},{1,13},{5,1},{9,5},{13,9},{2,14},{6,2},{... | collective-permute-start | bytes 1671176 | tf_op jit(solution)/shard_map/ppermute | solution.py:24
  27.8 4.0 %all-to-all-done.refs_2_.refs_7_.refs_3_ = f32[8,8,256]{2,1,0:T(8,128)S(1)} async-done(((f32[8,8,256]{2,1,0:T(8,128)}), f32[8,8,256]{2,1,0:T(8,128)S(1)}, u32[]{:S(2)}, u32[]{:S(2)}) %all-to-all-start) | async-done | bytes 65568 | tf_op jit(solution)/shard_map/all_to_all | solution.py:248
  31.8 10.4 %bulk.2.refs_3_ = f32[2048,128]{1,0:T(8,128)S(1)} custom-call(f32[4,136,256]{2,1,0:T(8,128)S(1)} %pad_maximum_fusion.refs_0_, f32[4,136,256]{2,1,0:T(8,128)S(1)} %collective-permute-done.3.refs_1_, f32[8,8,256]{2,1,0:T(8,128)S(1)} %all-to-all-done.refs_2_.refs_7_.refs_3_), custom_call_target="tpu_custom_call" | custom-call | flops 8589934592 | bytes 1048576 | tf_op jit(solution)/shard_map/bulk/pallas_call | solution.py:144
  46.3 1.8 %collective-permute-start.7 = (f32[2,136,256]{2,1,0:T(8,128)}, f32[2,136,256]{2,1,0:T(8,128)S(1)}, u32[]{:S(2)}, u32[]{:S(2)}) collective-permute-start(f32[2,136,256]{2,1,0:T(8,128)} %slice.7), channel_id=1, source_target_pairs={{0,12},{4,0},{8,4},{12,8},{1,13},{5,1},{9,5},{13,9},{2,14},{6,2},{... | collective-permute-start | bytes 835592 | tf_op jit(solution)/shard_map/ppermute | solution.py:24
  48.7 5.7 %collective-permute-done.6.refs_2_ = f32[2,136,256]{2,1,0:T(8,128)S(1)} collective-permute-done((f32[2,136,256]{2,1,0:T(8,128)}, f32[2,136,256]{2,1,0:T(8,128)S(1)}, u32[]{:S(2)}, u32[]{:S(2)}) %collective-permute-start.6) | collective-permute-done | bytes 278560 | tf_op jit(solution)/shard_map/ppermute | solution.py:24
  55.6 10.5 %bulk.3.refs_8_.refs_4_ = f32[2048,128]{1,0:T(8,128)S(1)} custom-call(f32[4,136,256]{2,1,0:T(8,128)S(1)} %collective-permute-done.4.refs_0_, f32[4,136,256]{2,1,0:T(8,128)S(1)} %collective-permute-done.11.refs_1_, f32[8,8,256]{2,1,0:T(8,128)S(1)} %all-to-all-done.refs_2_.refs_7_.refs_3_, f32[2048,128]{1,0:T(8,128)S(1)} %bulk.2.refs_3_), custom_call_target="tpu_custom_call" | custom-call | flops 8589934592 | bytes 1048576 | tf_op jit(solution)/shard_map/bulk/pallas_call | solution.py:144
  66.1 3.3 %ring_step.8 = (f32[256,128]{1,0:T(8,128)S(1)}, bf16[256,4096]{1,0:T(8,128)(2,1)S(1)}, f32[24,4096]{1,0:T(8,128)S(1)}) custom-call(s32[1]{0:T(128)} %bitcast.refs_0_, f32[4,136,256]{2,1,0:T(8,128)S(1)} %collective-permute-done.5.refs_1_, f32[2,136,256]{2,1,0:T(8,128)S(1)} %collective-permute-done.6.refs_2_, ...), custom_call_target="tpu_custom_call" | custom-call | flops 2147483648 | bytes 131072 | tf_op jit(solution)/shard_map/ring_step/pallas_call | solution.py:174
  70.7 3.0 %ring_step.13 = f32[256,128]{1,0:T(8,128)S(1)} custom-call(s32[1]{0:T(128)} %bitcast.refs_0_, bf16[256,4096]{1,0:T(8,128)(2,1)S(1)} %get-tuple-element.14.refs_1_, f32[24,4096]{1,0:T(8,128)S(1)} %get-tuple-element.15.refs_2_, f32[8,8,256]{2,1,0:T(8,128)S(1)} %all-to-all-done.refs_2_.refs_7_.refs_3_, f32[2048,128]{1,0:T(8,128)S(1)} %bulk.3.refs_8_.refs_4_), custom_call_target="tpu_custom_call" | custom-call | flops 2147483648 | bytes 131072 | tf_op jit(solution)/shard_map/ring_step/pallas_call | solution.py:174
  75.7 3.0 %ring_step.10 = f32[256,128]{1,0:T(8,128)S(1)} custom-call(s32[1]{0:T(128)} %bitcast.refs_0_, bf16[256,4096]{1,0:T(8,128)(2,1)S(1)} %get-tuple-element.14.refs_1_, f32[24,4096]{1,0:T(8,128)S(1)} %get-tuple-element.15.refs_2_, f32[8,8,256]{2,1,0:T(8,128)S(1)} %all-to-all-done.refs_2_.refs_7_.refs_3_, f32[2048,128]{1,0:T(8,128)S(1)} %bulk.3.refs_8_.refs_4_, ...), custom_call_target="tpu_custom_call" | custom-call | flops 2147483648 | bytes 131072 | tf_op jit(solution)/shard_map/ring_step/pallas_call | solution.py:174
  78.8 3.0 %ring_step.14 = f32[256,128]{1,0:T(8,128)S(1)} custom-call(s32[1]{0:T(128)} %bitcast.refs_0_, bf16[256,4096]{1,0:T(8,128)(2,1)S(1)} %get-tuple-element.14.refs_1_, f32[24,4096]{1,0:T(8,128)S(1)} %get-tuple-element.15.refs_2_, f32[8,8,256]{2,1,0:T(8,128)S(1)} %all-to-all-done.refs_2_.refs_7_.refs_3_, f32[2048,128]{1,0:T(8,128)S(1)} %bulk.3.refs_8_.refs_4_, ...), custom_call_target="tpu_custom_call" | custom-call | flops 2147483648 | bytes 131072 | tf_op jit(solution)/shard_map/ring_step/pallas_call | solution.py:174
  81.9 2.7 %collective-permute-start.17 = (f32[256,128]{1,0:T(8,128)S(1)}, f32[256,128]{1,0:T(8,128)S(1)}, u32[]{:S(2)}, u32[]{:S(2)}) collective-permute-start(f32[256,128]{1,0:T(8,128)S(1)} %ring_step.14), channel_id=1, source_target_pairs={{0,35},{32,0},{1,32},{33,1},{2,33},{34,2},{3,34},{35,3},{4,39},{36... | collective-permute-start | bytes 393224 | tf_op jit(solution)/shard_map/ppermute | solution.py:33
  84.6 3.0 %ring_step.11 = f32[256,128]{1,0:T(8,128)S(1)} custom-call(s32[1]{0:T(128)} %bitcast.refs_0_, bf16[256,4096]{1,0:T(8,128)(2,1)S(1)} %get-tuple-element.14.refs_1_, f32[24,4096]{1,0:T(8,128)S(1)} %get-tuple-element.15.refs_2_, f32[8,8,256]{2,1,0:T(8,128)S(1)} %all-to-all-done.refs_2_.refs_7_.refs_3_, f32[2048,128]{1,0:T(8,128)S(1)} %bulk.3.refs_8_.refs_4_, ...), custom_call_target="tpu_custom_call" | custom-call | flops 2147483648 | bytes 131072 | tf_op jit(solution)/shard_map/ring_step/pallas_call | solution.py:174
  87.7 3.0 %ring_step.15 = f32[256,128]{1,0:T(8,128)S(1)} custom-call(s32[1]{0:T(128)} %bitcast.refs_0_, bf16[256,4096]{1,0:T(8,128)(2,1)S(1)} %get-tuple-element.14.refs_1_, f32[24,4096]{1,0:T(8,128)S(1)} %get-tuple-element.15.refs_2_, f32[8,8,256]{2,1,0:T(8,128)S(1)} %all-to-all-done.refs_2_.refs_7_.refs_3_, f32[2048,128]{1,0:T(8,128)S(1)} %bulk.3.refs_8_.refs_4_, ...), custom_call_target="tpu_custom_call" | custom-call | flops 2147483648 | bytes 131072 | tf_op jit(solution)/shard_map/ring_step/pallas_call | solution.py:174
  90.8 2.9 %collective-permute-start.18 = (f32[256,128]{1,0:T(8,128)S(1)}, f32[256,128]{1,0:T(8,128)S(1)}, u32[]{:S(2)}, u32[]{:S(2)}) collective-permute-start(f32[256,128]{1,0:T(8,128)S(1)} %ring_step.15), channel_id=1, source_target_pairs={{0,35},{32,0},{1,32},{33,1},{2,33},{34,2},{3,34},{35,3},{4,39},{36... | collective-permute-start | bytes 393224 | tf_op jit(solution)/shard_map/ppermute | solution.py:33
  93.7 3.0 %ring_step.12 = f32[256,128]{1,0:T(8,128)S(1)} custom-call(s32[1]{0:T(128)} %bitcast.refs_0_, bf16[256,4096]{1,0:T(8,128)(2,1)S(1)} %get-tuple-element.14.refs_1_, f32[24,4096]{1,0:T(8,128)S(1)} %get-tuple-element.15.refs_2_, f32[8,8,256]{2,1,0:T(8,128)S(1)} %all-to-all-done.refs_2_.refs_7_.refs_3_, f32[2048,128]{1,0:T(8,128)S(1)} %bulk.3.refs_8_.refs_4_, ...), custom_call_target="tpu_custom_call" | custom-call | flops 2147483648 | bytes 131072 | tf_op jit(solution)/shard_map/ring_step/pallas_call | solution.py:174
  96.9 3.0 %ring_step.9.own = f32[256,128]{1,0:T(8,128)S(1)} custom-call(s32[1]{0:T(128)} %bitcast.refs_0_, bf16[256,4096]{1,0:T(8,128)(2,1)S(1)} %get-tuple-element.14.refs_1_, f32[24,4096]{1,0:T(8,128)S(1)} %get-tuple-element.15.refs_2_, f32[8,8,256]{2,1,0:T(8,128)S(1)} %all-to-all-done.refs_2_.refs_7_.refs_3_, f32[2048,128]{1,0:T(8,128)S(1)} %bulk.3.refs_8_.refs_4_), custom_call_target="tpu_custom_call" | custom-call | flops 2147483648 | bytes 131072 | tf_op jit(solution)/shard_map/ring_step/pallas_call | solution.py:174
  100.0 2.0 %collective-permute-done.15.up = f32[256,128]{1,0:T(8,128)S(1)} collective-permute-done((f32[256,128]{1,0:T(8,128)S(1)}, f32[256,128]{1,0:T(8,128)S(1)}, u32[]{:S(2)}, u32[]{:S(2)}) %collective-permute-start.15) | collective-permute-done | bytes 131104 | tf_op jit(solution)/shard_map/ppermute | solution.py:33
  102.2 15.1 %all_to_all.15.parts = f32[32,1,512]{2,1,0:T(1,128)S(1)} all-to-all(f32[32,1,512]{2,1,0:T(1,128)S(1)} %get-tuple-element.17), channel_id=1, replica_groups=mesh['x'=4,'zl'=2,'c'=2,'y'=4,'zh'=4] {'x','c','y'}, dimensions={0} | all-to-all | bytes 131072 | tf_op jit(solution)/shard_map/all_to_all | solution.py:287
  117.3 13.0 %all_to_all.16.sums_ref = f32[8,1,512]{2,1,0:T(1,128)S(1)} all-to-all(f32[8,1,512]{2,1,0:T(1,128)S(1)} %spread.1), channel_id=1, replica_groups=mesh['x'=4,'zl'=2,'c'=2,'y'=4,'zh'=4] {'zl','zh'}, dimensions={0} | all-to-all | bytes 32768 | tf_op jit(solution)/shard_map/all_to_all | solution.py:295
  (47 shorter events, 13.8 us)
Async XLA Ops:
  1.7 5.7 %collective-permute-start.1 = (f32[136,256]{1,0:T(8,128)S(1)}, f32[136,256]{1,0:T(8,128)S(1)}, u32[]{:S(2)}, u32[]{:S(2)}) collective-permute-start(f32[136,256]{1,0:T(8,128)S(1)} %get-tuple-element.20), channel_id=1, source_target_pairs={{0,192},{64,0},{128,64},{192,128},{1,193},{65,1},{129,65},{193,129... | collective-permute-start | bytes 417800 | tf_op jit(solution)/shard_map/ppermute | solution.py:24
  5.1 7.2 %collective-permute-start = (f32[136,256]{1,0:T(8,128)S(1)}, f32[136,256]{1,0:T(8,128)S(1)}, u32[]{:S(2)}, u32[]{:S(2)}) collective-permute-start(f32[136,256]{1,0:T(8,128)S(1)} %get-tuple-element.20), channel_id=1, source_target_pairs={{0,64},{64,128},{128,192},{192,0},{1,65},{65,129},{129,193},{193,1... | collective-permute-start | bytes 417800 | tf_op jit(solution)/shard_map/ppermute | solution.py:24
  5.1 7.5 %collective-permute-start.2 = (f32[136,256]{1,0:T(8,128)S(1)}, f32[136,256]{1,0:T(8,128)S(1)}, u32[]{:S(2)}, u32[]{:S(2)}) collective-permute-start(f32[136,256]{1,0:T(8,128)S(1)} %get-tuple-element.20), channel_id=1, source_target_pairs={{0,128},{64,192},{128,0},{192,64},{1,129},{65,193},{129,1},{193,65... | collective-permute-start | bytes 417800 | tf_op jit(solution)/shard_map/ppermute | solution.py:24
  12.6 19.2 %collective-permute-start.3 = (f32[4,136,256]{2,1,0:T(8,128)S(1)}, f32[4,136,256]{2,1,0:T(8,128)S(1)}, u32[]{:S(2)}, u32[]{:S(2)}) collective-permute-start(f32[4,136,256]{2,1,0:T(8,128)S(1)} %pad_maximum_fusion.refs_0_), channel_id=1, source_target_pairs={{0,16},{16,0},{1,17},{17,1},{2,18},{18,2},{3,19},{19,3},{4,20},{20... | collective-permute-start | bytes 1671176 | tf_op jit(solution)/shard_map/ppermute | solution.py:24
  16.9 14.9 %all-to-all-start = ((f32[8,8,256]{2,1,0:T(8,128)}), f32[8,8,256]{2,1,0:T(8,128)S(1)}, u32[]{:S(2)}, u32[]{:S(2)}) async-start(f32[8,8,256]{2,1,0:T(8,128)} %broadcast_in_dim.4), calls=%async_computation | async-start | bytes 131072 | tf_op jit(solution)/shard_map/all_to_all | solution.py:248
  25.0 17.1 %collective-permute-start.5 = (f32[4,136,256]{2,1,0:T(8,128)S(1)}, f32[4,136,256]{2,1,0:T(8,128)S(1)}, u32[]{:S(2)}, u32[]{:S(2)}) collective-permute-start(f32[4,136,256]{2,1,0:T(8,128)S(1)} %pad_maximum_fusion.refs_0_), channel_id=1, source_target_pairs={{0,12},{4,0},{8,4},{12,8},{1,13},{5,1},{9,5},{13,9},{2,14},{6,2},{... | collective-permute-start | bytes 1671176 | tf_op jit(solution)/shard_map/ppermute | solution.py:24
  27.8 14.8 %collective-permute-start.4 = (f32[4,136,256]{2,1,0:T(8,128)S(1)}, f32[4,136,256]{2,1,0:T(8,128)S(1)}, u32[]{:S(2)}, u32[]{:S(2)}) collective-permute-start(f32[4,136,256]{2,1,0:T(8,128)S(1)} %pad_maximum_fusion.refs_0_), channel_id=1, source_target_pairs={{0,4},{4,8},{8,12},{12,0},{1,5},{5,9},{9,13},{13,1},{2,6},{6,10},{... | collective-permute-start | bytes 1671176 | tf_op jit(solution)/shard_map/ppermute | solution.py:24
  42.6 13.0 %collective-permute-start.11 = (f32[4,136,256]{2,1,0:T(8,128)S(1)}, f32[4,136,256]{2,1,0:T(8,128)S(1)}, u32[]{:S(2)}, u32[]{:S(2)}) collective-permute-start(f32[4,136,256]{2,1,0:T(8,128)S(1)} %collective-permute-done.4.refs_0_), channel_id=1, source_target_pairs={{0,16},{16,0},{1,17},{17,1},{2,18},{18,2},{3,19},{19,3},{4,20},{20... | collective-permute-start | bytes 1671176 | tf_op jit(solution)/shard_map/ppermute | solution.py:24
  44.8 9.7 %collective-permute-start.6 = (f32[2,136,256]{2,1,0:T(8,128)}, f32[2,136,256]{2,1,0:T(8,128)S(1)}, u32[]{:S(2)}, u32[]{:S(2)}) collective-permute-start(f32[2,136,256]{2,1,0:T(8,128)} %slice.6), channel_id=1, source_target_pairs={{0,4},{4,8},{8,12},{12,0},{1,5},{5,9},{9,13},{13,1},{2,6},{6,10},{... | collective-permute-start | bytes 835592 | tf_op jit(solution)/shard_map/ppermute | solution.py:24
  46.3 8.9 %collective-permute-start.7 = (f32[2,136,256]{2,1,0:T(8,128)}, f32[2,136,256]{2,1,0:T(8,128)S(1)}, u32[]{:S(2)}, u32[]{:S(2)}) collective-permute-start(f32[2,136,256]{2,1,0:T(8,128)} %slice.7), channel_id=1, source_target_pairs={{0,12},{4,0},{8,4},{12,8},{1,13},{5,1},{9,5},{13,9},{2,14},{6,2},{... | collective-permute-start | bytes 835592 | tf_op jit(solution)/shard_map/ppermute | solution.py:24
  48.2 18.0 %collective-permute-start.8 = (f32[4,136,256]{2,1,0:T(8,128)S(1)}, f32[4,136,256]{2,1,0:T(8,128)S(1)}, u32[]{:S(2)}, u32[]{:S(2)}) collective-permute-start(f32[4,136,256]{2,1,0:T(8,128)S(1)} %collective-permute-done.5.refs_1_), channel_id=1, source_target_pairs={{0,16},{16,0},{1,17},{17,1},{2,18},{18,2},{3,19},{19,3},{4,20},{20... | collective-permute-start | bytes 1671176 | tf_op jit(solution)/shard_map/ppermute | solution.py:24
  54.5 11.6 %collective-permute-start.9 = (f32[2,136,256]{2,1,0:T(8,128)S(1)}, f32[2,136,256]{2,1,0:T(8,128)S(1)}, u32[]{:S(2)}, u32[]{:S(2)}) collective-permute-start(f32[2,136,256]{2,1,0:T(8,128)S(1)} %collective-permute-done.6.refs_2_), channel_id=1, source_target_pairs={{0,16},{16,0},{1,17},{17,1},{2,18},{18,2},{3,19},{19,3},{4,20},{20... | collective-permute-start | bytes 835592 | tf_op jit(solution)/shard_map/ppermute | solution.py:24
  55.3 10.8 %collective-permute-start.10 = (f32[2,136,256]{2,1,0:T(8,128)S(1)}, f32[2,136,256]{2,1,0:T(8,128)S(1)}, u32[]{:S(2)}, u32[]{:S(2)}) collective-permute-start(f32[2,136,256]{2,1,0:T(8,128)S(1)} %collective-permute-done.7.refs_3_), channel_id=1, source_target_pairs={{0,16},{16,0},{1,17},{17,1},{2,18},{18,2},{3,19},{19,3},{4,20},{20... | collective-permute-start | bytes 835592 | tf_op jit(solution)/shard_map/ppermute | solution.py:24
  69.5 6.2 %collective-permute-start.12 = (f32[256,128]{1,0:T(8,128)S(1)}, f32[256,128]{1,0:T(8,128)S(1)}, u32[]{:S(2)}, u32[]{:S(2)}) collective-permute-start(f32[256,128]{1,0:T(8,128)S(1)} %get-tuple-element.16), channel_id=1, source_target_pairs={{0,32},{32,1},{1,33},{33,2},{2,34},{34,3},{3,35},{35,0},{4,36},{36... | collective-permute-start | bytes 393224 | tf_op jit(solution)/shard_map/ppermute | solution.py:33
  73.8 5.0 %collective-permute-start.16 = (f32[256,128]{1,0:T(8,128)S(1)}, f32[256,128]{1,0:T(8,128)S(1)}, u32[]{:S(2)}, u32[]{:S(2)}) collective-permute-start(f32[256,128]{1,0:T(8,128)S(1)} %ring_step.13), channel_id=1, source_target_pairs={{0,35},{32,0},{1,32},{33,1},{2,33},{34,2},{3,34},{35,3},{4,39},{36... | collective-permute-start | bytes 393224 | tf_op jit(solution)/shard_map/ppermute | solution.py:33
  78.7 5.9 %collective-permute-start.13 = (f32[256,128]{1,0:T(8,128)S(1)}, f32[256,128]{1,0:T(8,128)S(1)}, u32[]{:S(2)}, u32[]{:S(2)}) collective-permute-start(f32[256,128]{1,0:T(8,128)S(1)} %ring_step.10), channel_id=1, source_target_pairs={{0,32},{32,1},{1,33},{33,2},{2,34},{34,3},{3,35},{35,0},{4,36},{36... | collective-permute-start | bytes 393224 | tf_op jit(solution)/shard_map/ppermute | solution.py:33
  81.9 5.9 %collective-permute-start.17 = (f32[256,128]{1,0:T(8,128)S(1)}, f32[256,128]{1,0:T(8,128)S(1)}, u32[]{:S(2)}, u32[]{:S(2)}) collective-permute-start(f32[256,128]{1,0:T(8,128)S(1)} %ring_step.14), channel_id=1, source_target_pairs={{0,35},{32,0},{1,32},{33,1},{2,33},{34,2},{3,34},{35,3},{4,39},{36... | collective-permute-start | bytes 393224 | tf_op jit(solution)/shard_map/ppermute | solution.py:33
  87.6 6.1 %collective-permute-start.14 = (f32[256,128]{1,0:T(8,128)S(1)}, f32[256,128]{1,0:T(8,128)S(1)}, u32[]{:S(2)}, u32[]{:S(2)}) collective-permute-start(f32[256,128]{1,0:T(8,128)S(1)} %ring_step.11), channel_id=1, source_target_pairs={{0,32},{32,1},{1,33},{33,2},{2,34},{34,3},{3,35},{35,0},{4,36},{36... | collective-permute-start | bytes 393224 | tf_op jit(solution)/shard_map/ppermute | solution.py:33
  90.8 9.2 %collective-permute-start.18 = (f32[256,128]{1,0:T(8,128)S(1)}, f32[256,128]{1,0:T(8,128)S(1)}, u32[]{:S(2)}, u32[]{:S(2)}) collective-permute-start(f32[256,128]{1,0:T(8,128)S(1)} %ring_step.15), channel_id=1, source_target_pairs={{0,35},{32,0},{1,32},{33,1},{2,33},{34,2},{3,34},{35,3},{4,39},{36... | collective-permute-start | bytes 393224 | tf_op jit(solution)/shard_map/ppermute | solution.py:33
  96.8 5.2 %copy-start = (f32[128,256]{1,0:T(8,128)S(1)}, f32[128,256]{1,0:T(8,128)}, u32[]{:S(2)}) copy-start(f32[128,256]{1,0:T(8,128)} %direction_ref.3) | copy-start | bytes 393220
  96.8 5.1 %copy-start.1 = (f32[128,256]{1,0:T(8,128)S(1)}, f32[128,256]{1,0:T(8,128)}, u32[]{:S(2)}) copy-start(f32[128,256]{1,0:T(8,128)} %residual_ref.3) | copy-start | bytes 393220
  96.8 5.1 %copy-start.3 = (f32[256]{0:T(256)S(1)}, f32[256]{0:T(256)}, u32[]{:S(2)}) copy-start(f32[256]{0:T(256)} %param.6) | copy-start | bytes 3076
  96.8 33.5 %copy-start.2 = (f32[128,256]{1,0:T(8,128)S(1)}, f32[128,256]{1,0:T(8,128)}, u32[]{:S(2)}) copy-start(f32[128,256]{1,0:T(8,128)} %solution_ref.1) | copy-start | bytes 393220
  96.8 5.1 %collective-permute-start.15 = (f32[256,128]{1,0:T(8,128)S(1)}, f32[256,128]{1,0:T(8,128)S(1)}, u32[]{:S(2)}, u32[]{:S(2)}) collective-permute-start(f32[256,128]{1,0:T(8,128)S(1)} %ring_step.12), channel_id=1, source_target_pairs={{0,32},{32,1},{1,33},{33,2},{2,34},{34,3},{3,35},{35,0},{4,36},{36... | collective-permute-start | bytes 393224 | tf_op jit(solution)/shard_map/ppermute | solution.py:33

commit v3 on v2

--- a/solution.py
+++ b/solution.py
@@ -31,6 +31,14 @@
 def ring_shift(value, by):
     size = lax.axis_size(RING)
     return lax.ppermute(value, RING, [(ring_index(z), ring_index((z + by) % size)) for z in range(size)])
+
+
+def pack_kernel(points, direction, mine, coords):
+    systems = direction.shape[0]
+    mine[...] = jnp.zeros_like(mine)
+    mine[:systems, :] = direction[...]
+    mine[systems : systems + 3, :] = points[...]
+    coords[...] = jnp.broadcast_to(mine[systems:, :][None], coords.shape)
 
 
 def prepare(groups, weights, rows):
@@ -242,17 +250,29 @@
     here = jnp.reshape(lax.axis_index("zh") * 2 + lax.axis_index("zl"), (1,))
     small = pltpu.CompilerParams(vmem_limit_bytes=16 * 2**20)
 
-    mine = jnp.concatenate([direction, points, jnp.zeros((COORDS - 3, block), jnp.float32)], axis=0)
-    coords = jnp.concatenate([points, jnp.zeros((COORDS - 3, block), jnp.float32)], axis=0)
-    line = jnp.stack([mine, shift(mine, "x", 1), shift(mine, "x", -1), shift(mine, "x", 2)])
-    targets = lax.all_to_all(jnp.broadcast_to(coords[None], (ring,) + coords.shape), RING, 0, 0)
+    mine, coords = pl.pallas_call(
+        pack_kernel,
+        out_shape=(
+            jax.ShapeDtypeStruct((systems + COORDS, block), jnp.float32),
+            jax.ShapeDtypeStruct((ring, COORDS, block), jnp.float32),
+        ),
+        in_specs=[VMEM] * 2,
+        out_specs=(VMEM, VMEM),
+        compiler_params=small,
+        name="pack",
+    )(points, direction)
+    targets = lax.all_to_all(coords, RING, 0, 0)
+    near = [shift(mine, "x", 1), shift(mine, "x", -1), shift(mine, "x", 2)]
+    targets, *near = lax.optimization_barrier((targets, *near))
+    line = jnp.stack([mine, *near])
     above, below = shift(line, "y", 1), shift(line, "y", -1)
     sums = bulk([line, shift(line, "c", 1)], targets, None, smoothing)
     sums, above, below = lax.optimization_barrier((sums, above, below))
     far = [shift(above[:2], "y", 1), shift(below[2:], "y", -1)]
-    sums = bulk([above, shift(above, "c", 1)], targets, sums, smoothing)
-    last = [below, *far]
-    last += [shift(part, "c", 1) for part in last]
+    copies = [shift(above, "c", 1), shift(below, "c", 1)]
+    sums = bulk([above, below], targets, sums, smoothing)
+    sums, *far = lax.optimization_barrier((sums, *far))
+    last = copies + far + [shift(part, "c", 1) for part in far]
 
     up, *prepared = ring_step(here, 4, last, [], targets, sums, None, smoothing)
     up = ring_shift(up, 1)

time: 131 us -> 122 us (0.931)
  blocking collectives: 28.1 us -> 38.8 us
  waiting for transfers between devices: 18.3 us -> 8.13 us
  starting transfers between devices: 33.5 us -> 23.6 us
    all_to_all x0 -> x1, blocking collectives: none -> 14.6 us  [on_device(): targets = lax.all_to_all(coords, RING, 0, 0)]
    all_to_all x1 -> x0, starting transfers between devices: 8.19 us -> none  [on_device(): lax.all_to_all(jnp.broadcast_to(coords[None], (ring,) + coords.shape), RI...]
    ppermute x12, waiting for transfers between devices: 11.9 us -> 6.03 us  [shift(): lax.ppermute(value, axes, [(i, (i + by) % size) for i in range(size)])]
    all_to_all x1, blocking collectives: 13 us -> 8.95 us  [on_device(): lax.all_to_all(shares, RING, 0, 0)]
    all_to_all x1 -> x0, waiting for transfers between devices: 4.02 us -> none  [on_device(): lax.all_to_all(jnp.broadcast_to(coords[None], (ring,) + coords.shape), RI...]
    unnamed x8 -> x18, local copies, waits for them, and re-layouts: 0.03 us -> 3.82 us
    ppermute x12, starting transfers between devices: 16.6 us -> 15.1 us  [shift(): lax.ppermute(value, axes, [(i, (i + by) % size) for i in range(size)])]
    slice x2, local copies, waits for them, and re-layouts: 1.45 us -> 0.04 us  [on_device(): far = [shift(above[:2], 'y', 1), shift(below[2:], 'y', -1)]]
  transfers between devices with their start and end apart: 20 -> 19, of which waited for: 8 -> 6; matrix products, arithmetic and copies ran while one was open for 2% -> 0% of each run, Pallas kernels for 32% -> 34%
where the time goes in v3:
time: 122 us
  Pallas kernels  46.5 us (38%)
  blocking collectives  38.8 us (32%)
  starting transfers between devices  23.6 us (19%)
  waiting for transfers between devices  8.13 us (7%)
  local copies, waits for them, and re-layouts  3.86 us (3%)
    pallas_call x8, Pallas kernels, ring_step(): pl.pallas_call(functools.partial(step_kernel, smoothing, wide, offset % r...  24.6 us
    pallas_call x2, Pallas kernels, bulk(): pl.pallas_call(functools.partial(bulk_kernel, smoothing, wide, len(groups...  20.7 us
    all_to_all x1, blocking collectives, on_device(): lax.all_to_all(shares, PLANE, 0, 0)  15.3 us
    ppermute x12, starting transfers between devices, shift(): lax.ppermute(value, axes, [(i, (i + by) % size) for i in range(size)])  15.1 us
    all_to_all x1, blocking collectives, on_device(): targets = lax.all_to_all(coords, RING, 0, 0)  14.6 us
    all_to_all x1, blocking collectives, on_device(): lax.all_to_all(shares, RING, 0, 0)  8.95 us
    ppermute x7, starting transfers between devices, ring_shift(): lax.ppermute(value, RING, [(ring_index(z), ring_index((z + by) % size)) f...  8.53 us
    ppermute x12, waiting for transfers between devices, shift(): lax.ppermute(value, axes, [(i, (i + by) % size) for i in range(size)])  6.03 us
  transfers between devices with their start and end apart: 19, of which 6 were waited for; matrix products, arithmetic and copies ran while one was open for 0% of the time, Pallas kernels for 34%

profile of v3, /device:TPU:1, one launch (start us, length us, event | category | flops | bytes accessed | tf_op | source)
XLA Modules:
  0.0 121.8 jit_solution(8354246978115584014)
XLA Ops:
  2.2 3.7 %collective-permute-start.2 = (f32[136,256]{1,0:T(8,128)S(1)}, f32[136,256]{1,0:T(8,128)S(1)}, u32[]{:S(2)}, u32[]{:S(2)}) collective-permute-start(f32[136,256]{1,0:T(8,128)S(1)} %get-tuple-element.20), channel_id=1, source_target_pairs={{0,128},{64,192},{128,0},{192,64},{1,129},{65,193},{129,1},{193,65... | collective-permute-start | bytes 417800 | tf_op jit(solution)/shard_map/ppermute | solution.py:24
  7.4 14.6 %all_to_all.15.refs_2_.refs_7_.refs_3_ = f32[8,8,256]{2,1,0:T(8,128)S(1)} all-to-all(f32[8,8,256]{2,1,0:T(8,128)S(1)} %get-tuple-element.21), channel_id=1, replica_groups=mesh['x'=4,'zl'=2,'c'=2,'y'=4,'zh'=4] {'zl','zh'}, dimensions={0} | all-to-all | bytes 131072 | tf_op jit(solution)/shard_map/all_to_all | solution.py:264
  22.0 3.0 %collective-permute-start.3 = (f32[4,136,256]{2,1,0:T(8,128)S(1)}, f32[4,136,256]{2,1,0:T(8,128)S(1)}, u32[]{:S(2)}, u32[]{:S(2)}) collective-permute-start(f32[4,136,256]{2,1,0:T(8,128)S(1)} %pad_maximum_fusion.refs_0_), channel_id=1, source_target_pairs={{0,16},{16,0},{1,17},{17,1},{2,18},{18,2},{3,19},{19,3},{4,20},{20... | collective-permute-start | bytes 1671176 | tf_op jit(solution)/shard_map/ppermute | solution.py:24
  25.1 2.7 %collective-permute-start.5 = (f32[4,136,256]{2,1,0:T(8,128)S(1)}, f32[4,136,256]{2,1,0:T(8,128)S(1)}, u32[]{:S(2)}, u32[]{:S(2)}) collective-permute-start(f32[4,136,256]{2,1,0:T(8,128)S(1)} %pad_maximum_fusion.refs_0_), channel_id=1, source_target_pairs={{0,12},{4,0},{8,4},{12,8},{1,13},{5,1},{9,5},{13,9},{2,14},{6,2},{... | collective-permute-start | bytes 1671176 | tf_op jit(solution)/shard_map/ppermute | solution.py:24
  27.8 10.4 %bulk.2.refs_3_ = f32[2048,128]{1,0:T(8,128)S(1)} custom-call(f32[4,136,256]{2,1,0:T(8,128)S(1)} %pad_maximum_fusion.refs_0_, f32[4,136,256]{2,1,0:T(8,128)S(1)} %collective-permute-done.3.refs_1_, f32[8,8,256]{2,1,0:T(8,128)S(1)} %all_to_all.15.refs_2_.refs_7_.refs_3_), custom_call_target="tpu_custom_call" | custom-call | flops 8589934592 | bytes 1048576 | tf_op jit(solution)/shard_map/bulk/pallas_call | solution.py:152
  38.2 1.6 %collective-permute-done.5.refs_1_ = f32[4,136,256]{2,1,0:T(8,128)S(1)} collective-permute-done((f32[4,136,256]{2,1,0:T(8,128)S(1)}, f32[4,136,256]{2,1,0:T(8,128)S(1)}, u32[]{:S(2)}, u32[]{:S(2)}) %collective-permute-start.5) | collective-permute-done | bytes 557088 | tf_op jit(solution)/shard_map/ppermute | solution.py:24
  39.8 3.1 %collective-permute-done.4.refs_0_ = f32[4,136,256]{2,1,0:T(8,128)S(1)} collective-permute-done((f32[4,136,256]{2,1,0:T(8,128)S(1)}, f32[4,136,256]{2,1,0:T(8,128)S(1)}, u32[]{:S(2)}, u32[]{:S(2)}) %collective-permute-start.4) | collective-permute-done | bytes 557088 | tf_op jit(solution)/shard_map/ppermute | solution.py:24
  42.9 1.3 %collective-permute-start.6 = (f32[4,136,256]{2,1,0:T(8,128)S(1)}, f32[4,136,256]{2,1,0:T(8,128)S(1)}, u32[]{:S(2)}, u32[]{:S(2)}) collective-permute-start(f32[4,136,256]{2,1,0:T(8,128)S(1)} %collective-permute-done.4.refs_0_), channel_id=1, source_target_pairs={{0,16},{16,0},{1,17},{17,1},{2,18},{18,2},{3,19},{19,3},{4,20},{20... | collective-permute-start | bytes 1671176 | tf_op jit(solution)/shard_map/ppermute | solution.py:24
  44.4 1.5 %collective-permute-start.8 = (f32[2,136,256]{2,1,0:T(8,128)S(1)}, f32[2,136,256]{2,1,0:T(8,128)S(1)}, u32[]{:S(2)}, u32[]{:S(2)}) collective-permute-start(f32[2,136,256]{2,1,0:T(8,128)S(1)} %slice.6), channel_id=1, source_target_pairs={{0,4},{4,8},{8,12},{12,0},{1,5},{5,9},{9,13},{13,1},{2,6},{6,10},{... | collective-permute-start | bytes 835592 | tf_op jit(solution)/shard_map/ppermute | solution.py:24
  45.8 10.3 %bulk.3.refs_8_.refs_4_ = f32[2048,128]{1,0:T(8,128)S(1)} custom-call(f32[4,136,256]{2,1,0:T(8,128)S(1)} %collective-permute-done.4.refs_0_, f32[4,136,256]{2,1,0:T(8,128)S(1)} %collective-permute-done.5.refs_1_, f32[8,8,256]{2,1,0:T(8,128)S(1)} %all_to_all.15.refs_2_.refs_7_.refs_3_, f32[2048,128]{1,0:T(8,128)S(1)} %bulk.2.refs_3_), custom_call_target="tpu_custom_call" | custom-call | flops 8589934592 | bytes 1048576 | tf_op jit(solution)/shard_map/bulk/pallas_call | solution.py:152
  61.0 3.4 %ring_step.8 = (f32[256,128]{1,0:T(8,128)S(1)}, bf16[256,4096]{1,0:T(8,128)(2,1)S(1)}, f32[24,4096]{1,0:T(8,128)S(1)}) custom-call(s32[1]{0:T(128)} %bitcast.refs_0_, f32[4,136,256]{2,1,0:T(8,128)S(1)} %collective-permute-done.6.refs_1_, f32[4,136,256]{2,1,0:T(8,128)S(1)} %collective-permute-done.7.refs_2_, ...), custom_call_target="tpu_custom_call" | custom-call | flops 2147483648 | bytes 131072 | tf_op jit(solution)/shard_map/ring_step/pallas_call | solution.py:182
  65.3 3.0 %ring_step.13 = f32[256,128]{1,0:T(8,128)S(1)} custom-call(s32[1]{0:T(128)} %bitcast.refs_0_, bf16[256,4096]{1,0:T(8,128)(2,1)S(1)} %get-tuple-element.32.refs_1_, f32[24,4096]{1,0:T(8,128)S(1)} %get-tuple-element.33.refs_2_, f32[8,8,256]{2,1,0:T(8,128)S(1)} %all_to_all.15.refs_2_.refs_7_.refs_3_, f32[2048,128]{1,0:T(8,128)S(1)} %copy-done.7), custom_call_target="tpu_custom_call" | custom-call | flops 2147483648 | bytes 131072 | tf_op jit(solution)/shard_map/ring_step/pallas_call | solution.py:182
  68.4 1.9 %collective-permute-start.16 = (f32[256,128]{1,0:T(8,128)S(1)}, f32[256,128]{1,0:T(8,128)S(1)}, u32[]{:S(2)}, u32[]{:S(2)}) collective-permute-start(f32[256,128]{1,0:T(8,128)S(1)} %ring_step.13), channel_id=1, source_target_pairs={{0,35},{32,0},{1,32},{33,1},{2,33},{34,2},{3,34},{35,3},{4,39},{36... | collective-permute-start | bytes 393224 | tf_op jit(solution)/shard_map/ppermute | solution.py:33
  70.4 3.0 %ring_step.10 = f32[256,128]{1,0:T(8,128)S(1)} custom-call(s32[1]{0:T(128)} %bitcast.refs_0_, bf16[256,4096]{1,0:T(8,128)(2,1)S(1)} %get-tuple-element.32.refs_1_, f32[24,4096]{1,0:T(8,128)S(1)} %get-tuple-element.33.refs_2_, f32[8,8,256]{2,1,0:T(8,128)S(1)} %all_to_all.15.refs_2_.refs_7_.refs_3_, f32[2048,128]{1,0:T(8,128)S(1)} %copy-done.7, ...), custom_call_target="tpu_custom_call" | custom-call | flops 2147483648 | bytes 131072 | tf_op jit(solution)/shard_map/ring_step/pallas_call | solution.py:182
  73.5 3.0 %ring_step.14 = f32[256,128]{1,0:T(8,128)S(1)} custom-call(s32[1]{0:T(128)} %bitcast.refs_0_, bf16[256,4096]{1,0:T(8,128)(2,1)S(1)} %get-tuple-element.32.refs_1_, f32[24,4096]{1,0:T(8,128)S(1)} %get-tuple-element.33.refs_2_, f32[8,8,256]{2,1,0:T(8,128)S(1)} %all_to_all.15.refs_2_.refs_7_.refs_3_, f32[2048,128]{1,0:T(8,128)S(1)} %copy-done.7, ...), custom_call_target="tpu_custom_call" | custom-call | flops 2147483648 | bytes 131072 | tf_op jit(solution)/shard_map/ring_step/pallas_call | solution.py:182
  76.6 2.7 %collective-permute-start.17 = (f32[256,128]{1,0:T(8,128)S(1)}, f32[256,128]{1,0:T(8,128)S(1)}, u32[]{:S(2)}, u32[]{:S(2)}) collective-permute-start(f32[256,128]{1,0:T(8,128)S(1)} %ring_step.14), channel_id=1, source_target_pairs={{0,35},{32,0},{1,32},{33,1},{2,33},{34,2},{3,34},{35,3},{4,39},{36... | collective-permute-start | bytes 393224 | tf_op jit(solution)/shard_map/ppermute | solution.py:33
  79.3 3.0 %ring_step.11 = f32[256,128]{1,0:T(8,128)S(1)} custom-call(s32[1]{0:T(128)} %bitcast.refs_0_, bf16[256,4096]{1,0:T(8,128)(2,1)S(1)} %get-tuple-element.32.refs_1_, f32[24,4096]{1,0:T(8,128)S(1)} %get-tuple-element.33.refs_2_, f32[8,8,256]{2,1,0:T(8,128)S(1)} %all_to_all.15.refs_2_.refs_7_.refs_3_, f32[2048,128]{1,0:T(8,128)S(1)} %copy-done.7, ...), custom_call_target="tpu_custom_call" | custom-call | flops 2147483648 | bytes 131072 | tf_op jit(solution)/shard_map/ring_step/pallas_call | solution.py:182
  82.4 3.0 %ring_step.15 = f32[256,128]{1,0:T(8,128)S(1)} custom-call(s32[1]{0:T(128)} %bitcast.refs_0_, bf16[256,4096]{1,0:T(8,128)(2,1)S(1)} %get-tuple-element.32.refs_1_, f32[24,4096]{1,0:T(8,128)S(1)} %get-tuple-element.33.refs_2_, f32[8,8,256]{2,1,0:T(8,128)S(1)} %all_to_all.15.refs_2_.refs_7_.refs_3_, f32[2048,128]{1,0:T(8,128)S(1)} %copy-done.7, ...), custom_call_target="tpu_custom_call" | custom-call | flops 2147483648 | bytes 131072 | tf_op jit(solution)/shard_map/ring_step/pallas_call | solution.py:182
  85.5 2.7 %collective-permute-start.18 = (f32[256,128]{1,0:T(8,128)S(1)}, f32[256,128]{1,0:T(8,128)S(1)}, u32[]{:S(2)}, u32[]{:S(2)}) collective-permute-start(f32[256,128]{1,0:T(8,128)S(1)} %ring_step.15), channel_id=1, source_target_pairs={{0,35},{32,0},{1,32},{33,1},{2,33},{34,2},{3,34},{35,3},{4,39},{36... | collective-permute-start | bytes 393224 | tf_op jit(solution)/shard_map/ppermute | solution.py:33
  88.2 3.0 %ring_step.12 = f32[256,128]{1,0:T(8,128)S(1)} custom-call(s32[1]{0:T(128)} %bitcast.refs_0_, bf16[256,4096]{1,0:T(8,128)(2,1)S(1)} %get-tuple-element.32.refs_1_, f32[24,4096]{1,0:T(8,128)S(1)} %get-tuple-element.33.refs_2_, f32[8,8,256]{2,1,0:T(8,128)S(1)} %all_to_all.15.refs_2_.refs_7_.refs_3_, f32[2048,128]{1,0:T(8,128)S(1)} %copy-done.7, ...), custom_call_target="tpu_custom_call" | custom-call | flops 2147483648 | bytes 131072 | tf_op jit(solution)/shard_map/ring_step/pallas_call | solution.py:182
  91.4 3.0 %ring_step.9.own = f32[256,128]{1,0:T(8,128)S(1)} custom-call(s32[1]{0:T(128)} %bitcast.refs_0_, bf16[256,4096]{1,0:T(8,128)(2,1)S(1)} %get-tuple-element.32.refs_1_, f32[24,4096]{1,0:T(8,128)S(1)} %get-tuple-element.33.refs_2_, f32[8,8,256]{2,1,0:T(8,128)S(1)} %all_to_all.15.refs_2_.refs_7_.refs_3_, f32[2048,128]{1,0:T(8,128)S(1)} %copy-done.8), custom_call_target="tpu_custom_call" | custom-call | flops 2147483648 | bytes 131072 | tf_op jit(solution)/shard_map/ring_step/pallas_call | solution.py:182
  94.5 2.0 %collective-permute-done.15.up = f32[256,128]{1,0:T(8,128)S(1)} collective-permute-done((f32[256,128]{1,0:T(8,128)S(1)}, f32[256,128]{1,0:T(8,128)S(1)}, u32[]{:S(2)}, u32[]{:S(2)}) %collective-permute-start.15) | collective-permute-done | bytes 131104 | tf_op jit(solution)/shard_map/ppermute | solution.py:33
  96.7 15.3 %all_to_all.16.parts = f32[32,1,512]{2,1,0:T(1,128)S(1)} all-to-all(f32[32,1,512]{2,1,0:T(1,128)S(1)} %get-tuple-element.35), channel_id=1, replica_groups=mesh['x'=4,'zl'=2,'c'=2,'y'=4,'zh'=4] {'x','c','y'}, dimensions={0} | all-to-all | bytes 131072 | tf_op jit(solution)/shard_map/all_to_all | solution.py:307
  112.0 9.0 %all_to_all.17.sums_ref = f32[8,1,512]{2,1,0:T(1,128)S(1)} all-to-all(f32[8,1,512]{2,1,0:T(1,128)S(1)} %spread.1), channel_id=1, replica_groups=mesh['x'=4,'zl'=2,'c'=2,'y'=4,'zh'=4] {'zl','zh'}, dimensions={0} | all-to-all | bytes 32768 | tf_op jit(solution)/shard_map/all_to_all | solution.py:315
  (52 shorter events, 10.7 us)
Async XLA Ops:
  2.2 19.7 %collective-permute-start.2 = (f32[136,256]{1,0:T(8,128)S(1)}, f32[136,256]{1,0:T(8,128)S(1)}, u32[]{:S(2)}, u32[]{:S(2)}) collective-permute-start(f32[136,256]{1,0:T(8,128)S(1)} %get-tuple-element.20), channel_id=1, source_target_pairs={{0,128},{64,192},{128,0},{192,64},{1,129},{65,193},{129,1},{193,65... | collective-permute-start | bytes 417800 | tf_op jit(solution)/shard_map/ppermute | solution.py:24
  5.9 16.1 %collective-permute-start.1 = (f32[136,256]{1,0:T(8,128)S(1)}, f32[136,256]{1,0:T(8,128)S(1)}, u32[]{:S(2)}, u32[]{:S(2)}) collective-permute-start(f32[136,256]{1,0:T(8,128)S(1)} %get-tuple-element.20), channel_id=1, source_target_pairs={{0,192},{64,0},{128,64},{192,128},{1,193},{65,1},{129,65},{193,129... | collective-permute-start | bytes 417800 | tf_op jit(solution)/shard_map/ppermute | solution.py:24
  6.8 15.2 %collective-permute-start = (f32[136,256]{1,0:T(8,128)S(1)}, f32[136,256]{1,0:T(8,128)S(1)}, u32[]{:S(2)}, u32[]{:S(2)}) collective-permute-start(f32[136,256]{1,0:T(8,128)S(1)} %get-tuple-element.20), channel_id=1, source_target_pairs={{0,64},{64,128},{128,192},{192,0},{1,65},{65,129},{129,193},{193,1... | collective-permute-start | bytes 417800 | tf_op jit(solution)/shard_map/ppermute | solution.py:24
  22.0 5.8 %collective-permute-start.3 = (f32[4,136,256]{2,1,0:T(8,128)S(1)}, f32[4,136,256]{2,1,0:T(8,128)S(1)}, u32[]{:S(2)}, u32[]{:S(2)}) collective-permute-start(f32[4,136,256]{2,1,0:T(8,128)S(1)} %pad_maximum_fusion.refs_0_), channel_id=1, source_target_pairs={{0,16},{16,0},{1,17},{17,1},{2,18},{18,2},{3,19},{19,3},{4,20},{20... | collective-permute-start | bytes 1671176 | tf_op jit(solution)/shard_map/ppermute | solution.py:24
  25.1 14.7 %collective-permute-start.5 = (f32[4,136,256]{2,1,0:T(8,128)S(1)}, f32[4,136,256]{2,1,0:T(8,128)S(1)}, u32[]{:S(2)}, u32[]{:S(2)}) collective-permute-start(f32[4,136,256]{2,1,0:T(8,128)S(1)} %pad_maximum_fusion.refs_0_), channel_id=1, source_target_pairs={{0,12},{4,0},{8,4},{12,8},{1,13},{5,1},{9,5},{13,9},{2,14},{6,2},{... | collective-permute-start | bytes 1671176 | tf_op jit(solution)/shard_map/ppermute | solution.py:24
  27.8 15.1 %collective-permute-start.4 = (f32[4,136,256]{2,1,0:T(8,128)S(1)}, f32[4,136,256]{2,1,0:T(8,128)S(1)}, u32[]{:S(2)}, u32[]{:S(2)}) collective-permute-start(f32[4,136,256]{2,1,0:T(8,128)S(1)} %pad_maximum_fusion.refs_0_), channel_id=1, source_target_pairs={{0,4},{4,8},{8,12},{12,0},{1,5},{5,9},{9,13},{13,1},{2,6},{6,10},{... | collective-permute-start | bytes 1671176 | tf_op jit(solution)/shard_map/ppermute | solution.py:24
  42.9 16.9 %collective-permute-start.6 = (f32[4,136,256]{2,1,0:T(8,128)S(1)}, f32[4,136,256]{2,1,0:T(8,128)S(1)}, u32[]{:S(2)}, u32[]{:S(2)}) collective-permute-start(f32[4,136,256]{2,1,0:T(8,128)S(1)} %collective-permute-done.4.refs_0_), channel_id=1, source_target_pairs={{0,16},{16,0},{1,17},{17,1},{2,18},{18,2},{3,19},{19,3},{4,20},{20... | collective-permute-start | bytes 1671176 | tf_op jit(solution)/shard_map/ppermute | solution.py:24
  44.2 15.6 %collective-permute-start.7 = (f32[4,136,256]{2,1,0:T(8,128)S(1)}, f32[4,136,256]{2,1,0:T(8,128)S(1)}, u32[]{:S(2)}, u32[]{:S(2)}) collective-permute-start(f32[4,136,256]{2,1,0:T(8,128)S(1)} %collective-permute-done.5.refs_1_), channel_id=1, source_target_pairs={{0,16},{16,0},{1,17},{17,1},{2,18},{18,2},{3,19},{19,3},{4,20},{20... | collective-permute-start | bytes 1671176 | tf_op jit(solution)/shard_map/ppermute | solution.py:24
  44.3 12.9 %collective-permute-start.9 = (f32[2,136,256]{2,1,0:T(8,128)S(1)}, f32[2,136,256]{2,1,0:T(8,128)S(1)}, u32[]{:S(2)}, u32[]{:S(2)}) collective-permute-start(f32[2,136,256]{2,1,0:T(8,128)S(1)} %slice.7), channel_id=1, source_target_pairs={{0,12},{4,0},{8,4},{12,8},{1,13},{5,1},{9,5},{13,9},{2,14},{6,2},{... | collective-permute-start | bytes 835592 | tf_op jit(solution)/shard_map/ppermute | solution.py:24
  44.4 12.8 %collective-permute-start.8 = (f32[2,136,256]{2,1,0:T(8,128)S(1)}, f32[2,136,256]{2,1,0:T(8,128)S(1)}, u32[]{:S(2)}, u32[]{:S(2)}) collective-permute-start(f32[2,136,256]{2,1,0:T(8,128)S(1)} %slice.6), channel_id=1, source_target_pairs={{0,4},{4,8},{8,12},{12,0},{1,5},{5,9},{9,13},{13,1},{2,6},{6,10},{... | collective-permute-start | bytes 835592 | tf_op jit(solution)/shard_map/ppermute | solution.py:24
  57.2 2.2 %collective-permute-start.10 = (f32[2,136,256]{2,1,0:T(8,128)S(1)}, f32[2,136,256]{2,1,0:T(8,128)S(1)}, u32[]{:S(2)}, u32[]{:S(2)}) collective-permute-start(f32[2,136,256]{2,1,0:T(8,128)S(1)} %collective-permute-done.8.refs_3_), channel_id=1, source_target_pairs={{0,16},{16,0},{1,17},{17,1},{2,18},{18,2},{3,19},{19,3},{4,20},{20... | collective-permute-start | bytes 835592 | tf_op jit(solution)/shard_map/ppermute | solution.py:24
  58.2 1.6 %collective-permute-start.11 = (f32[2,136,256]{2,1,0:T(8,128)S(1)}, f32[2,136,256]{2,1,0:T(8,128)S(1)}, u32[]{:S(2)}, u32[]{:S(2)}) collective-permute-start(f32[2,136,256]{2,1,0:T(8,128)S(1)} %collective-permute-done.9.refs_4_), channel_id=1, source_target_pairs={{0,16},{16,0},{1,17},{17,1},{2,18},{18,2},{3,19},{19,3},{4,20},{20... | collective-permute-start | bytes 835592 | tf_op jit(solution)/shard_map/ppermute | solution.py:24
  64.4 6.0 %collective-permute-start.12 = (f32[256,128]{1,0:T(8,128)S(1)}, f32[256,128]{1,0:T(8,128)S(1)}, u32[]{:S(2)}, u32[]{:S(2)}) collective-permute-start(f32[256,128]{1,0:T(8,128)S(1)} %get-tuple-element.34), channel_id=1, source_target_pairs={{0,32},{32,1},{1,33},{33,2},{2,34},{34,3},{3,35},{35,0},{4,36},{36... | collective-permute-start | bytes 393224 | tf_op jit(solution)/shard_map/ppermute | solution.py:33
  68.4 5.1 %collective-permute-start.16 = (f32[256,128]{1,0:T(8,128)S(1)}, f32[256,128]{1,0:T(8,128)S(1)}, u32[]{:S(2)}, u32[]{:S(2)}) collective-permute-start(f32[256,128]{1,0:T(8,128)S(1)} %ring_step.13), channel_id=1, source_target_pairs={{0,35},{32,0},{1,32},{33,1},{2,33},{34,2},{3,34},{35,3},{4,39},{36... | collective-permute-start | bytes 393224 | tf_op jit(solution)/shard_map/ppermute | solution.py:33
  73.4 5.9 %collective-permute-start.13 = (f32[256,128]{1,0:T(8,128)S(1)}, f32[256,128]{1,0:T(8,128)S(1)}, u32[]{:S(2)}, u32[]{:S(2)}) collective-permute-start(f32[256,128]{1,0:T(8,128)S(1)} %ring_step.10), channel_id=1, source_target_pairs={{0,32},{32,1},{1,33},{33,2},{2,34},{34,3},{3,35},{35,0},{4,36},{36... | collective-permute-start | bytes 393224 | tf_op jit(solution)/shard_map/ppermute | solution.py:33
  76.6 5.9 %collective-permute-start.17 = (f32[256,128]{1,0:T(8,128)S(1)}, f32[256,128]{1,0:T(8,128)S(1)}, u32[]{:S(2)}, u32[]{:S(2)}) collective-permute-start(f32[256,128]{1,0:T(8,128)S(1)} %ring_step.14), channel_id=1, source_target_pairs={{0,35},{32,0},{1,32},{33,1},{2,33},{34,2},{3,34},{35,3},{4,39},{36... | collective-permute-start | bytes 393224 | tf_op jit(solution)/shard_map/ppermute | solution.py:33
  82.3 5.9 %collective-permute-start.14 = (f32[256,128]{1,0:T(8,128)S(1)}, f32[256,128]{1,0:T(8,128)S(1)}, u32[]{:S(2)}, u32[]{:S(2)}) collective-permute-start(f32[256,128]{1,0:T(8,128)S(1)} %ring_step.11), channel_id=1, source_target_pairs={{0,32},{32,1},{1,33},{33,2},{2,34},{34,3},{3,35},{35,0},{4,36},{36... | collective-permute-start | bytes 393224 | tf_op jit(solution)/shard_map/ppermute | solution.py:33
  85.5 5.9 %copy-start.8 = (f32[2048,128]{1,0:T(8,128)S(1)}, f32[2048,128]{1,0:T(8,128)}, u32[]{:S(2)}) copy-start(f32[2048,128]{1,0:T(8,128)} %copy-done.6) | copy-start | bytes 3145732
  85.5 9.0 %collective-permute-start.18 = (f32[256,128]{1,0:T(8,128)S(1)}, f32[256,128]{1,0:T(8,128)S(1)}, u32[]{:S(2)}, u32[]{:S(2)}) collective-permute-start(f32[256,128]{1,0:T(8,128)S(1)} %ring_step.15), channel_id=1, source_target_pairs={{0,35},{32,0},{1,32},{33,1},{2,33},{34,2},{3,34},{35,3},{4,39},{36... | collective-permute-start | bytes 393224 | tf_op jit(solution)/shard_map/ppermute | solution.py:33
  91.3 5.2 %copy-start.1 = (f32[128,256]{1,0:T(8,128)S(1)}, f32[128,256]{1,0:T(8,128)}, u32[]{:S(2)}) copy-start(f32[128,256]{1,0:T(8,128)} %direction_ref.3) | copy-start | bytes 393220
  91.3 5.1 %copy-start.2 = (f32[128,256]{1,0:T(8,128)S(1)}, f32[128,256]{1,0:T(8,128)}, u32[]{:S(2)}) copy-start(f32[128,256]{1,0:T(8,128)} %residual_ref.3) | copy-start | bytes 393220
  91.3 5.1 %copy-start.5 = (f32[256]{0:T(256)S(1)}, f32[256]{0:T(256)}, u32[]{:S(2)}) copy-start(f32[256]{0:T(256)} %param.6) | copy-start | bytes 3076
  91.3 29.6 %copy-start.3 = (f32[128,256]{1,0:T(8,128)S(1)}, f32[128,256]{1,0:T(8,128)}, u32[]{:S(2)}) copy-start(f32[128,256]{1,0:T(8,128)} %solution_ref.1) | copy-start | bytes 393220
  91.3 5.1 %collective-permute-start.15 = (f32[256,128]{1,0:T(8,128)S(1)}, f32[256,128]{1,0:T(8,128)S(1)}, u32[]{:S(2)}, u32[]{:S(2)}) collective-permute-start(f32[256,128]{1,0:T(8,128)S(1)} %ring_step.12), channel_id=1, source_target_pairs={{0,32},{32,1},{1,33},{33,2},{2,34},{34,3},{3,35},{35,0},{4,36},{36... | collective-permute-start | bytes 393224 | tf_op jit(solution)/shard_map/ppermute | solution.py:33
  (4 other events, 3.8 us)

commit v4 on v3

--- a/solution.py
+++ b/solution.py
@@ -11,6 +11,7 @@
 FINE = ("x", "zl", "c", "y", "zh")
 SIZES = (4, 2, 2, 4, 4)
 RING = ("zl", "zh")
+TARGETS = ("zl", "c", "zh")
 PLANE = ("x", "c", "y")
 PART = 256
 LANES = 256
@@ -128,13 +129,15 @@
         weights, rows, refs = refs[0], refs[1], refs[2:]
         prepare(groups, weights, rows)
     columns, tile_a, tile_b = refs
-    length = target.shape[0]
-    z = lax.rem(here[0] + offset, length)
-    which = lax.rem(z, 2) * (length // 2) + lax.div(z, 2)
-    columns[...] = jnp.transpose(target[which])
-    block = out.shape[0]
-    earlier = before[pl.ds(pl.multiple_of(which * block, block), block), :]
-    out[...] = earlier + came[...] if arrived else earlier
+    chips = target.shape[0] // 2
+    z = lax.rem(here[0] + offset, chips)
+    block = target.shape[2]
+    for core in range(2):
+        which = lax.rem(z, 2) * chips + core * (chips // 2) + lax.div(z, 2)
+        rows_of_core = slice(core * block, (core + 1) * block)
+        columns[rows_of_core, :] = jnp.transpose(target[which])
+        earlier = before[pl.ds(pl.multiple_of(which * block, block), block), :]
+        out[rows_of_core, :] = earlier + came[rows_of_core, :] if arrived else earlier
     accumulate(smoothing, wide, weights, rows, columns, out, tile_a, tile_b)
 
 
@@ -144,7 +147,7 @@
     )
 
 
-def bulk(groups, targets, before, smoothing, wide=1024):
+def bulk(groups, targets, before, smoothing, wide=1792):
     ring, coords, block = targets.shape
     systems = groups[0].shape[1] - coords
     sources = sum(g.shape[0] for g in groups) * block
@@ -167,12 +170,12 @@
     )(*groups, targets, *([before] if started else []))
 
 
-def ring_step(here, offset, groups, prepared, targets, before, arrived, smoothing, wide=512):
-    ring, coords, block = targets.shape
+def ring_step(here, offset, groups, prepared, targets, before, arrived, smoothing, wide=768):
+    shards, coords, block = targets.shape
     systems = before.shape[1]
     sources = prepared[0].shape[1] if prepared else sum(g.shape[0] for g in groups) * block
     came = [] if arrived is None else [arrived]
-    outs = [jax.ShapeDtypeStruct((block, systems), jnp.float32)]
+    outs = [jax.ShapeDtypeStruct((2 * block, systems), jnp.float32)]
     if groups:
         outs += [
             jax.ShapeDtypeStruct((2 * systems, sources), jnp.bfloat16),
@@ -180,17 +183,17 @@
         ]
     operands = [*groups, *prepared, targets, before, *came]
     return pl.pallas_call(
-        functools.partial(step_kernel, smoothing, wide, offset % ring, len(groups), bool(came)),
+        functools.partial(step_kernel, smoothing, wide, offset % (shards // 2), len(groups), bool(came)),
         out_shape=outs,
         in_specs=[SMEM] + [VMEM] * len(operands),
         out_specs=[VMEM] * len(outs),
         scratch_shapes=[
-            pltpu.VMEM((block, coords), jnp.float32),
+            pltpu.VMEM((2 * block, coords), jnp.float32),
             pltpu.VMEM((2 * PART, wide), jnp.bfloat16),
             pltpu.VMEM((2 * PART, wide), jnp.bfloat16),
         ],
         compiler_params=pltpu.CompilerParams(vmem_limit_bytes=24 * 2**20),
-        cost_estimate=cost(block, sources, systems),
+        cost_estimate=cost(2 * block, sources, systems),
         name="ring_step",
     )(here, *operands)
 
@@ -200,8 +203,15 @@
     return jnp.sum(jnp.transpose(values[:, :half] + values[:, half:]), axis=0, keepdims=True)
 
 
-def products_kernel(scale, own, up, down, self_term, residual_ref, direction_ref, applied_ref, sums_ref):
-    total = (own[...] + up[...]) + down[...]
+def merge_kernel(here, own, up, down, keep, give):
+    block = keep.shape[0]
+    for out, core in ((keep, here[1]), (give, 1 - here[1])):
+        at = pl.ds(pl.multiple_of(core * block, block), block)
+        out[...] = (own[at, :] + up[at, :]) + down[at, :]
+
+
+def products_kernel(scale, kept, got, self_term, residual_ref, direction_ref, applied_ref, sums_ref):
+    total = kept[...] + got[...]
     direction = direction_ref[...]
     residual = residual_ref[...]
     applied = self_term[...] * direction + jnp.transpose(total) * scale
@@ -247,34 +257,30 @@
     total = block * math.prod(SIZES)
     smoothing = 1.0 / math.sqrt(total)
     ring = lax.axis_size(RING)
-    here = jnp.reshape(lax.axis_index("zh") * 2 + lax.axis_index("zl"), (1,))
+    here = jnp.stack([lax.axis_index("zh") * 2 + lax.axis_index("zl"), lax.axis_index("c")])
     small = pltpu.CompilerParams(vmem_limit_bytes=16 * 2**20)
 
     mine, coords = pl.pallas_call(
         pack_kernel,
         out_shape=(
             jax.ShapeDtypeStruct((systems + COORDS, block), jnp.float32),
-            jax.ShapeDtypeStruct((ring, COORDS, block), jnp.float32),
+            jax.ShapeDtypeStruct((2 * ring, COORDS, block), jnp.float32),
         ),
         in_specs=[VMEM] * 2,
         out_specs=(VMEM, VMEM),
         compiler_params=small,
         name="pack",
     )(points, direction)
-    targets = lax.all_to_all(coords, RING, 0, 0)
-    near = [shift(mine, "x", 1), shift(mine, "x", -1), shift(mine, "x", 2)]
-    targets, *near = lax.optimization_barrier((targets, *near))
-    line = jnp.stack([mine, *near])
-    above, below = shift(line, "y", 1), shift(line, "y", -1)
-    sums = bulk([line, shift(line, "c", 1)], targets, None, smoothing)
-    sums, above, below = lax.optimization_barrier((sums, above, below))
-    far = [shift(above[:2], "y", 1), shift(below[2:], "y", -1)]
-    copies = [shift(above, "c", 1), shift(below, "c", 1)]
-    sums = bulk([above, below], targets, sums, smoothing)
-    sums, *far = lax.optimization_barrier((sums, *far))
-    last = copies + far + [shift(part, "c", 1) for part in far]
-
-    up, *prepared = ring_step(here, 4, last, [], targets, sums, None, smoothing)
+    targets = lax.all_to_all(coords, TARGETS, 0, 0)
+    line = [shift(mine, "x", by) for by in (1, -1, 2)]
+    column = [shift(mine, "y", by) for by in (1, -1, 2)]
+    targets, *cross = lax.optimization_barrier((targets, *line, *column))
+    line, column = jnp.stack(cross[:3]), cross[3:]
+    rest = [shift(line, "y", 1), shift(line, "y", -1)] + [shift(column[2][None], "x", by) for by in (1, -1, 2)]
+    sums = bulk([mine[None], line] + [part[None] for part in column], targets, None, smoothing)
+    sums, *rest = lax.optimization_barrier((sums, *rest))
+
+    up, *prepared = ring_step(here, 4, rest, [], targets, sums, None, smoothing)
     up = ring_shift(up, 1)
     (down,) = ring_step(here, -3, [], prepared, targets, sums, None, smoothing)
     down = ring_shift(down, -1)
@@ -286,17 +292,25 @@
             down = ring_shift(down, -1)
     (own,) = ring_step(here, 0, [], prepared, targets, sums, None, smoothing)
 
+    keep, give = pl.pallas_call(
+        merge_kernel,
+        out_shape=(jax.ShapeDtypeStruct((block, systems), jnp.float32),) * 2,
+        in_specs=[SMEM] + [VMEM] * 3,
+        out_specs=(VMEM, VMEM),
+        compiler_params=small,
+        name="merge",
+    )(here, own, up, down)
     applied, shares = pl.pallas_call(
         functools.partial(products_kernel, 1.0 / math.sqrt(total)),
         out_shape=(
             jax.ShapeDtypeStruct((systems, block), jnp.float32),
             jax.ShapeDtypeStruct((lax.axis_size(PLANE), 1, 4 * systems), jnp.float32),
         ),
-        in_specs=[VMEM] * 6,
+        in_specs=[VMEM] * 5,
         out_specs=(VMEM, VMEM),
         compiler_params=small,
         name="products",
-    )(own, up, down, self_term[None, :], residual, direction)
+    )(keep, shift(give, "c", 1), self_term[None, :], residual, direction)
     shares = pl.pallas_call(
         spread_kernel,
         out_shape=jax.ShapeDtypeStruct((ring, 1, 4 * systems), jnp.float32),

time: 122 us -> 130 us (1.066)
  starting transfers between devices: 23.6 us -> 39.8 us
  blocking collectives: 38.8 us -> 26.6 us
  Pallas kernels: 46.5 us -> 51.4 us
  local copies, waits for them, and re-layouts: 3.86 us -> 1.61 us
    all_to_all x1 -> x0, blocking collectives: 14.6 us -> none  [on_device(): targets = lax.all_to_all(coords, RING, 0, 0)]
    all_to_all x0 -> x1, starting transfers between devices: none -> 9.43 us  [on_device(): targets = lax.all_to_all(coords, TARGETS, 0, 0)]
    pallas_call x8 -> x9, Pallas kernels: 24.6 us -> 32.3 us  [the longest x8 31.8 us: ring_step(): pl.pallas_call(functools.partial(step_kernel, smoothing, wide, offset % (...]
    ppermute x12, starting transfers between devices: 15.1 us -> 21.6 us  [shift(): lax.ppermute(value, axes, [(i, (i + by) % size) for i in range(size)])]
    all_to_all x1, blocking collectives: 8.95 us -> 12.8 us  [on_device(): lax.all_to_all(shares, RING, 0, 0)]
    pallas_call x2 -> x1, Pallas kernels: 20.7 us -> 17.2 us  [bulk(): pl.pallas_call(functools.partial(bulk_kernel, smoothing, wide, len(groups...]
    unnamed x18 -> x12, local copies, waits for them, and re-layouts: 3.82 us -> 1.61 us
    all_to_all x1, blocking collectives: 15.3 us -> 13.8 us  [on_device(): lax.all_to_all(shares, PLANE, 0, 0)]
  transfers between devices with their start and end apart: 19 -> 20, of which waited for: 6 -> 7; matrix products, arithmetic and copies ran while one was open for 0% -> 0% of each run, Pallas kernels for 34% -> 35%
where the time goes in v4:
time: 130 us; the launch traced here: 129 us
  Pallas kernels  51.4 us (40%)
  starting transfers between devices  39.8 us (31%)
  blocking collectives  26.6 us (20%)
  waiting for transfers between devices  9.17 us (7%)
  local copies, waits for them, and re-layouts  1.61 us (1%)
    pallas_call x8, Pallas kernels, ring_step(): pl.pallas_call(functools.partial(step_kernel, smoothing, wide, offset % (...  31.8 us
    ppermute x12, starting transfers between devices, shift(): lax.ppermute(value, axes, [(i, (i + by) % size) for i in range(size)])  21.6 us
    pallas_call x1, Pallas kernels, bulk(): pl.pallas_call(functools.partial(bulk_kernel, smoothing, wide, len(groups...  17.2 us
    all_to_all x1, blocking collectives, on_device(): lax.all_to_all(shares, PLANE, 0, 0)  13.8 us
    all_to_all x1, blocking collectives, on_device(): lax.all_to_all(shares, RING, 0, 0)  12.8 us
    all_to_all x1, starting transfers between devices, on_device(): targets = lax.all_to_all(coords, TARGETS, 0, 0)  9.43 us
    ppermute x7, starting transfers between devices, ring_shift(): lax.ppermute(value, RING, [(ring_index(z), ring_index((z + by) % size)) f...  8.76 us
    ppermute x12, waiting for transfers between devices, shift(): lax.ppermute(value, axes, [(i, (i + by) % size) for i in range(size)])  6.22 us
  transfers between devices with their start and end apart: 20, of which 7 were waited for; matrix products, arithmetic and copies ran while one was open for 0% of the time, Pallas kernels for 35%

profile of v4, /device:TPU:1, one launch (start us, length us, event | category | flops | bytes accessed | tf_op | source)
XLA Modules:
  0.0 129.5 jit_solution(6860409339426033955)
XLA Ops:
  2.9 3.7 %collective-permute-start.5 = (f32[136,256]{1,0:T(8,128)S(1)}, f32[136,256]{1,0:T(8,128)S(1)}, u32[]{:S(2)}, u32[]{:S(2)}) collective-permute-start(f32[136,256]{1,0:T(8,128)S(1)} %get-tuple-element.25), channel_id=1, source_target_pairs={{0,8},{4,12},{8,0},{12,4},{1,9},{5,13},{9,1},{13,5},{2,10},{6,14},... | collective-permute-start | bytes 417800 | tf_op jit(solution)/shard_map/ppermute | solution.py:25
  6.6 9.4 %all-to-all-start = ((f32[16,8,256]{2,1,0:T(8,128)}), f32[16,8,256]{2,1,0:T(8,128)S(1)}, u32[]{:S(2)}, u32[]{:S(2)}) async-start(f32[16,8,256]{2,1,0:T(8,128)} %get-tuple-element.26), calls=%async_computation | async-start | bytes 262144 | tf_op jit(solution)/shard_map/all_to_all | solution.py:274
  17.5 2.7 %collective-permute-start.2 = (f32[136,256]{1,0:T(8,128)S(1)}, f32[136,256]{1,0:T(8,128)S(1)}, u32[]{:S(2)}, u32[]{:S(2)}) collective-permute-start(f32[136,256]{1,0:T(8,128)S(1)} %get-tuple-element.25), channel_id=1, source_target_pairs={{0,128},{64,192},{128,0},{192,64},{1,129},{65,193},{129,1},{193,65... | collective-permute-start | bytes 417800 | tf_op jit(solution)/shard_map/ppermute | solution.py:25
  23.5 3.1 %collective-permute-done.1 = f32[136,256]{1,0:T(8,128)S(1)} collective-permute-done((f32[136,256]{1,0:T(8,128)S(1)}, f32[136,256]{1,0:T(8,128)S(1)}, u32[]{:S(2)}, u32[]{:S(2)}) %collective-permute-start.1) | collective-permute-done | bytes 139296 | tf_op jit(solution)/shard_map/ppermute | solution.py:25
  27.1 3.1 %collective-permute-start.10 = (f32[1,136,256]{2,1,0:T(8,128)S(1)}, f32[1,136,256]{2,1,0:T(8,128)S(1)}, u32[]{:S(2)}, u32[]{:S(2)}) collective-permute-start(f32[1,136,256]{2,1,0:T(8,128)S(1)} %bitcast.11), channel_id=1, source_target_pairs={{0,128},{64,192},{128,0},{192,64},{1,129},{65,193},{129,1},{193,65... | collective-permute-start | bytes 417800 | tf_op jit(solution)/shard_map/ppermute | solution.py:25
  30.2 1.1 collective-permute-start.9
  31.7 2.1 %collective-permute-start.7 = (f32[3,136,256]{2,1,0:T(8,128)S(1)}, f32[3,136,256]{2,1,0:T(8,128)S(1)}, u32[]{:S(2)}, u32[]{:S(2)}) collective-permute-start(f32[3,136,256]{2,1,0:T(8,128)S(1)} %pad_maximum_fusion.refs_1_), channel_id=1, source_target_pairs={{0,12},{4,0},{8,4},{12,8},{1,13},{5,1},{9,5},{13,9},{2,14},{6,2},{... | collective-permute-start | bytes 1253384 | tf_op jit(solution)/shard_map/ppermute | solution.py:25
  33.8 17.2 %bulk.1.refs_7_.refs_4_ = f32[4096,128]{1,0:T(8,128)S(1)} custom-call(f32[1,136,256]{2,1,0:T(8,128)S(1)} %bitcast.15, f32[3,136,256]{2,1,0:T(8,128)S(1)} %pad_maximum_fusion.refs_1_, f32[1,136,256]{2,1,0:T(8,128)S(1)} %bitcast.17, f32[1,136,256]{2,1,0:T(8,128)S(1)} %bitcast.16, f32[1,136,256]{2,1,0:T(8,128)S(1)} %bitcast.14, ...), custom_call_target="tpu_custom_call" | custom-call | flops 15032385536 | bytes 2097152 | tf_op jit(solution)/shard_map/bulk/pallas_call | solution.py:155
  51.0 4.1 %ring_step.8 = (f32[512,128]{1,0:T(8,128)S(1)}, bf16[256,2304]{1,0:T(8,128)(2,1)S(1)}, f32[24,2304]{1,0:T(8,128)S(1)}) custom-call(s32[2]{0:T(128)S(1)} %pad_add_fusion.refs_0_.here, f32[3,136,256]{2,1,0:T(8,128)S(1)} %collective-permute-done.6.refs_1_, f32[3,136,256]{2,1,0:T(8,128)S(1)} %collective-permute-done.7.refs_2_, ...), custom_call_target="tpu_custom_call" | custom-call | flops 2415919104 | bytes 262144 | tf_op jit(solution)/shard_map/ring_step/pallas_call | solution.py:185
  55.1 1.2 collective-permute-start.11
  56.3 4.0 %ring_step.13 = f32[512,128]{1,0:T(8,128)S(1)} custom-call(s32[2]{0:T(128)S(1)} %pad_add_fusion.refs_0_.here, bf16[256,2304]{1,0:T(8,128)(2,1)S(1)} %get-tuple-element.40.refs_1_, f32[24,2304]{1,0:T(8,128)S(1)} %get-tuple-element.41.refs_2_, f32[16,8,256]{2,1,0:T(8,128)S(1)} %all-to-all-done.refs_5_.refs_6_.refs_3_, f32[4096,128]{1,0:T(8,128)S(1)} %bulk.1.refs_7_.refs_4_), custom_call_target="tpu_custom_call" | custom-call | flops 2415919104 | bytes 262144 | tf_op jit(solution)/shard_map/ring_step/pallas_call | solution.py:185
  60.3 1.6 %collective-permute-start.15 = (f32[512,128]{1,0:T(8,128)S(1)}, f32[512,128]{1,0:T(8,128)S(1)}, u32[]{:S(2)}, u32[]{:S(2)}) collective-permute-start(f32[512,128]{1,0:T(8,128)S(1)} %ring_step.13), channel_id=1, source_target_pairs={{0,35},{32,0},{1,32},{33,1},{2,33},{34,2},{3,34},{35,3},{4,39},{36... | collective-permute-start | bytes 786440 | tf_op jit(solution)/shard_map/ppermute | solution.py:34
  62.4 4.0 %ring_step.10 = f32[512,128]{1,0:T(8,128)S(1)} custom-call(s32[2]{0:T(128)S(1)} %pad_add_fusion.refs_0_.here, bf16[256,2304]{1,0:T(8,128)(2,1)S(1)} %get-tuple-element.40.refs_1_, f32[24,2304]{1,0:T(8,128)S(1)} %get-tuple-element.41.refs_2_, f32[16,8,256]{2,1,0:T(8,128)S(1)} %all-to-all-done.refs_5_.refs_6_.refs_3_, f32[4096,128]{1,0:T(8,128)S(1)} %bulk.1.refs_7_.refs_4_, ...), custom_call_target="tpu_custom_call" | custom-call | flops 2415919104 | bytes 262144 | tf_op jit(solution)/shard_map/ring_step/pallas_call | solution.py:185
  66.5 4.0 %ring_step.14 = f32[512,128]{1,0:T(8,128)S(1)} custom-call(s32[2]{0:T(128)S(1)} %pad_add_fusion.refs_0_.here, bf16[256,2304]{1,0:T(8,128)(2,1)S(1)} %get-tuple-element.40.refs_1_, f32[24,2304]{1,0:T(8,128)S(1)} %get-tuple-element.41.refs_2_, f32[16,8,256]{2,1,0:T(8,128)S(1)} %all-to-all-done.refs_5_.refs_6_.refs_3_, f32[4096,128]{1,0:T(8,128)S(1)} %bulk.1.refs_7_.refs_4_, ...), custom_call_target="tpu_custom_call" | custom-call | flops 2415919104 | bytes 262144 | tf_op jit(solution)/shard_map/ring_step/pallas_call | solution.py:185
  70.4 3.0 %collective-permute-start.16 = (f32[512,128]{1,0:T(8,128)S(1)}, f32[512,128]{1,0:T(8,128)S(1)}, u32[]{:S(2)}, u32[]{:S(2)}) collective-permute-start(f32[512,128]{1,0:T(8,128)S(1)} %ring_step.14), channel_id=1, source_target_pairs={{0,35},{32,0},{1,32},{33,1},{2,33},{34,2},{3,34},{35,3},{4,39},{36... | collective-permute-start | bytes 786440 | tf_op jit(solution)/shard_map/ppermute | solution.py:34
  73.4 4.0 %ring_step.11 = f32[512,128]{1,0:T(8,128)S(1)} custom-call(s32[2]{0:T(128)S(1)} %pad_add_fusion.refs_0_.here, bf16[256,2304]{1,0:T(8,128)(2,1)S(1)} %get-tuple-element.40.refs_1_, f32[24,2304]{1,0:T(8,128)S(1)} %get-tuple-element.41.refs_2_, f32[16,8,256]{2,1,0:T(8,128)S(1)} %all-to-all-done.refs_5_.refs_6_.refs_3_, f32[4096,128]{1,0:T(8,128)S(1)} %bulk.1.refs_7_.refs_4_, ...), custom_call_target="tpu_custom_call" | custom-call | flops 2415919104 | bytes 262144 | tf_op jit(solution)/shard_map/ring_step/pallas_call | solution.py:185
  77.5 3.9 %ring_step.15 = f32[512,128]{1,0:T(8,128)S(1)} custom-call(s32[2]{0:T(128)S(1)} %pad_add_fusion.refs_0_.here, bf16[256,2304]{1,0:T(8,128)(2,1)S(1)} %get-tuple-element.40.refs_1_, f32[24,2304]{1,0:T(8,128)S(1)} %get-tuple-element.41.refs_2_, f32[16,8,256]{2,1,0:T(8,128)S(1)} %all-to-all-done.refs_5_.refs_6_.refs_3_, f32[4096,128]{1,0:T(8,128)S(1)} %bulk.1.refs_7_.refs_4_, ...), custom_call_target="tpu_custom_call" | custom-call | flops 2415919104 | bytes 262144 | tf_op jit(solution)/shard_map/ring_step/pallas_call | solution.py:185
  81.4 2.7 %collective-permute-start.17 = (f32[512,128]{1,0:T(8,128)S(1)}, f32[512,128]{1,0:T(8,128)S(1)}, u32[]{:S(2)}, u32[]{:S(2)}) collective-permute-start(f32[512,128]{1,0:T(8,128)S(1)} %ring_step.15), channel_id=1, source_target_pairs={{0,35},{32,0},{1,32},{33,1},{2,33},{34,2},{3,34},{35,3},{4,39},{36... | collective-permute-start | bytes 786440 | tf_op jit(solution)/shard_map/ppermute | solution.py:34
  84.1 3.9 %ring_step.12 = f32[512,128]{1,0:T(8,128)S(1)} custom-call(s32[2]{0:T(128)S(1)} %pad_add_fusion.refs_0_.here, bf16[256,2304]{1,0:T(8,128)(2,1)S(1)} %get-tuple-element.40.refs_1_, f32[24,2304]{1,0:T(8,128)S(1)} %get-tuple-element.41.refs_2_, f32[16,8,256]{2,1,0:T(8,128)S(1)} %all-to-all-done.refs_5_.refs_6_.refs_3_, f32[4096,128]{1,0:T(8,128)S(1)} %bulk.1.refs_7_.refs_4_, ...), custom_call_target="tpu_custom_call" | custom-call | flops 2415919104 | bytes 262144 | tf_op jit(solution)/shard_map/ring_step/pallas_call | solution.py:185
  88.2 4.0 %ring_step.9.own = f32[512,128]{1,0:T(8,128)S(1)} custom-call(s32[2]{0:T(128)S(1)} %pad_add_fusion.refs_0_.here, bf16[256,2304]{1,0:T(8,128)(2,1)S(1)} %get-tuple-element.40.refs_1_, f32[24,2304]{1,0:T(8,128)S(1)} %get-tuple-element.41.refs_2_, f32[16,8,256]{2,1,0:T(8,128)S(1)} %all-to-all-done.refs_5_.refs_6_.refs_3_, f32[4096,128]{1,0:T(8,128)S(1)} %bulk.1.refs_7_.refs_4_), custom_call_target="tpu_custom_call" | custom-call | flops 2415919104 | bytes 262144 | tf_op jit(solution)/shard_map/ring_step/pallas_call | solution.py:185
  92.2 2.4 %collective-permute-done.14.up = f32[512,128]{1,0:T(8,128)S(1)} collective-permute-done((f32[512,128]{1,0:T(8,128)S(1)}, f32[512,128]{1,0:T(8,128)S(1)}, u32[]{:S(2)}, u32[]{:S(2)}) %collective-permute-start.14) | collective-permute-done | bytes 262176 | tf_op jit(solution)/shard_map/ppermute | solution.py:34
  95.2 5.5 %collective-permute-start.18 = (f32[256,128]{1,0:T(8,128)S(1)}, f32[256,128]{1,0:T(8,128)S(1)}, u32[]{:S(2)}, u32[]{:S(2)}) collective-permute-start(f32[256,128]{1,0:T(8,128)S(1)} %get-tuple-element.44), channel_id=1, source_target_pairs={{0,16},{16,0},{1,17},{17,1},{2,18},{18,2},{3,19},{19,3},{4,20},{20... | collective-permute-start | bytes 393224 | tf_op jit(solution)/shard_map/ppermute | solution.py:25
  101.9 13.8 %all_to_all.15.parts = f32[32,1,512]{2,1,0:T(1,128)S(1)} all-to-all(f32[32,1,512]{2,1,0:T(1,128)S(1)} %get-tuple-element.45), channel_id=1, replica_groups=mesh['x'=4,'zl'=2,'c'=2,'y'=4,'zh'=4] {'x','c','y'}, dimensions={0} | all-to-all | bytes 131072 | tf_op jit(solution)/shard_map/all_to_all | solution.py:321
  115.8 12.8 %all_to_all.16.sums_ref = f32[8,1,512]{2,1,0:T(1,128)S(1)} all-to-all(f32[8,1,512]{2,1,0:T(1,128)S(1)} %spread.1), channel_id=1, replica_groups=mesh['x'=4,'zl'=2,'c'=2,'y'=4,'zh'=4] {'zl','zh'}, dimensions={0} | all-to-all | bytes 32768 | tf_op jit(solution)/shard_map/all_to_all | solution.py:329
  (46 shorter events, 11.4 us)
Async XLA Ops:
  2.9 18.3 %collective-permute-start.5 = (f32[136,256]{1,0:T(8,128)S(1)}, f32[136,256]{1,0:T(8,128)S(1)}, u32[]{:S(2)}, u32[]{:S(2)}) collective-permute-start(f32[136,256]{1,0:T(8,128)S(1)} %get-tuple-element.25), channel_id=1, source_target_pairs={{0,8},{4,12},{8,0},{12,4},{1,9},{5,13},{9,1},{13,5},{2,10},{6,14},... | collective-permute-start | bytes 417800 | tf_op jit(solution)/shard_map/ppermute | solution.py:25
  6.6 20.4 %all-to-all-start = ((f32[16,8,256]{2,1,0:T(8,128)}), f32[16,8,256]{2,1,0:T(8,128)S(1)}, u32[]{:S(2)}, u32[]{:S(2)}) async-start(f32[16,8,256]{2,1,0:T(8,128)} %get-tuple-element.26), calls=%async_computation | async-start | bytes 262144 | tf_op jit(solution)/shard_map/all_to_all | solution.py:274
  16.1 5.8 %collective-permute-start.4 = (f32[136,256]{1,0:T(8,128)S(1)}, f32[136,256]{1,0:T(8,128)S(1)}, u32[]{:S(2)}, u32[]{:S(2)}) collective-permute-start(f32[136,256]{1,0:T(8,128)S(1)} %get-tuple-element.25), channel_id=1, source_target_pairs={{0,12},{4,0},{8,4},{12,8},{1,13},{5,1},{9,5},{13,9},{2,14},{6,2},{... | collective-permute-start | bytes 417800 | tf_op jit(solution)/shard_map/ppermute | solution.py:25
  16.9 6.0 %collective-permute-start.3 = (f32[136,256]{1,0:T(8,128)S(1)}, f32[136,256]{1,0:T(8,128)S(1)}, u32[]{:S(2)}, u32[]{:S(2)}) collective-permute-start(f32[136,256]{1,0:T(8,128)S(1)} %get-tuple-element.25), channel_id=1, source_target_pairs={{0,4},{4,8},{8,12},{12,0},{1,5},{5,9},{9,13},{13,1},{2,6},{6,10},{... | collective-permute-start | bytes 417800 | tf_op jit(solution)/shard_map/ppermute | solution.py:25
  17.5 6.0 %collective-permute-start.2 = (f32[136,256]{1,0:T(8,128)S(1)}, f32[136,256]{1,0:T(8,128)S(1)}, u32[]{:S(2)}, u32[]{:S(2)}) collective-permute-start(f32[136,256]{1,0:T(8,128)S(1)} %get-tuple-element.25), channel_id=1, source_target_pairs={{0,128},{64,192},{128,0},{192,64},{1,129},{65,193},{129,1},{193,65... | collective-permute-start | bytes 417800 | tf_op jit(solution)/shard_map/ppermute | solution.py:25
  20.3 6.3 %collective-permute-start.1 = (f32[136,256]{1,0:T(8,128)S(1)}, f32[136,256]{1,0:T(8,128)S(1)}, u32[]{:S(2)}, u32[]{:S(2)}) collective-permute-start(f32[136,256]{1,0:T(8,128)S(1)} %get-tuple-element.25), channel_id=1, source_target_pairs={{0,192},{64,0},{128,64},{192,128},{1,193},{65,1},{129,65},{193,129... | collective-permute-start | bytes 417800 | tf_op jit(solution)/shard_map/ppermute | solution.py:25
  21.2 5.9 %collective-permute-start = (f32[136,256]{1,0:T(8,128)S(1)}, f32[136,256]{1,0:T(8,128)S(1)}, u32[]{:S(2)}, u32[]{:S(2)}) collective-permute-start(f32[136,256]{1,0:T(8,128)S(1)} %get-tuple-element.25), channel_id=1, source_target_pairs={{0,64},{64,128},{128,192},{192,0},{1,65},{65,129},{129,193},{193,1... | collective-permute-start | bytes 417800 | tf_op jit(solution)/shard_map/ppermute | solution.py:25
  27.1 23.9 %collective-permute-start.10 = (f32[1,136,256]{2,1,0:T(8,128)S(1)}, f32[1,136,256]{2,1,0:T(8,128)S(1)}, u32[]{:S(2)}, u32[]{:S(2)}) collective-permute-start(f32[1,136,256]{2,1,0:T(8,128)S(1)} %bitcast.11), channel_id=1, source_target_pairs={{0,128},{64,192},{128,0},{192,64},{1,129},{65,193},{129,1},{193,65... | collective-permute-start | bytes 417800 | tf_op jit(solution)/shard_map/ppermute | solution.py:25
  30.2 20.8 %collective-permute-start.9 = (f32[1,136,256]{2,1,0:T(8,128)S(1)}, f32[1,136,256]{2,1,0:T(8,128)S(1)}, u32[]{:S(2)}, u32[]{:S(2)}) collective-permute-start(f32[1,136,256]{2,1,0:T(8,128)S(1)} %bitcast.12), channel_id=1, source_target_pairs={{0,192},{64,0},{128,64},{192,128},{1,193},{65,1},{129,65},{193,129... | collective-permute-start | bytes 417800 | tf_op jit(solution)/shard_map/ppermute | solution.py:25
  31.2 19.7 %collective-permute-start.8 = (f32[1,136,256]{2,1,0:T(8,128)S(1)}, f32[1,136,256]{2,1,0:T(8,128)S(1)}, u32[]{:S(2)}, u32[]{:S(2)}) collective-permute-start(f32[1,136,256]{2,1,0:T(8,128)S(1)} %bitcast.13), channel_id=1, source_target_pairs={{0,64},{64,128},{128,192},{192,0},{1,65},{65,129},{129,193},{193,1... | collective-permute-start | bytes 417800 | tf_op jit(solution)/shard_map/ppermute | solution.py:25
  31.7 19.3 %collective-permute-start.7 = (f32[3,136,256]{2,1,0:T(8,128)S(1)}, f32[3,136,256]{2,1,0:T(8,128)S(1)}, u32[]{:S(2)}, u32[]{:S(2)}) collective-permute-start(f32[3,136,256]{2,1,0:T(8,128)S(1)} %pad_maximum_fusion.refs_1_), channel_id=1, source_target_pairs={{0,12},{4,0},{8,4},{12,8},{1,13},{5,1},{9,5},{13,9},{2,14},{6,2},{... | collective-permute-start | bytes 1253384 | tf_op jit(solution)/shard_map/ppermute | solution.py:25
  33.7 17.2 %collective-permute-start.6 = (f32[3,136,256]{2,1,0:T(8,128)S(1)}, f32[3,136,256]{2,1,0:T(8,128)S(1)}, u32[]{:S(2)}, u32[]{:S(2)}) collective-permute-start(f32[3,136,256]{2,1,0:T(8,128)S(1)} %pad_maximum_fusion.refs_1_), channel_id=1, source_target_pairs={{0,4},{4,8},{8,12},{12,0},{1,5},{5,9},{9,13},{13,1},{2,6},{6,10},{... | collective-permute-start | bytes 1253384 | tf_op jit(solution)/shard_map/ppermute | solution.py:25
  55.1 7.3 %collective-permute-start.11 = (f32[512,128]{1,0:T(8,128)S(1)}, f32[512,128]{1,0:T(8,128)S(1)}, u32[]{:S(2)}, u32[]{:S(2)}) collective-permute-start(f32[512,128]{1,0:T(8,128)S(1)} %get-tuple-element.42), channel_id=1, source_target_pairs={{0,32},{32,1},{1,33},{33,2},{2,34},{34,3},{3,35},{35,0},{4,36},{36... | collective-permute-start | bytes 786440 | tf_op jit(solution)/shard_map/ppermute | solution.py:34
  60.3 6.2 %collective-permute-start.15 = (f32[512,128]{1,0:T(8,128)S(1)}, f32[512,128]{1,0:T(8,128)S(1)}, u32[]{:S(2)}, u32[]{:S(2)}) collective-permute-start(f32[512,128]{1,0:T(8,128)S(1)} %ring_step.13), channel_id=1, source_target_pairs={{0,35},{32,0},{1,32},{33,1},{2,33},{34,2},{3,34},{35,3},{4,39},{36... | collective-permute-start | bytes 786440 | tf_op jit(solution)/shard_map/ppermute | solution.py:34
  66.4 7.0 %collective-permute-start.12 = (f32[512,128]{1,0:T(8,128)S(1)}, f32[512,128]{1,0:T(8,128)S(1)}, u32[]{:S(2)}, u32[]{:S(2)}) collective-permute-start(f32[512,128]{1,0:T(8,128)S(1)} %ring_step.10), channel_id=1, source_target_pairs={{0,32},{32,1},{1,33},{33,2},{2,34},{34,3},{3,35},{35,0},{4,36},{36... | collective-permute-start | bytes 786440 | tf_op jit(solution)/shard_map/ppermute | solution.py:34
  70.4 7.0 %collective-permute-start.16 = (f32[512,128]{1,0:T(8,128)S(1)}, f32[512,128]{1,0:T(8,128)S(1)}, u32[]{:S(2)}, u32[]{:S(2)}) collective-permute-start(f32[512,128]{1,0:T(8,128)S(1)} %ring_step.14), channel_id=1, source_target_pairs={{0,35},{32,0},{1,32},{33,1},{2,33},{34,2},{3,34},{35,3},{4,39},{36... | collective-permute-start | bytes 786440 | tf_op jit(solution)/shard_map/ppermute | solution.py:34
  77.4 6.8 %collective-permute-start.13 = (f32[512,128]{1,0:T(8,128)S(1)}, f32[512,128]{1,0:T(8,128)S(1)}, u32[]{:S(2)}, u32[]{:S(2)}) collective-permute-start(f32[512,128]{1,0:T(8,128)S(1)} %ring_step.11), channel_id=1, source_target_pairs={{0,32},{32,1},{1,33},{33,2},{2,34},{34,3},{3,35},{35,0},{4,36},{36... | collective-permute-start | bytes 786440 | tf_op jit(solution)/shard_map/ppermute | solution.py:34
  81.4 10.8 %collective-permute-start.17 = (f32[512,128]{1,0:T(8,128)S(1)}, f32[512,128]{1,0:T(8,128)S(1)}, u32[]{:S(2)}, u32[]{:S(2)}) collective-permute-start(f32[512,128]{1,0:T(8,128)S(1)} %ring_step.15), channel_id=1, source_target_pairs={{0,35},{32,0},{1,32},{33,1},{2,33},{34,2},{3,34},{35,3},{4,39},{36... | collective-permute-start | bytes 786440 | tf_op jit(solution)/shard_map/ppermute | solution.py:34
  88.1 13.6 %copy-start.1 = (f32[128,256]{1,0:T(8,128)S(1)}, f32[128,256]{1,0:T(8,128)}, u32[]{:S(2)}) copy-start(f32[128,256]{1,0:T(8,128)} %direction_ref.3) | copy-start | bytes 393220
  88.1 13.6 %copy-start.2 = (f32[128,256]{1,0:T(8,128)S(1)}, f32[128,256]{1,0:T(8,128)}, u32[]{:S(2)}) copy-start(f32[128,256]{1,0:T(8,128)} %residual_ref.3) | copy-start | bytes 393220
  88.1 13.6 %copy-start.5 = (f32[256]{0:T(256)S(1)}, f32[256]{0:T(256)}, u32[]{:S(2)}) copy-start(f32[256]{0:T(256)} %param.6) | copy-start | bytes 3076
  88.1 40.5 %copy-start.3 = (f32[128,256]{1,0:T(8,128)S(1)}, f32[128,256]{1,0:T(8,128)}, u32[]{:S(2)}) copy-start(f32[128,256]{1,0:T(8,128)} %solution_ref.1) | copy-start | bytes 393220
  88.1 6.5 %collective-permute-start.14 = (f32[512,128]{1,0:T(8,128)S(1)}, f32[512,128]{1,0:T(8,128)S(1)}, u32[]{:S(2)}, u32[]{:S(2)}) collective-permute-start(f32[512,128]{1,0:T(8,128)S(1)} %ring_step.12), channel_id=1, source_target_pairs={{0,32},{32,1},{1,33},{33,2},{2,34},{34,3},{3,35},{35,0},{4,36},{36... | collective-permute-start | bytes 786440 | tf_op jit(solution)/shard_map/ppermute | solution.py:34
  95.2 6.5 %collective-permute-start.18 = (f32[256,128]{1,0:T(8,128)S(1)}, f32[256,128]{1,0:T(8,128)S(1)}, u32[]{:S(2)}, u32[]{:S(2)}) collective-permute-start(f32[256,128]{1,0:T(8,128)S(1)} %get-tuple-element.44), channel_id=1, source_target_pairs={{0,16},{16,0},{1,17},{17,1},{2,18},{18,2},{3,19},{19,3},{4,20},{20... | collective-permute-start | bytes 393224 | tf_op jit(solution)/shard_map/ppermute | solution.py:25
  (2 other events, 1.6 us)

commit v5 on v4

--- a/solution.py
+++ b/solution.py
@@ -34,12 +34,17 @@
     return lax.ppermute(value, RING, [(ring_index(z), ring_index((z + by) % size)) for z in range(size)])
 
 
-def pack_kernel(points, direction, mine, coords):
+def pack_kernel(points, direction, mine, coords, held, sems):
     systems = direction.shape[0]
-    mine[...] = jnp.zeros_like(mine)
-    mine[:systems, :] = direction[...]
-    mine[systems : systems + 3, :] = points[...]
-    coords[...] = jnp.broadcast_to(mine[systems:, :][None], coords.shape)
+    first = pltpu.make_async_copy(points, held, sems.at[0])
+    second = pltpu.make_async_copy(direction, mine.at[pl.ds(0, systems)], sems.at[1])
+    first.start()
+    second.start()
+    first.wait()
+    spread = jnp.concatenate([held[...], jnp.zeros((COORDS - 3, held.shape[1]), jnp.float32)], axis=0)
+    mine[systems:, :] = spread
+    coords[...] = jnp.broadcast_to(spread[None], coords.shape)
+    second.wait()
 
 
 def prepare(groups, weights, rows):
@@ -61,47 +66,52 @@
 def accumulate(smoothing, wide, weights, rows, columns, out, tile_a, tile_b):
     systems = out.shape[1]
     across = weights.shape[1] // wide
-    steps = (out.shape[0] // PART) * across
+    parts = out.shape[0] // PART
+    assert parts == 2 or across == 1
+    pairs = parts * across // 2
     tiles = (tile_a, tile_b)
 
-    def make(step, tile):
-        first = pl.multiple_of((step // across) * PART, PART)
-        column = pl.multiple_of((step % across) * wide, wide)
+    def at(pair, half):
+        if across == 1:
+            return pl.ds(pl.multiple_of((2 * pair + half) * PART, PART), PART), pl.ds(0, wide)
+        return pl.ds(half * PART, PART), pl.ds(pl.multiple_of(pair * wide, wide), wide)
+
+    def make(place, tile):
+        down, columns_here = place
         for r in range(0, PART, 16):
-            place = [jnp.broadcast_to(columns[pl.ds(first + r, 16), i : i + 1], (16, LANES)) for i in range(3)]
+            here = [jnp.broadcast_to(columns[pl.ds(down.start + r, 16), i : i + 1], (16, LANES)) for i in range(3)]
             for c in range(0, wide, LANES):
-                lanes = pl.ds(column + c, LANES)
+                lanes = pl.ds(columns_here.start + c, LANES)
                 far = [jnp.concatenate([rows[8 * i : 8 * i + 8, lanes]] * 2, axis=0) for i in range(3)]
-                dx, dy, dz = (far[i] - place[i] for i in range(3))
+                dx, dy, dz = (far[i] - here[i] for i in range(3))
                 kernel = lax.rsqrt(dx * dx + dy * dy + (dz * dz + smoothing * smoothing))
                 high = kernel.astype(jnp.bfloat16)
                 low = (kernel - high.astype(jnp.float32)).astype(jnp.bfloat16)
                 tile[r : r + 16, c : c + LANES] = high
                 tile[PART + r : PART + r + 16, c : c + LANES] = low
 
-    def multiply(step, tile):
-        at = pl.ds(pl.multiple_of((step // across) * PART, PART), PART)
-        column = pl.multiple_of((step % across) * wide, wide)
+    def multiply(place, tile):
+        down, columns_here = place
         product = lax.dot_general(
             tile[...],
-            weights[:, pl.ds(column, wide)],
+            weights[:, columns_here],
             (((1,), (1,)), ((), ())),
             preferred_element_type=jnp.float32,
         )
-        out[at, :] += (product[:PART, :systems] + product[PART:, systems:]) + (
+        out[down, :] += (product[:PART, :systems] + product[PART:, systems:]) + (
             product[:PART, systems:] + product[PART:, :systems]
         )
 
-    make(0, tile_a)
+    make(at(0, 0), tile_a)
 
     def two_steps(pair, carry):
-        for half in range(2):
-            step = pair * 2 + half
-            make(jnp.minimum(step + 1, steps - 1), tiles[1 - half])
-            multiply(step, tiles[half])
+        make(at(pair, 1), tile_b)
+        multiply(at(pair, 0), tile_a)
+        make(at(jnp.minimum(pair + 1, pairs - 1), 0), tile_a)
+        multiply(at(pair, 1), tile_b)
         return carry
 
-    lax.fori_loop(0, steps // 2, two_steps, 0)
+    lax.fori_loop(0, pairs, two_steps, 0)
 
 
 def bulk_kernel(smoothing, wide, count, started, *refs):
@@ -266,16 +276,18 @@
             jax.ShapeDtypeStruct((systems + COORDS, block), jnp.float32),
             jax.ShapeDtypeStruct((2 * ring, COORDS, block), jnp.float32),
         ),
-        in_specs=[VMEM] * 2,
+        in_specs=[pl.BlockSpec(memory_space=pl.ANY)] * 2,
         out_specs=(VMEM, VMEM),
+        scratch_shapes=[pltpu.VMEM(points.shape, jnp.float32), pltpu.SemaphoreType.DMA((2,))],
         compiler_params=small,
         name="pack",
     )(points, direction)
-    targets = lax.all_to_all(coords, TARGETS, 0, 0)
     line = [shift(mine, "x", by) for by in (1, -1, 2)]
     column = [shift(mine, "y", by) for by in (1, -1, 2)]
-    targets, *cross = lax.optimization_barrier((targets, *line, *column))
-    line, column = jnp.stack(cross[:3]), cross[3:]
+    line[0], coords = lax.optimization_barrier((line[0], coords))
+    targets = lax.all_to_all(coords, TARGETS, 0, 0)
+    targets, *line = lax.optimization_barrier((targets, *line))
+    line = jnp.stack(line)
     rest = [shift(line, "y", 1), shift(line, "y", -1)] + [shift(column[2][None], "x", by) for by in (1, -1, 2)]
     sums = bulk([mine[None], line] + [part[None] for part in column], targets, None, smoothing)
     sums, *rest = lax.optimization_barrier((sums, *rest))

time: 130 us -> 130 us (level)
    all_to_all x1, starting transfers between devices: 9.43 us -> 10.9 us  [on_device(): targets = lax.all_to_all(coords, TARGETS, 0, 0)]
  transfers between devices with their start and end apart: 20 -> 20, of which waited for: 7 -> 6; matrix products, arithmetic and copies ran while one was open for 0% -> 0% of each run, Pallas kernels for 35% -> 35%
where the time goes in v5:
time: 130 us
  Pallas kernels  51.6 us (40%)
  starting transfers between devices  40.5 us (31%)
  blocking collectives  25.7 us (20%)
  waiting for transfers between devices  9.8 us (8%)
  local copies, waits for them, and re-layouts  1.61 us (1%)
    pallas_call x8, Pallas kernels, ring_step(): pl.pallas_call(functools.partial(step_kernel, smoothing, wide, offset % (...  31.8 us
    ppermute x12, starting transfers between devices, shift(): lax.ppermute(value, axes, [(i, (i + by) % size) for i in range(size)])  20.7 us
    pallas_call x1, Pallas kernels, bulk(): pl.pallas_call(functools.partial(bulk_kernel, smoothing, wide, len(groups...  17.2 us
    all_to_all x1, blocking collectives, on_device(): lax.all_to_all(shares, RING, 0, 0)  13 us
    all_to_all x1, blocking collectives, on_device(): lax.all_to_all(shares, PLANE, 0, 0)  12.7 us
    all_to_all x1, starting transfers between devices, on_device(): targets = lax.all_to_all(coords, TARGETS, 0, 0)  10.9 us
    ppermute x7, starting transfers between devices, ring_shift(): lax.ppermute(value, RING, [(ring_index(z), ring_index((z + by) % size)) f...  8.94 us
    ppermute x12, waiting for transfers between devices, shift(): lax.ppermute(value, axes, [(i, (i + by) % size) for i in range(size)])  6.49 us
  transfers between devices with their start and end apart: 20, of which 6 were waited for; matrix products, arithmetic and copies ran while one was open for 0% of the time, Pallas kernels for 35%

profile of v5, /device:TPU:1, one launch (start us, length us, event | category | flops | bytes accessed | tf_op | source)
XLA Modules:
  0.0 130.2 jit_solution(14051691655175074195)
XLA Ops:
  3.1 2.1 %collective-permute-start = (f32[136,256]{1,0:T(8,128)S(1)}, f32[136,256]{1,0:T(8,128)S(1)}, u32[]{:S(2)}, u32[]{:S(2)}) collective-permute-start(f32[136,256]{1,0:T(8,128)S(1)} %get-tuple-element.24), channel_id=1, source_target_pairs={{0,64},{64,128},{128,192},{192,0},{1,65},{65,129},{129,193},{193,1... | collective-permute-start | bytes 417800 | tf_op jit(solution)/shard_map/ppermute | solution.py:25
  5.2 3.7 %collective-permute-done = f32[136,256]{1,0:T(8,128)S(1)} collective-permute-done((f32[136,256]{1,0:T(8,128)S(1)}, f32[136,256]{1,0:T(8,128)S(1)}, u32[]{:S(2)}, u32[]{:S(2)}) %collective-permute-start) | collective-permute-done | bytes 139296 | tf_op jit(solution)/shard_map/ppermute | solution.py:25
  8.9 10.9 %all-to-all-start = ((f32[16,8,256]{2,1,0:T(8,128)}), f32[16,8,256]{2,1,0:T(8,128)S(1)}, u32[]{:S(2)}, u32[]{:S(2)}) async-start(f32[16,8,256]{2,1,0:T(8,128)} %get-tuple-element.26), calls=%async_computation | async-start | bytes 262144 | tf_op jit(solution)/shard_map/all_to_all | solution.py:288
  19.7 2.9 %collective-permute-start.5 = (f32[136,256]{1,0:T(8,128)S(1)}, f32[136,256]{1,0:T(8,128)S(1)}, u32[]{:S(2)}, u32[]{:S(2)}) collective-permute-start(f32[136,256]{1,0:T(8,128)S(1)} %get-tuple-element.24), channel_id=1, source_target_pairs={{0,8},{4,12},{8,0},{12,4},{1,9},{5,13},{9,1},{13,5},{2,10},{6,14},... | collective-permute-start | bytes 417800 | tf_op jit(solution)/shard_map/ppermute | solution.py:25
  22.7 1.5 %collective-permute-start.2 = (f32[136,256]{1,0:T(8,128)S(1)}, f32[136,256]{1,0:T(8,128)S(1)}, u32[]{:S(2)}, u32[]{:S(2)}) collective-permute-start(f32[136,256]{1,0:T(8,128)S(1)} %get-tuple-element.24), channel_id=1, source_target_pairs={{0,128},{64,192},{128,0},{192,64},{1,129},{65,193},{129,1},{193,65... | collective-permute-start | bytes 417800 | tf_op jit(solution)/shard_map/ppermute | solution.py:25
  30.9 2.6 %collective-permute-start.8 = (f32[1,136,256]{2,1,0:T(8,128)S(1)}, f32[1,136,256]{2,1,0:T(8,128)S(1)}, u32[]{:S(2)}, u32[]{:S(2)}) collective-permute-start(f32[1,136,256]{2,1,0:T(8,128)S(1)} %bitcast.14), channel_id=1, source_target_pairs={{0,64},{64,128},{128,192},{192,0},{1,65},{65,129},{129,193},{193,1... | collective-permute-start | bytes 417800 | tf_op jit(solution)/shard_map/ppermute | solution.py:25
  33.7 1.4 %collective-permute-start.6 = (f32[3,136,256]{2,1,0:T(8,128)S(1)}, f32[3,136,256]{2,1,0:T(8,128)S(1)}, u32[]{:S(2)}, u32[]{:S(2)}) collective-permute-start(f32[3,136,256]{2,1,0:T(8,128)S(1)} %pad_maximum_fusion.refs_1_), channel_id=1, source_target_pairs={{0,4},{4,8},{8,12},{12,0},{1,5},{5,9},{9,13},{13,1},{2,6},{6,10},{... | collective-permute-start | bytes 1253384 | tf_op jit(solution)/shard_map/ppermute | solution.py:25
  35.1 17.2 %bulk.1.refs_7_.refs_4_ = f32[4096,128]{1,0:T(8,128)S(1)} custom-call(f32[1,136,256]{2,1,0:T(8,128)S(1)} %bitcast.11, f32[3,136,256]{2,1,0:T(8,128)S(1)} %pad_maximum_fusion.refs_1_, f32[1,136,256]{2,1,0:T(8,128)S(1)} %bitcast.17, f32[1,136,256]{2,1,0:T(8,128)S(1)} %bitcast.16, f32[1,136,256]{2,1,0:T(8,128)S(1)} %bitcast.15, ...), custom_call_target="tpu_custom_call" | custom-call | flops 15032385536 | bytes 2097152 | tf_op jit(solution)/shard_map/bulk/pallas_call | solution.py:165
  52.4 4.1 %ring_step.8 = (f32[512,128]{1,0:T(8,128)S(1)}, bf16[256,2304]{1,0:T(8,128)(2,1)S(1)}, f32[24,2304]{1,0:T(8,128)S(1)}) custom-call(s32[2]{0:T(128)S(1)} %pad_add_fusion.refs_0_.here, f32[3,136,256]{2,1,0:T(8,128)S(1)} %collective-permute-done.6.refs_1_, f32[3,136,256]{2,1,0:T(8,128)S(1)} %collective-permute-done.7.refs_2_, ...), custom_call_target="tpu_custom_call" | custom-call | flops 2415919104 | bytes 262144 | tf_op jit(solution)/shard_map/ring_step/pallas_call | solution.py:195
  56.5 1.7 %collective-permute-start.11 = (f32[512,128]{1,0:T(8,128)S(1)}, f32[512,128]{1,0:T(8,128)S(1)}, u32[]{:S(2)}, u32[]{:S(2)}) collective-permute-start(f32[512,128]{1,0:T(8,128)S(1)} %get-tuple-element.40), channel_id=1, source_target_pairs={{0,32},{32,1},{1,33},{33,2},{2,34},{34,3},{3,35},{35,0},{4,36},{36... | collective-permute-start | bytes 786440 | tf_op jit(solution)/shard_map/ppermute | solution.py:34
  58.2 4.0 %ring_step.13 = f32[512,128]{1,0:T(8,128)S(1)} custom-call(s32[2]{0:T(128)S(1)} %pad_add_fusion.refs_0_.here, bf16[256,2304]{1,0:T(8,128)(2,1)S(1)} %get-tuple-element.38.refs_1_, f32[24,2304]{1,0:T(8,128)S(1)} %get-tuple-element.39.refs_2_, f32[16,8,256]{2,1,0:T(8,128)S(1)} %all-to-all-done.refs_5_.refs_6_.refs_3_, f32[4096,128]{1,0:T(8,128)S(1)} %bulk.1.refs_7_.refs_4_), custom_call_target="tpu_custom_call" | custom-call | flops 2415919104 | bytes 262144 | tf_op jit(solution)/shard_map/ring_step/pallas_call | solution.py:195
  62.2 1.3 %collective-permute-start.15 = (f32[512,128]{1,0:T(8,128)S(1)}, f32[512,128]{1,0:T(8,128)S(1)}, u32[]{:S(2)}, u32[]{:S(2)}) collective-permute-start(f32[512,128]{1,0:T(8,128)S(1)} %ring_step.13), channel_id=1, source_target_pairs={{0,35},{32,0},{1,32},{33,1},{2,33},{34,2},{3,34},{35,3},{4,39},{36... | collective-permute-start | bytes 786440 | tf_op jit(solution)/shard_map/ppermute | solution.py:34
  64.3 4.0 %ring_step.10 = f32[512,128]{1,0:T(8,128)S(1)} custom-call(s32[2]{0:T(128)S(1)} %pad_add_fusion.refs_0_.here, bf16[256,2304]{1,0:T(8,128)(2,1)S(1)} %get-tuple-element.38.refs_1_, f32[24,2304]{1,0:T(8,128)S(1)} %get-tuple-element.39.refs_2_, f32[16,8,256]{2,1,0:T(8,128)S(1)} %all-to-all-done.refs_5_.refs_6_.refs_3_, f32[4096,128]{1,0:T(8,128)S(1)} %bulk.1.refs_7_.refs_4_, ...), custom_call_target="tpu_custom_call" | custom-call | flops 2415919104 | bytes 262144 | tf_op jit(solution)/shard_map/ring_step/pallas_call | solution.py:195
  68.5 4.0 %ring_step.14 = f32[512,128]{1,0:T(8,128)S(1)} custom-call(s32[2]{0:T(128)S(1)} %pad_add_fusion.refs_0_.here, bf16[256,2304]{1,0:T(8,128)(2,1)S(1)} %get-tuple-element.38.refs_1_, f32[24,2304]{1,0:T(8,128)S(1)} %get-tuple-element.39.refs_2_, f32[16,8,256]{2,1,0:T(8,128)S(1)} %all-to-all-done.refs_5_.refs_6_.refs_3_, f32[4096,128]{1,0:T(8,128)S(1)} %bulk.1.refs_7_.refs_4_, ...), custom_call_target="tpu_custom_call" | custom-call | flops 2415919104 | bytes 262144 | tf_op jit(solution)/shard_map/ring_step/pallas_call | solution.py:195
  72.5 2.8 %collective-permute-start.16 = (f32[512,128]{1,0:T(8,128)S(1)}, f32[512,128]{1,0:T(8,128)S(1)}, u32[]{:S(2)}, u32[]{:S(2)}) collective-permute-start(f32[512,128]{1,0:T(8,128)S(1)} %ring_step.14), channel_id=1, source_target_pairs={{0,35},{32,0},{1,32},{33,1},{2,33},{34,2},{3,34},{35,3},{4,39},{36... | collective-permute-start | bytes 786440 | tf_op jit(solution)/shard_map/ppermute | solution.py:34
  75.4 4.0 %ring_step.11 = f32[512,128]{1,0:T(8,128)S(1)} custom-call(s32[2]{0:T(128)S(1)} %pad_add_fusion.refs_0_.here, bf16[256,2304]{1,0:T(8,128)(2,1)S(1)} %get-tuple-element.38.refs_1_, f32[24,2304]{1,0:T(8,128)S(1)} %get-tuple-element.39.refs_2_, f32[16,8,256]{2,1,0:T(8,128)S(1)} %all-to-all-done.refs_5_.refs_6_.refs_3_, f32[4096,128]{1,0:T(8,128)S(1)} %bulk.1.refs_7_.refs_4_, ...), custom_call_target="tpu_custom_call" | custom-call | flops 2415919104 | bytes 262144 | tf_op jit(solution)/shard_map/ring_step/pallas_call | solution.py:195
  79.4 3.9 %ring_step.15 = f32[512,128]{1,0:T(8,128)S(1)} custom-call(s32[2]{0:T(128)S(1)} %pad_add_fusion.refs_0_.here, bf16[256,2304]{1,0:T(8,128)(2,1)S(1)} %get-tuple-element.38.refs_1_, f32[24,2304]{1,0:T(8,128)S(1)} %get-tuple-element.39.refs_2_, f32[16,8,256]{2,1,0:T(8,128)S(1)} %all-to-all-done.refs_5_.refs_6_.refs_3_, f32[4096,128]{1,0:T(8,128)S(1)} %bulk.1.refs_7_.refs_4_, ...), custom_call_target="tpu_custom_call" | custom-call | flops 2415919104 | bytes 262144 | tf_op jit(solution)/shard_map/ring_step/pallas_call | solution.py:195
  83.4 2.7 %collective-permute-start.17 = (f32[512,128]{1,0:T(8,128)S(1)}, f32[512,128]{1,0:T(8,128)S(1)}, u32[]{:S(2)}, u32[]{:S(2)}) collective-permute-start(f32[512,128]{1,0:T(8,128)S(1)} %ring_step.15), channel_id=1, source_target_pairs={{0,35},{32,0},{1,32},{33,1},{2,33},{34,2},{3,34},{35,3},{4,39},{36... | collective-permute-start | bytes 786440 | tf_op jit(solution)/shard_map/ppermute | solution.py:34
  86.1 3.9 %ring_step.12 = f32[512,128]{1,0:T(8,128)S(1)} custom-call(s32[2]{0:T(128)S(1)} %pad_add_fusion.refs_0_.here, bf16[256,2304]{1,0:T(8,128)(2,1)S(1)} %get-tuple-element.38.refs_1_, f32[24,2304]{1,0:T(8,128)S(1)} %get-tuple-element.39.refs_2_, f32[16,8,256]{2,1,0:T(8,128)S(1)} %all-to-all-done.refs_5_.refs_6_.refs_3_, f32[4096,128]{1,0:T(8,128)S(1)} %bulk.1.refs_7_.refs_4_, ...), custom_call_target="tpu_custom_call" | custom-call | flops 2415919104 | bytes 262144 | tf_op jit(solution)/shard_map/ring_step/pallas_call | solution.py:195
  90.2 4.0 %ring_step.9.own = f32[512,128]{1,0:T(8,128)S(1)} custom-call(s32[2]{0:T(128)S(1)} %pad_add_fusion.refs_0_.here, bf16[256,2304]{1,0:T(8,128)(2,1)S(1)} %get-tuple-element.38.refs_1_, f32[24,2304]{1,0:T(8,128)S(1)} %get-tuple-element.39.refs_2_, f32[16,8,256]{2,1,0:T(8,128)S(1)} %all-to-all-done.refs_5_.refs_6_.refs_3_, f32[4096,128]{1,0:T(8,128)S(1)} %bulk.1.refs_7_.refs_4_), custom_call_target="tpu_custom_call" | custom-call | flops 2415919104 | bytes 262144 | tf_op jit(solution)/shard_map/ring_step/pallas_call | solution.py:195
  94.2 2.4 %collective-permute-done.14.up = f32[512,128]{1,0:T(8,128)S(1)} collective-permute-done((f32[512,128]{1,0:T(8,128)S(1)}, f32[512,128]{1,0:T(8,128)S(1)}, u32[]{:S(2)}, u32[]{:S(2)}) %collective-permute-start.14) | collective-permute-done | bytes 262176 | tf_op jit(solution)/shard_map/ppermute | solution.py:34
  97.2 5.1 %collective-permute-start.18 = (f32[256,128]{1,0:T(8,128)S(1)}, f32[256,128]{1,0:T(8,128)S(1)}, u32[]{:S(2)}, u32[]{:S(2)}) collective-permute-start(f32[256,128]{1,0:T(8,128)S(1)} %get-tuple-element.42), channel_id=1, source_target_pairs={{0,16},{16,0},{1,17},{17,1},{2,18},{18,2},{3,19},{19,3},{4,20},{20... | collective-permute-start | bytes 393224 | tf_op jit(solution)/shard_map/ppermute | solution.py:25
  103.5 12.7 %all_to_all.15.parts = f32[32,1,512]{2,1,0:T(1,128)S(1)} all-to-all(f32[32,1,512]{2,1,0:T(1,128)S(1)} %get-tuple-element.43), channel_id=1, replica_groups=mesh['x'=4,'zl'=2,'c'=2,'y'=4,'zh'=4] {'x','c','y'}, dimensions={0} | all-to-all | bytes 131072 | tf_op jit(solution)/shard_map/all_to_all | solution.py:333
  116.3 13.0 %all_to_all.16.sums_ref = f32[8,1,512]{2,1,0:T(1,128)S(1)} all-to-all(f32[8,1,512]{2,1,0:T(1,128)S(1)} %spread.1), channel_id=1, replica_groups=mesh['x'=4,'zl'=2,'c'=2,'y'=4,'zh'=4] {'zl','zh'}, dimensions={0} | all-to-all | bytes 32768 | tf_op jit(solution)/shard_map/all_to_all | solution.py:341
  (46 shorter events, 13.3 us)
Async XLA Ops:
  3.1 5.8 %collective-permute-start = (f32[136,256]{1,0:T(8,128)S(1)}, f32[136,256]{1,0:T(8,128)S(1)}, u32[]{:S(2)}, u32[]{:S(2)}) collective-permute-start(f32[136,256]{1,0:T(8,128)S(1)} %get-tuple-element.24), channel_id=1, source_target_pairs={{0,64},{64,128},{128,192},{192,0},{1,65},{65,129},{129,193},{193,1... | collective-permute-start | bytes 417800 | tf_op jit(solution)/shard_map/ppermute | solution.py:25
  8.9 24.6 %all-to-all-start = ((f32[16,8,256]{2,1,0:T(8,128)}), f32[16,8,256]{2,1,0:T(8,128)S(1)}, u32[]{:S(2)}, u32[]{:S(2)}) async-start(f32[16,8,256]{2,1,0:T(8,128)} %get-tuple-element.26), calls=%async_computation | async-start | bytes 262144 | tf_op jit(solution)/shard_map/all_to_all | solution.py:288
  19.7 6.9 %collective-permute-start.5 = (f32[136,256]{1,0:T(8,128)S(1)}, f32[136,256]{1,0:T(8,128)S(1)}, u32[]{:S(2)}, u32[]{:S(2)}) collective-permute-start(f32[136,256]{1,0:T(8,128)S(1)} %get-tuple-element.24), channel_id=1, source_target_pairs={{0,8},{4,12},{8,0},{12,4},{1,9},{5,13},{9,1},{13,5},{2,10},{6,14},... | collective-permute-start | bytes 417800 | tf_op jit(solution)/shard_map/ppermute | solution.py:25
  22.7 6.3 %collective-permute-start.2 = (f32[136,256]{1,0:T(8,128)S(1)}, f32[136,256]{1,0:T(8,128)S(1)}, u32[]{:S(2)}, u32[]{:S(2)}) collective-permute-start(f32[136,256]{1,0:T(8,128)S(1)} %get-tuple-element.24), channel_id=1, source_target_pairs={{0,128},{64,192},{128,0},{192,64},{1,129},{65,193},{129,1},{193,65... | collective-permute-start | bytes 417800 | tf_op jit(solution)/shard_map/ppermute | solution.py:25
  24.2 6.7 %collective-permute-start.1 = (f32[136,256]{1,0:T(8,128)S(1)}, f32[136,256]{1,0:T(8,128)S(1)}, u32[]{:S(2)}, u32[]{:S(2)}) collective-permute-start(f32[136,256]{1,0:T(8,128)S(1)} %get-tuple-element.24), channel_id=1, source_target_pairs={{0,192},{64,0},{128,64},{192,128},{1,193},{65,1},{129,65},{193,129... | collective-permute-start | bytes 417800 | tf_op jit(solution)/shard_map/ppermute | solution.py:25
  25.1 8.5 %collective-permute-start.4 = (f32[136,256]{1,0:T(8,128)S(1)}, f32[136,256]{1,0:T(8,128)S(1)}, u32[]{:S(2)}, u32[]{:S(2)}) collective-permute-start(f32[136,256]{1,0:T(8,128)S(1)} %get-tuple-element.24), channel_id=1, source_target_pairs={{0,12},{4,0},{8,4},{12,8},{1,13},{5,1},{9,5},{13,9},{2,14},{6,2},{... | collective-permute-start | bytes 417800 | tf_op jit(solution)/shard_map/ppermute | solution.py:25
  25.8 7.8 %collective-permute-start.3 = (f32[136,256]{1,0:T(8,128)S(1)}, f32[136,256]{1,0:T(8,128)S(1)}, u32[]{:S(2)}, u32[]{:S(2)}) collective-permute-start(f32[136,256]{1,0:T(8,128)S(1)} %get-tuple-element.24), channel_id=1, source_target_pairs={{0,4},{4,8},{8,12},{12,0},{1,5},{5,9},{9,13},{13,1},{2,6},{6,10},{... | collective-permute-start | bytes 417800 | tf_op jit(solution)/shard_map/ppermute | solution.py:25
  26.6 25.8 %collective-permute-start.10 = (f32[1,136,256]{2,1,0:T(8,128)S(1)}, f32[1,136,256]{2,1,0:T(8,128)S(1)}, u32[]{:S(2)}, u32[]{:S(2)}) collective-permute-start(f32[1,136,256]{2,1,0:T(8,128)S(1)} %bitcast.12), channel_id=1, source_target_pairs={{0,128},{64,192},{128,0},{192,64},{1,129},{65,193},{129,1},{193,65... | collective-permute-start | bytes 417800 | tf_op jit(solution)/shard_map/ppermute | solution.py:25
  28.9 23.4 %collective-permute-start.9 = (f32[1,136,256]{2,1,0:T(8,128)S(1)}, f32[1,136,256]{2,1,0:T(8,128)S(1)}, u32[]{:S(2)}, u32[]{:S(2)}) collective-permute-start(f32[1,136,256]{2,1,0:T(8,128)S(1)} %bitcast.13), channel_id=1, source_target_pairs={{0,192},{64,0},{128,64},{192,128},{1,193},{65,1},{129,65},{193,129... | collective-permute-start | bytes 417800 | tf_op jit(solution)/shard_map/ppermute | solution.py:25
  30.9 21.5 %collective-permute-start.8 = (f32[1,136,256]{2,1,0:T(8,128)S(1)}, f32[1,136,256]{2,1,0:T(8,128)S(1)}, u32[]{:S(2)}, u32[]{:S(2)}) collective-permute-start(f32[1,136,256]{2,1,0:T(8,128)S(1)} %bitcast.14), channel_id=1, source_target_pairs={{0,64},{64,128},{128,192},{192,0},{1,65},{65,129},{129,193},{193,1... | collective-permute-start | bytes 417800 | tf_op jit(solution)/shard_map/ppermute | solution.py:25
  33.6 18.8 %collective-permute-start.7 = (f32[3,136,256]{2,1,0:T(8,128)S(1)}, f32[3,136,256]{2,1,0:T(8,128)S(1)}, u32[]{:S(2)}, u32[]{:S(2)}) collective-permute-start(f32[3,136,256]{2,1,0:T(8,128)S(1)} %pad_maximum_fusion.refs_1_), channel_id=1, source_target_pairs={{0,12},{4,0},{8,4},{12,8},{1,13},{5,1},{9,5},{13,9},{2,14},{6,2},{... | collective-permute-start | bytes 1253384 | tf_op jit(solution)/shard_map/ppermute | solution.py:25
  33.7 18.7 %collective-permute-start.6 = (f32[3,136,256]{2,1,0:T(8,128)S(1)}, f32[3,136,256]{2,1,0:T(8,128)S(1)}, u32[]{:S(2)}, u32[]{:S(2)}) collective-permute-start(f32[3,136,256]{2,1,0:T(8,128)S(1)} %pad_maximum_fusion.refs_1_), channel_id=1, source_target_pairs={{0,4},{4,8},{8,12},{12,0},{1,5},{5,9},{9,13},{13,1},{2,6},{6,10},{... | collective-permute-start | bytes 1253384 | tf_op jit(solution)/shard_map/ppermute | solution.py:25
  56.5 7.8 %collective-permute-start.11 = (f32[512,128]{1,0:T(8,128)S(1)}, f32[512,128]{1,0:T(8,128)S(1)}, u32[]{:S(2)}, u32[]{:S(2)}) collective-permute-start(f32[512,128]{1,0:T(8,128)S(1)} %get-tuple-element.40), channel_id=1, source_target_pairs={{0,32},{32,1},{1,33},{33,2},{2,34},{34,3},{3,35},{35,0},{4,36},{36... | collective-permute-start | bytes 786440 | tf_op jit(solution)/shard_map/ppermute | solution.py:34
  62.2 6.4 %collective-permute-start.15 = (f32[512,128]{1,0:T(8,128)S(1)}, f32[512,128]{1,0:T(8,128)S(1)}, u32[]{:S(2)}, u32[]{:S(2)}) collective-permute-start(f32[512,128]{1,0:T(8,128)S(1)} %ring_step.13), channel_id=1, source_target_pairs={{0,35},{32,0},{1,32},{33,1},{2,33},{34,2},{3,34},{35,3},{4,39},{36... | collective-permute-start | bytes 786440 | tf_op jit(solution)/shard_map/ppermute | solution.py:34
  68.3 7.0 %collective-permute-start.12 = (f32[512,128]{1,0:T(8,128)S(1)}, f32[512,128]{1,0:T(8,128)S(1)}, u32[]{:S(2)}, u32[]{:S(2)}) collective-permute-start(f32[512,128]{1,0:T(8,128)S(1)} %ring_step.10), channel_id=1, source_target_pairs={{0,32},{32,1},{1,33},{33,2},{2,34},{34,3},{3,35},{35,0},{4,36},{36... | collective-permute-start | bytes 786440 | tf_op jit(solution)/shard_map/ppermute | solution.py:34
  72.5 6.9 %collective-permute-start.16 = (f32[512,128]{1,0:T(8,128)S(1)}, f32[512,128]{1,0:T(8,128)S(1)}, u32[]{:S(2)}, u32[]{:S(2)}) collective-permute-start(f32[512,128]{1,0:T(8,128)S(1)} %ring_step.14), channel_id=1, source_target_pairs={{0,35},{32,0},{1,32},{33,1},{2,33},{34,2},{3,34},{35,3},{4,39},{36... | collective-permute-start | bytes 786440 | tf_op jit(solution)/shard_map/ppermute | solution.py:34
  79.3 6.8 %collective-permute-start.13 = (f32[512,128]{1,0:T(8,128)S(1)}, f32[512,128]{1,0:T(8,128)S(1)}, u32[]{:S(2)}, u32[]{:S(2)}) collective-permute-start(f32[512,128]{1,0:T(8,128)S(1)} %ring_step.11), channel_id=1, source_target_pairs={{0,32},{32,1},{1,33},{33,2},{2,34},{34,3},{3,35},{35,0},{4,36},{36... | collective-permute-start | bytes 786440 | tf_op jit(solution)/shard_map/ppermute | solution.py:34
  83.4 10.8 %collective-permute-start.17 = (f32[512,128]{1,0:T(8,128)S(1)}, f32[512,128]{1,0:T(8,128)S(1)}, u32[]{:S(2)}, u32[]{:S(2)}) collective-permute-start(f32[512,128]{1,0:T(8,128)S(1)} %ring_step.15), channel_id=1, source_target_pairs={{0,35},{32,0},{1,32},{33,1},{2,33},{34,2},{3,34},{35,3},{4,39},{36... | collective-permute-start | bytes 786440 | tf_op jit(solution)/shard_map/ppermute | solution.py:34
  90.1 13.2 %copy-start.1 = (f32[128,256]{1,0:T(8,128)S(1)}, f32[128,256]{1,0:T(8,128)}, u32[]{:S(2)}) copy-start(f32[128,256]{1,0:T(8,128)} %direction_ref.3) | copy-start | bytes 393220
  90.1 13.2 %copy-start.2 = (f32[128,256]{1,0:T(8,128)S(1)}, f32[128,256]{1,0:T(8,128)}, u32[]{:S(2)}) copy-start(f32[128,256]{1,0:T(8,128)} %residual_ref.3) | copy-start | bytes 393220
  90.1 13.2 %copy-start.5 = (f32[256]{0:T(256)S(1)}, f32[256]{0:T(256)}, u32[]{:S(2)}) copy-start(f32[256]{0:T(256)} %param.6) | copy-start | bytes 3076
  90.1 39.2 %copy-start.3 = (f32[128,256]{1,0:T(8,128)S(1)}, f32[128,256]{1,0:T(8,128)}, u32[]{:S(2)}) copy-start(f32[128,256]{1,0:T(8,128)} %solution_ref.1) | copy-start | bytes 393220
  90.1 6.5 %collective-permute-start.14 = (f32[512,128]{1,0:T(8,128)S(1)}, f32[512,128]{1,0:T(8,128)S(1)}, u32[]{:S(2)}, u32[]{:S(2)}) collective-permute-start(f32[512,128]{1,0:T(8,128)S(1)} %ring_step.12), channel_id=1, source_target_pairs={{0,32},{32,1},{1,33},{33,2},{2,34},{34,3},{3,35},{35,0},{4,36},{36... | collective-permute-start | bytes 786440 | tf_op jit(solution)/shard_map/ppermute | solution.py:34
  97.2 6.1 %collective-permute-start.18 = (f32[256,128]{1,0:T(8,128)S(1)}, f32[256,128]{1,0:T(8,128)S(1)}, u32[]{:S(2)}, u32[]{:S(2)}) collective-permute-start(f32[256,128]{1,0:T(8,128)S(1)} %get-tuple-element.42), channel_id=1, source_target_pairs={{0,16},{16,0},{1,17},{17,1},{2,18},{18,2},{3,19},{19,3},{4,20},{20... | collective-permute-start | bytes 393224 | tf_op jit(solution)/shard_map/ppermute | solution.py:25
  (2 other events, 1.6 us)

commit v6 on v3

--- a/solution.py
+++ b/solution.py
@@ -15,6 +15,7 @@
 PART = 256
 LANES = 256
 COORDS = 8
+KERNEL_VMEM = 10 * 2**20
 VMEM = pl.BlockSpec(memory_space=pltpu.VMEM)
 SMEM = pl.BlockSpec(memory_space=pltpu.SMEM)
 
@@ -57,85 +58,93 @@
             at += block
 
 
-def accumulate(smoothing, wide, weights, rows, columns, out, tile_a, tile_b):
+def accumulate(smoothing, wide, pairs, at, weights, rows, columns, out, tile_a, tile_b):
     systems = out.shape[1]
-    across = weights.shape[1] // wide
-    steps = (out.shape[0] // PART) * across
-    tiles = (tile_a, tile_b)
-
-    def make(step, tile):
-        first = pl.multiple_of((step // across) * PART, PART)
-        column = pl.multiple_of((step % across) * wide, wide)
+
+    def make(place, tile):
+        first, column = place
         for r in range(0, PART, 16):
-            place = [jnp.broadcast_to(columns[pl.ds(first + r, 16), i : i + 1], (16, LANES)) for i in range(3)]
+            here = [jnp.broadcast_to(columns[pl.ds(first + r, 16), i : i + 1], (16, LANES)) for i in range(3)]
             for c in range(0, wide, LANES):
                 lanes = pl.ds(column + c, LANES)
                 far = [jnp.concatenate([rows[8 * i : 8 * i + 8, lanes]] * 2, axis=0) for i in range(3)]
-                dx, dy, dz = (far[i] - place[i] for i in range(3))
+                dx, dy, dz = (far[i] - here[i] for i in range(3))
                 kernel = lax.rsqrt(dx * dx + dy * dy + (dz * dz + smoothing * smoothing))
                 high = kernel.astype(jnp.bfloat16)
                 low = (kernel - high.astype(jnp.float32)).astype(jnp.bfloat16)
                 tile[r : r + 16, c : c + LANES] = high
                 tile[PART + r : PART + r + 16, c : c + LANES] = low
 
-    def multiply(step, tile):
-        at = pl.ds(pl.multiple_of((step // across) * PART, PART), PART)
-        column = pl.multiple_of((step % across) * wide, wide)
+    def multiply(place, tile):
+        first, column = place
         product = lax.dot_general(
             tile[...],
             weights[:, pl.ds(column, wide)],
             (((1,), (1,)), ((), ())),
             preferred_element_type=jnp.float32,
         )
-        out[at, :] += (product[:PART, :systems] + product[PART:, systems:]) + (
+        out[pl.ds(first, PART), :] += (product[:PART, :systems] + product[PART:, systems:]) + (
             product[:PART, systems:] + product[PART:, :systems]
         )
 
-    make(0, tile_a)
+    make(at(0, 0), tile_a)
 
     def two_steps(pair, carry):
-        for half in range(2):
-            step = pair * 2 + half
-            make(jnp.minimum(step + 1, steps - 1), tiles[1 - half])
-            multiply(step, tiles[half])
+        make(at(pair, 1), tile_b)
+        multiply(at(pair, 0), tile_a)
+        make(at(jnp.minimum(pair + 1, pairs - 1), 0), tile_a)
+        multiply(at(pair, 1), tile_b)
         return carry
 
-    lax.fori_loop(0, steps // 2, two_steps, 0)
-
-
-def bulk_kernel(smoothing, wide, count, started, *refs):
+    lax.fori_loop(0, pairs, two_steps, 0)
+
+
+def shard_at(z, offset, chips):
+    z = lax.rem(z + offset, chips)
+    return lax.rem(z, 2) * (chips // 2) + lax.div(z, 2)
+
+
+def bulk_kernel(smoothing, wide, count, started, here, *refs):
     groups, refs = refs[:count], refs[count:]
     target, refs = refs[0], refs[1:]
     before, refs = (refs[0], refs[1:]) if started else (None, refs)
     out, weights, rows, columns, tile_a, tile_b = refs
-    block = target.shape[2]
-    for b in range(target.shape[0]):
+    chips, _, block = target.shape
+    for b in range(chips):
         columns[b * block : (b + 1) * block, :] = jnp.transpose(target[b])
     prepare(groups, weights, rows)
     out[...] = before[...] if started else jnp.zeros_like(out)
-    accumulate(smoothing, wide, weights, rows, columns, out, tile_a, tile_b)
-
-
-def step_kernel(smoothing, wide, offset, count, arrived, *refs):
-    here, refs = refs[0], refs[1:]
+
+    def at(pair, half):
+        shard = shard_at(here[0], pair + 1, chips) if started else pair
+        return pl.multiple_of(shard * block, block), half * wide
+
+    accumulate(smoothing, wide, chips - started, at, weights, rows, columns, out, tile_a, tile_b)
+
+
+def step_kernel(smoothing, wide, offset, count, sets, arrived, here, *refs):
     groups, refs = refs[:count], refs[count:]
-    if not count:
-        weights, rows, refs = refs[0], refs[1], refs[2:]
+    prepared, refs = refs[: 2 * sets], refs[2 * sets :]
     target, before, refs = refs[0], refs[1], refs[2:]
     came, refs = (refs[0], refs[1:]) if arrived else (None, refs)
     out, refs = refs[0], refs[1:]
     if count:
-        weights, rows, refs = refs[0], refs[1], refs[2:]
-        prepare(groups, weights, rows)
+        prepared, refs = refs[:2], refs[2:]
+        prepare(groups, *prepared)
     columns, tile_a, tile_b = refs
-    length = target.shape[0]
-    z = lax.rem(here[0] + offset, length)
-    which = lax.rem(z, 2) * (length // 2) + lax.div(z, 2)
+    chips, _, block = target.shape
+    which = shard_at(here[0], offset, chips)
     columns[...] = jnp.transpose(target[which])
-    block = out.shape[0]
     earlier = before[pl.ds(pl.multiple_of(which * block, block), block), :]
     out[...] = earlier + came[...] if arrived else earlier
-    accumulate(smoothing, wide, weights, rows, columns, out, tile_a, tile_b)
+
+    def at(pair, half):
+        return 0, pl.multiple_of((2 * pair + half) * wide, wide)
+
+    for i in range(0, len(prepared), 2):
+        weights, rows = prepared[i : i + 2]
+        pairs = weights.shape[1] // (2 * wide)
+        accumulate(smoothing, wide, pairs, at, weights, rows, columns, out, tile_a, tile_b)
 
 
 def cost(targets, sources, systems):
@@ -144,43 +153,48 @@
     )
 
 
-def bulk(groups, targets, before, smoothing, wide=1024):
-    ring, coords, block = targets.shape
+def prepared_shapes(systems, sources):
+    return [
+        jax.ShapeDtypeStruct((2 * systems, sources), jnp.bfloat16),
+        jax.ShapeDtypeStruct((24, sources), jnp.float32),
+    ]
+
+
+def bulk(here, groups, targets, before, smoothing):
+    chips, coords, block = targets.shape
     systems = groups[0].shape[1] - coords
     sources = sum(g.shape[0] for g in groups) * block
+    wide = sources // 2
     started = before is not None
+    held = prepared_shapes(systems, sources)
     return pl.pallas_call(
         functools.partial(bulk_kernel, smoothing, wide, len(groups), started),
-        out_shape=jax.ShapeDtypeStruct((ring * block, systems), jnp.float32),
-        in_specs=[VMEM] * (len(groups) + 1 + started),
-        out_specs=VMEM,
-        scratch_shapes=[
-            pltpu.VMEM((2 * systems, sources), jnp.bfloat16),
-            pltpu.VMEM((24, sources), jnp.float32),
-            pltpu.VMEM((ring * block, coords), jnp.float32),
+        out_shape=[jax.ShapeDtypeStruct((chips * block, systems), jnp.float32)] + (held if started else []),
+        in_specs=[SMEM] + [VMEM] * (len(groups) + 1 + started),
+        out_specs=[VMEM] * (3 if started else 1),
+        scratch_shapes=([] if started else [pltpu.VMEM(h.shape, h.dtype) for h in held])
+        + [
+            pltpu.VMEM((chips * block, coords), jnp.float32),
             pltpu.VMEM((2 * PART, wide), jnp.bfloat16),
             pltpu.VMEM((2 * PART, wide), jnp.bfloat16),
         ],
-        compiler_params=pltpu.CompilerParams(vmem_limit_bytes=24 * 2**20),
-        cost_estimate=cost(ring * block, sources, systems),
+        compiler_params=pltpu.CompilerParams(vmem_limit_bytes=KERNEL_VMEM),
+        cost_estimate=cost(chips * block, sources, systems),
         name="bulk",
-    )(*groups, targets, *([before] if started else []))
+    )(here, *groups, targets, *([before] if started else []))
 
 
 def ring_step(here, offset, groups, prepared, targets, before, arrived, smoothing, wide=512):
-    ring, coords, block = targets.shape
+    chips, coords, block = targets.shape
     systems = before.shape[1]
-    sources = prepared[0].shape[1] if prepared else sum(g.shape[0] for g in groups) * block
+    sources = sum(g.shape[0] for g in groups) * block + sum(p.shape[1] for p in prepared[::2])
     came = [] if arrived is None else [arrived]
     outs = [jax.ShapeDtypeStruct((block, systems), jnp.float32)]
     if groups:
-        outs += [
-            jax.ShapeDtypeStruct((2 * systems, sources), jnp.bfloat16),
-            jax.ShapeDtypeStruct((24, sources), jnp.float32),
-        ]
+        outs += prepared_shapes(systems, sources)
     operands = [*groups, *prepared, targets, before, *came]
     return pl.pallas_call(
-        functools.partial(step_kernel, smoothing, wide, offset % ring, len(groups), bool(came)),
+        functools.partial(step_kernel, smoothing, wide, offset % chips, len(groups), len(prepared) // 2, bool(came)),
         out_shape=outs,
         in_specs=[SMEM] + [VMEM] * len(operands),
         out_specs=[VMEM] * len(outs),
@@ -189,7 +203,7 @@
             pltpu.VMEM((2 * PART, wide), jnp.bfloat16),
             pltpu.VMEM((2 * PART, wide), jnp.bfloat16),
         ],
-        compiler_params=pltpu.CompilerParams(vmem_limit_bytes=24 * 2**20),
+        compiler_params=pltpu.CompilerParams(vmem_limit_bytes=KERNEL_VMEM),
         cost_estimate=cost(block, sources, systems),
         name="ring_step",
     )(here, *operands)
@@ -261,30 +275,30 @@
         compiler_params=small,
         name="pack",
     )(points, direction)
+    near = [shift(mine, "x", 1), shift(mine, "x", -1), shift(mine, "x", 2)]
+    coords, *near = lax.optimization_barrier((coords, *near))
     targets = lax.all_to_all(coords, RING, 0, 0)
-    near = [shift(mine, "x", 1), shift(mine, "x", -1), shift(mine, "x", 2)]
-    targets, *near = lax.optimization_barrier((targets, *near))
     line = jnp.stack([mine, *near])
     above, below = shift(line, "y", 1), shift(line, "y", -1)
-    sums = bulk([line, shift(line, "c", 1)], targets, None, smoothing)
+    (sums,) = bulk(here, [line, shift(line, "c", 1)], targets, None, smoothing)
     sums, above, below = lax.optimization_barrier((sums, above, below))
     far = [shift(above[:2], "y", 1), shift(below[2:], "y", -1)]
     copies = [shift(above, "c", 1), shift(below, "c", 1)]
-    sums = bulk([above, below], targets, sums, smoothing)
+    sums, *second = bulk(here, [above, below], targets, sums, smoothing)
     sums, *far = lax.optimization_barrier((sums, *far))
     last = copies + far + [shift(part, "c", 1) for part in far]
 
-    up, *prepared = ring_step(here, 4, last, [], targets, sums, None, smoothing)
+    up, *third = ring_step(here, 4, last, [], targets, sums, None, smoothing)
     up = ring_shift(up, 1)
-    (down,) = ring_step(here, -3, [], prepared, targets, sums, None, smoothing)
+    (down,) = ring_step(here, -3, [], third, targets, sums, None, smoothing)
     down = ring_shift(down, -1)
     for away in (3, 2, 1):
-        (up,) = ring_step(here, away, [], prepared, targets, sums, up, smoothing)
+        (up,) = ring_step(here, away, [], third, targets, sums, up, smoothing)
         up = ring_shift(up, 1)
         if away > 1:
-            (down,) = ring_step(here, 1 - away, [], prepared, targets, sums, down, smoothing)
+            (down,) = ring_step(here, 1 - away, [], third, targets, sums, down, smoothing)
             down = ring_shift(down, -1)
-    (own,) = ring_step(here, 0, [], prepared, targets, sums, None, smoothing)
+    (own,) = ring_step(here, 0, [], second + third, targets, sums, None, smoothing)
 
     applied, shares = pl.pallas_call(
         functools.partial(products_kernel, 1.0 / math.sqrt(total)),

time: 122 us -> 121 us (level)
  blocking collectives: 38.8 us -> 27.7 us
  starting transfers between devices: 23.6 us -> 29.9 us
  waiting for transfers between devices: 8.13 us -> 13.1 us
  local copies, waits for them, and re-layouts: 3.86 us -> 1.65 us
  Pallas kernels: 46.5 us -> 47.9 us
    all_to_all x1 -> x0, blocking collectives: 14.6 us -> none  [on_device(): targets = lax.all_to_all(coords, RING, 0, 0)]
    all_to_all x0 -> x1, starting transfers between devices: none -> 7.32 us  [on_device(): targets = lax.all_to_all(coords, RING, 0, 0)]
    all_to_all x0 -> x1, waiting for transfers between devices: none -> 4.02 us  [on_device(): targets = lax.all_to_all(coords, RING, 0, 0)]
    ppermute x12, waiting for transfers between devices: 6.03 us -> 8.72 us  [shift(): lax.ppermute(value, axes, [(i, (i + by) % size) for i in range(size)])]
    unnamed x18 -> x12, local copies, waits for them, and re-layouts: 3.82 us -> 1.61 us
    all_to_all x1, blocking collectives: 8.95 us -> 10.7 us  [on_device(): lax.all_to_all(shares, RING, 0, 0)]
    ppermute x7, waiting for transfers between devices: 2.11 us -> 0.34 us  [ring_shift(): lax.ppermute(value, RING, [(ring_index(z), ring_index((z + by) % size)) f...]
    all_to_all x1, blocking collectives: 15.3 us -> 16.9 us  [on_device(): lax.all_to_all(shares, PLANE, 0, 0)]
  transfers between devices with their start and end apart: 19 -> 20, of which waited for: 6 -> 9; matrix products, arithmetic and copies ran while one was open for 0% -> 0% of each run, Pallas kernels for 34% -> 35%
where the time goes in v6:
time: 121 us
  Pallas kernels  47.9 us (40%)
  starting transfers between devices  29.9 us (25%)
  blocking collectives  27.7 us (23%)
  waiting for transfers between devices  13.1 us (11%)
  local copies, waits for them, and re-layouts  1.65 us (1%)
    pallas_call x8, Pallas kernels, ring_step(): pl.pallas_call(functools.partial(step_kernel, smoothing, wide, offset % c...  26.1 us
    pallas_call x2, Pallas kernels, bulk(): pl.pallas_call(functools.partial(bulk_kernel, smoothing, wide, len(groups...  19.9 us
    all_to_all x1, blocking collectives, on_device(): lax.all_to_all(shares, PLANE, 0, 0)  16.9 us
    ppermute x12, starting transfers between devices, shift(): lax.ppermute(value, axes, [(i, (i + by) % size) for i in range(size)])  13.8 us
    all_to_all x1, blocking collectives, on_device(): lax.all_to_all(shares, RING, 0, 0)  10.7 us
    ppermute x7, starting transfers between devices, ring_shift(): lax.ppermute(value, RING, [(ring_index(z), ring_index((z + by) % size)) f...  8.75 us
    ppermute x12, waiting for transfers between devices, shift(): lax.ppermute(value, axes, [(i, (i + by) % size) for i in range(size)])  8.72 us
    all_to_all x1, starting transfers between devices, on_device(): targets = lax.all_to_all(coords, RING, 0, 0)  7.32 us
  transfers between devices with their start and end apart: 20, of which 9 were waited for; matrix products, arithmetic and copies ran while one was open for 0% of the time, Pallas kernels for 35%

profile of v6, /device:TPU:1, one launch (start us, length us, event | category | flops | bytes accessed | tf_op | source)
XLA Modules:
  0.0 121.0 jit_solution(13187669656720824185)
XLA Ops:
  2.9 3.6 %collective-permute-start.2 = (f32[136,256]{1,0:T(8,128)S(1)}, f32[136,256]{1,0:T(8,128)S(1)}, u32[]{:S(2)}, u32[]{:S(2)}) collective-permute-start(f32[136,256]{1,0:T(8,128)S(1)} %get-tuple-element.23), channel_id=1, source_target_pairs={{0,128},{64,192},{128,0},{192,64},{1,129},{65,193},{129,1},{193,65... | collective-permute-start | bytes 417800 | tf_op jit(solution)/shard_map/ppermute | solution.py:25
  8.9 3.9 %collective-permute-done.1 = f32[136,256]{1,0:T(8,128)S(1)} collective-permute-done((f32[136,256]{1,0:T(8,128)S(1)}, f32[136,256]{1,0:T(8,128)S(1)}, u32[]{:S(2)}, u32[]{:S(2)}) %collective-permute-start.1) | collective-permute-done | bytes 139296 | tf_op jit(solution)/shard_map/ppermute | solution.py:25
  12.8 2.2 %collective-permute-done = f32[136,256]{1,0:T(8,128)S(1)} collective-permute-done((f32[136,256]{1,0:T(8,128)S(1)}, f32[136,256]{1,0:T(8,128)S(1)}, u32[]{:S(2)}, u32[]{:S(2)}) %collective-permute-start) | collective-permute-done | bytes 139296 | tf_op jit(solution)/shard_map/ppermute | solution.py:25
  16.0 7.3 %all-to-all-start = ((f32[8,8,256]{2,1,0:T(8,128)}), f32[8,8,256]{2,1,0:T(8,128)S(1)}, u32[]{:S(2)}, u32[]{:S(2)}) async-start(f32[8,8,256]{2,1,0:T(8,128)} %get-tuple-element.28), calls=%async_computation | async-start | bytes 131072 | tf_op jit(solution)/shard_map/all_to_all | solution.py:280
  23.3 2.7 %collective-permute-start.5 = (f32[4,136,256]{2,1,0:T(8,128)S(1)}, f32[4,136,256]{2,1,0:T(8,128)S(1)}, u32[]{:S(2)}, u32[]{:S(2)}) collective-permute-start(f32[4,136,256]{2,1,0:T(8,128)S(1)} %pad_maximum_fusion.refs_0_), channel_id=1, source_target_pairs={{0,12},{4,0},{8,4},{12,8},{1,13},{5,1},{9,5},{13,9},{2,14},{6,2},{... | collective-permute-start | bytes 1671176 | tf_op jit(solution)/shard_map/ppermute | solution.py:25
  26.1 4.0 %all-to-all-done.refs_2_.refs_6_.refs_4_ = f32[8,8,256]{2,1,0:T(8,128)S(1)} async-done(((f32[8,8,256]{2,1,0:T(8,128)}), f32[8,8,256]{2,1,0:T(8,128)S(1)}, u32[]{:S(2)}, u32[]{:S(2)}) %all-to-all-start) | async-done | bytes 65568 | tf_op jit(solution)/shard_map/all_to_all | solution.py:280
  30.1 10.4 %bulk.2.refs_3_ = f32[2048,128]{1,0:T(8,128)S(1)} custom-call(s32[1]{0:T(128)} %bitcast.here, f32[4,136,256]{2,1,0:T(8,128)S(1)} %pad_maximum_fusion.refs_0_, f32[4,136,256]{2,1,0:T(8,128)S(1)} %collective-permute-done.3.refs_1_, f32[8,8,256]{2,1,0:T(8,128)S(1)} %all-to-all-done.refs_2_.refs_6_.refs_4_), custom_call_target="tpu_custom_call" | custom-call | flops 8589934592 | bytes 1048576 | tf_op jit(solution)/shard_map/bulk/pallas_call | solution.py:170
  40.9 1.5 %collective-permute-start.6 = (f32[4,136,256]{2,1,0:T(8,128)S(1)}, f32[4,136,256]{2,1,0:T(8,128)S(1)}, u32[]{:S(2)}, u32[]{:S(2)}) collective-permute-start(f32[4,136,256]{2,1,0:T(8,128)S(1)} %collective-permute-done.4.refs_0_), channel_id=1, source_target_pairs={{0,16},{16,0},{1,17},{17,1},{2,18},{18,2},{3,19},{19,3},{4,20},{20... | collective-permute-start | bytes 1671176 | tf_op jit(solution)/shard_map/ppermute | solution.py:25
  42.6 2.4 %collective-permute-start.9 = (f32[2,136,256]{2,1,0:T(8,128)S(1)}, f32[2,136,256]{2,1,0:T(8,128)S(1)}, u32[]{:S(2)}, u32[]{:S(2)}) collective-permute-start(f32[2,136,256]{2,1,0:T(8,128)S(1)} %slice.7), channel_id=1, source_target_pairs={{0,12},{4,0},{8,4},{12,8},{1,13},{5,1},{9,5},{13,9},{2,14},{6,2},{... | collective-permute-start | bytes 835592 | tf_op jit(solution)/shard_map/ppermute | solution.py:25
  44.9 9.5 %bulk.3 = (f32[2048,128]{1,0:T(8,128)S(1)}, bf16[256,2048]{1,0:T(8,128)(2,1)S(1)}, f32[24,2048]{1,0:T(8,128)S(1)}) custom-call(s32[1]{0:T(128)} %bitcast.here, f32[4,136,256]{2,1,0:T(8,128)S(1)} %collective-permute-done.4.refs_0_, f32[4,136,256]{2,1,0:T(8,128)S(1)} %collective-permute-done.5.refs_1_, f32[8,8,256]{2,1,0:T(8,128)S(1)} %all-to-all-done.refs_2_.refs_6_.refs_4_, ...), custom_call_target="tpu_custom_call" | custom-call | flops 8589934592 | bytes 1048576 | tf_op jit(solution)/shard_map/bulk/pallas_call | solution.py:170
  56.8 3.3 %ring_step.8 = (f32[256,128]{1,0:T(8,128)S(1)}, bf16[256,4096]{1,0:T(8,128)(2,1)S(1)}, f32[24,4096]{1,0:T(8,128)S(1)}) custom-call(s32[1]{0:T(128)} %bitcast.here, f32[4,136,256]{2,1,0:T(8,128)S(1)} %collective-permute-done.6.refs_0_, f32[4,136,256]{2,1,0:T(8,128)S(1)} %collective-permute-done.7.refs_1_, f32[2,136,256]{2,1,0:T(8,128)S(1)} %collective-permute-done.8.refs_2_, ...), custom_call_target="tpu_custom_call" | custom-call | flops 2147483648 | bytes 131072 | tf_op jit(solution)/shard_map/ring_step/pallas_call | solution.py:196
  60.2 1.0 collective-permute-start.12
  61.2 3.0 %ring_step.13 = f32[256,128]{1,0:T(8,128)S(1)} custom-call(s32[1]{0:T(128)} %bitcast.here, bf16[256,4096]{1,0:T(8,128)(2,1)S(1)} %get-tuple-element.38.refs_2_.refs_0_, f32[24,4096]{1,0:T(8,128)S(1)} %get-tuple-element.39.refs_3_.refs_1_, f32[8,8,256]{2,1,0:T(8,128)S(1)} %all-to-all-done.refs_2_.refs_6_.refs_4_, ...), custom_call_target="tpu_custom_call" | custom-call | flops 2147483648 | bytes 131072 | tf_op jit(solution)/shard_map/ring_step/pallas_call | solution.py:196
  64.2 1.8 %collective-permute-start.16 = (f32[256,128]{1,0:T(8,128)S(1)}, f32[256,128]{1,0:T(8,128)S(1)}, u32[]{:S(2)}, u32[]{:S(2)}) collective-permute-start(f32[256,128]{1,0:T(8,128)S(1)} %ring_step.13), channel_id=1, source_target_pairs={{0,35},{32,0},{1,32},{33,1},{2,33},{34,2},{3,34},{35,3},{4,39},{36... | collective-permute-start | bytes 393224 | tf_op jit(solution)/shard_map/ppermute | solution.py:34
  66.2 3.0 %ring_step.10 = f32[256,128]{1,0:T(8,128)S(1)} custom-call(s32[1]{0:T(128)} %bitcast.here, bf16[256,4096]{1,0:T(8,128)(2,1)S(1)} %get-tuple-element.38.refs_2_.refs_0_, f32[24,4096]{1,0:T(8,128)S(1)} %get-tuple-element.39.refs_3_.refs_1_, f32[8,8,256]{2,1,0:T(8,128)S(1)} %all-to-all-done.refs_2_.refs_6_.refs_4_, ...), custom_call_target="tpu_custom_call" | custom-call | flops 2147483648 | bytes 131072 | tf_op jit(solution)/shard_map/ring_step/pallas_call | solution.py:196
  69.3 3.0 %ring_step.14 = f32[256,128]{1,0:T(8,128)S(1)} custom-call(s32[1]{0:T(128)} %bitcast.here, bf16[256,4096]{1,0:T(8,128)(2,1)S(1)} %get-tuple-element.38.refs_2_.refs_0_, f32[24,4096]{1,0:T(8,128)S(1)} %get-tuple-element.39.refs_3_.refs_1_, f32[8,8,256]{2,1,0:T(8,128)S(1)} %all-to-all-done.refs_2_.refs_6_.refs_4_, ...), custom_call_target="tpu_custom_call" | custom-call | flops 2147483648 | bytes 131072 | tf_op jit(solution)/shard_map/ring_step/pallas_call | solution.py:196
  72.3 2.7 %collective-permute-start.17 = (f32[256,128]{1,0:T(8,128)S(1)}, f32[256,128]{1,0:T(8,128)S(1)}, u32[]{:S(2)}, u32[]{:S(2)}) collective-permute-start(f32[256,128]{1,0:T(8,128)S(1)} %ring_step.14), channel_id=1, source_target_pairs={{0,35},{32,0},{1,32},{33,1},{2,33},{34,2},{3,34},{35,3},{4,39},{36... | collective-permute-start | bytes 393224 | tf_op jit(solution)/shard_map/ppermute | solution.py:34
  75.0 3.0 %ring_step.11 = f32[256,128]{1,0:T(8,128)S(1)} custom-call(s32[1]{0:T(128)} %bitcast.here, bf16[256,4096]{1,0:T(8,128)(2,1)S(1)} %get-tuple-element.38.refs_2_.refs_0_, f32[24,4096]{1,0:T(8,128)S(1)} %get-tuple-element.39.refs_3_.refs_1_, f32[8,8,256]{2,1,0:T(8,128)S(1)} %all-to-all-done.refs_2_.refs_6_.refs_4_, ...), custom_call_target="tpu_custom_call" | custom-call | flops 2147483648 | bytes 131072 | tf_op jit(solution)/shard_map/ring_step/pallas_call | solution.py:196
  78.2 3.0 %ring_step.15 = f32[256,128]{1,0:T(8,128)S(1)} custom-call(s32[1]{0:T(128)} %bitcast.here, bf16[256,4096]{1,0:T(8,128)(2,1)S(1)} %get-tuple-element.38.refs_2_.refs_0_, f32[24,4096]{1,0:T(8,128)S(1)} %get-tuple-element.39.refs_3_.refs_1_, f32[8,8,256]{2,1,0:T(8,128)S(1)} %all-to-all-done.refs_2_.refs_6_.refs_4_, ...), custom_call_target="tpu_custom_call" | custom-call | flops 2147483648 | bytes 131072 | tf_op jit(solution)/shard_map/ring_step/pallas_call | solution.py:196
  81.1 2.7 %collective-permute-start.18 = (f32[256,128]{1,0:T(8,128)S(1)}, f32[256,128]{1,0:T(8,128)S(1)}, u32[]{:S(2)}, u32[]{:S(2)}) collective-permute-start(f32[256,128]{1,0:T(8,128)S(1)} %ring_step.15), channel_id=1, source_target_pairs={{0,35},{32,0},{1,32},{33,1},{2,33},{34,2},{3,34},{35,3},{4,39},{36... | collective-permute-start | bytes 393224 | tf_op jit(solution)/shard_map/ppermute | solution.py:34
  83.9 3.0 %ring_step.12 = f32[256,128]{1,0:T(8,128)S(1)} custom-call(s32[1]{0:T(128)} %bitcast.here, bf16[256,4096]{1,0:T(8,128)(2,1)S(1)} %get-tuple-element.38.refs_2_.refs_0_, f32[24,4096]{1,0:T(8,128)S(1)} %get-tuple-element.39.refs_3_.refs_1_, f32[8,8,256]{2,1,0:T(8,128)S(1)} %all-to-all-done.refs_2_.refs_6_.refs_4_, ...), custom_call_target="tpu_custom_call" | custom-call | flops 2147483648 | bytes 131072 | tf_op jit(solution)/shard_map/ring_step/pallas_call | solution.py:196
  87.2 4.8 %ring_step.9.own = f32[256,128]{1,0:T(8,128)S(1)} custom-call(s32[1]{0:T(128)} %bitcast.here, bf16[256,2048]{1,0:T(8,128)(2,1)S(1)} %get-tuple-element.32.refs_0_, f32[24,2048]{1,0:T(8,128)S(1)} %get-tuple-element.33.refs_1_, bf16[256,4096]{1,0:T(8,128)(2,1)S(1)} %get-tuple-element.38.refs_2_.refs_0_, f32[24,4096]{1,0:T(8,128)S(1)} %get-tuple-element.39.refs_3_.refs_1_, ...), custom_call_target="tpu_custom_call" | custom-call | flops 3221225472 | bytes 131072 | tf_op jit(solution)/shard_map/ring_step/pallas_call | solution.py:196
  92.5 16.9 %all_to_all.15.parts = f32[32,1,512]{2,1,0:T(1,128)S(1)} all-to-all(f32[32,1,512]{2,1,0:T(1,128)S(1)} %get-tuple-element.41), channel_id=1, replica_groups=mesh['x'=4,'zl'=2,'c'=2,'y'=4,'zh'=4] {'x','c','y'}, dimensions={0} | all-to-all | bytes 131072 | tf_op jit(solution)/shard_map/all_to_all | solution.py:321
  109.4 10.7 %all_to_all.16.sums_ref = f32[8,1,512]{2,1,0:T(1,128)S(1)} all-to-all(f32[8,1,512]{2,1,0:T(1,128)S(1)} %spread.1), channel_id=1, replica_groups=mesh['x'=4,'zl'=2,'c'=2,'y'=4,'zh'=4] {'zl','zh'}, dimensions={0} | all-to-all | bytes 32768 | tf_op jit(solution)/shard_map/all_to_all | solution.py:329
  (47 shorter events, 10.5 us)
Async XLA Ops:
  2.9 6.0 %collective-permute-start.2 = (f32[136,256]{1,0:T(8,128)S(1)}, f32[136,256]{1,0:T(8,128)S(1)}, u32[]{:S(2)}, u32[]{:S(2)}) collective-permute-start(f32[136,256]{1,0:T(8,128)S(1)} %get-tuple-element.23), channel_id=1, source_target_pairs={{0,128},{64,192},{128,0},{192,64},{1,129},{65,193},{129,1},{193,65... | collective-permute-start | bytes 417800 | tf_op jit(solution)/shard_map/ppermute | solution.py:25
  6.4 6.4 %collective-permute-start.1 = (f32[136,256]{1,0:T(8,128)S(1)}, f32[136,256]{1,0:T(8,128)S(1)}, u32[]{:S(2)}, u32[]{:S(2)}) collective-permute-start(f32[136,256]{1,0:T(8,128)S(1)} %get-tuple-element.23), channel_id=1, source_target_pairs={{0,192},{64,0},{128,64},{192,128},{1,193},{65,1},{129,65},{193,129... | collective-permute-start | bytes 417800 | tf_op jit(solution)/shard_map/ppermute | solution.py:25
  7.3 7.7 %collective-permute-start = (f32[136,256]{1,0:T(8,128)S(1)}, f32[136,256]{1,0:T(8,128)S(1)}, u32[]{:S(2)}, u32[]{:S(2)}) collective-permute-start(f32[136,256]{1,0:T(8,128)S(1)} %get-tuple-element.23), channel_id=1, source_target_pairs={{0,64},{64,128},{128,192},{192,0},{1,65},{65,129},{129,193},{193,1... | collective-permute-start | bytes 417800 | tf_op jit(solution)/shard_map/ppermute | solution.py:25
  15.0 15.1 %collective-permute-start.3 = (f32[4,136,256]{2,1,0:T(8,128)S(1)}, f32[4,136,256]{2,1,0:T(8,128)S(1)}, u32[]{:S(2)}, u32[]{:S(2)}) collective-permute-start(f32[4,136,256]{2,1,0:T(8,128)S(1)} %pad_maximum_fusion.refs_0_), channel_id=1, source_target_pairs={{0,16},{16,0},{1,17},{17,1},{2,18},{18,2},{3,19},{19,3},{4,20},{20... | collective-permute-start | bytes 1671176 | tf_op jit(solution)/shard_map/ppermute | solution.py:25
  16.0 14.1 %all-to-all-start = ((f32[8,8,256]{2,1,0:T(8,128)}), f32[8,8,256]{2,1,0:T(8,128)S(1)}, u32[]{:S(2)}, u32[]{:S(2)}) async-start(f32[8,8,256]{2,1,0:T(8,128)} %get-tuple-element.28), calls=%async_computation | async-start | bytes 131072 | tf_op jit(solution)/shard_map/all_to_all | solution.py:280
  23.3 17.2 %collective-permute-start.5 = (f32[4,136,256]{2,1,0:T(8,128)S(1)}, f32[4,136,256]{2,1,0:T(8,128)S(1)}, u32[]{:S(2)}, u32[]{:S(2)}) collective-permute-start(f32[4,136,256]{2,1,0:T(8,128)S(1)} %pad_maximum_fusion.refs_0_), channel_id=1, source_target_pairs={{0,12},{4,0},{8,4},{12,8},{1,13},{5,1},{9,5},{13,9},{2,14},{6,2},{... | collective-permute-start | bytes 1671176 | tf_op jit(solution)/shard_map/ppermute | solution.py:25
  26.1 14.8 %collective-permute-start.4 = (f32[4,136,256]{2,1,0:T(8,128)S(1)}, f32[4,136,256]{2,1,0:T(8,128)S(1)}, u32[]{:S(2)}, u32[]{:S(2)}) collective-permute-start(f32[4,136,256]{2,1,0:T(8,128)S(1)} %pad_maximum_fusion.refs_0_), channel_id=1, source_target_pairs={{0,4},{4,8},{8,12},{12,0},{1,5},{5,9},{9,13},{13,1},{2,6},{6,10},{... | collective-permute-start | bytes 1671176 | tf_op jit(solution)/shard_map/ppermute | solution.py:25
  40.9 14.6 %collective-permute-start.6 = (f32[4,136,256]{2,1,0:T(8,128)S(1)}, f32[4,136,256]{2,1,0:T(8,128)S(1)}, u32[]{:S(2)}, u32[]{:S(2)}) collective-permute-start(f32[4,136,256]{2,1,0:T(8,128)S(1)} %collective-permute-done.4.refs_0_), channel_id=1, source_target_pairs={{0,16},{16,0},{1,17},{17,1},{2,18},{18,2},{3,19},{19,3},{4,20},{20... | collective-permute-start | bytes 1671176 | tf_op jit(solution)/shard_map/ppermute | solution.py:25
  42.4 13.1 %collective-permute-start.7 = (f32[4,136,256]{2,1,0:T(8,128)S(1)}, f32[4,136,256]{2,1,0:T(8,128)S(1)}, u32[]{:S(2)}, u32[]{:S(2)}) collective-permute-start(f32[4,136,256]{2,1,0:T(8,128)S(1)} %collective-permute-done.5.refs_1_), channel_id=1, source_target_pairs={{0,16},{16,0},{1,17},{17,1},{2,18},{18,2},{3,19},{19,3},{4,20},{20... | collective-permute-start | bytes 1671176 | tf_op jit(solution)/shard_map/ppermute | solution.py:25
  42.6 11.9 %collective-permute-start.9 = (f32[2,136,256]{2,1,0:T(8,128)S(1)}, f32[2,136,256]{2,1,0:T(8,128)S(1)}, u32[]{:S(2)}, u32[]{:S(2)}) collective-permute-start(f32[2,136,256]{2,1,0:T(8,128)S(1)} %slice.7), channel_id=1, source_target_pairs={{0,12},{4,0},{8,4},{12,8},{1,13},{5,1},{9,5},{13,9},{2,14},{6,2},{... | collective-permute-start | bytes 835592 | tf_op jit(solution)/shard_map/ppermute | solution.py:25
  44.9 9.5 %collective-permute-start.8 = (f32[2,136,256]{2,1,0:T(8,128)S(1)}, f32[2,136,256]{2,1,0:T(8,128)S(1)}, u32[]{:S(2)}, u32[]{:S(2)}) collective-permute-start(f32[2,136,256]{2,1,0:T(8,128)S(1)} %slice.6), channel_id=1, source_target_pairs={{0,4},{4,8},{8,12},{12,0},{1,5},{5,9},{9,13},{13,1},{2,6},{6,10},{... | collective-permute-start | bytes 835592 | tf_op jit(solution)/shard_map/ppermute | solution.py:25
  54.5 2.0 %collective-permute-start.10 = (f32[2,136,256]{2,1,0:T(8,128)S(1)}, f32[2,136,256]{2,1,0:T(8,128)S(1)}, u32[]{:S(2)}, u32[]{:S(2)}) collective-permute-start(f32[2,136,256]{2,1,0:T(8,128)S(1)} %collective-permute-done.8.refs_2_), channel_id=1, source_target_pairs={{0,16},{16,0},{1,17},{17,1},{2,18},{18,2},{3,19},{19,3},{4,20},{20... | collective-permute-start | bytes 835592 | tf_op jit(solution)/shard_map/ppermute | solution.py:25
  55.2 1.6 %collective-permute-start.11 = (f32[2,136,256]{2,1,0:T(8,128)S(1)}, f32[2,136,256]{2,1,0:T(8,128)S(1)}, u32[]{:S(2)}, u32[]{:S(2)}) collective-permute-start(f32[2,136,256]{2,1,0:T(8,128)S(1)} %collective-permute-done.9.refs_3_), channel_id=1, source_target_pairs={{0,16},{16,0},{1,17},{17,1},{2,18},{18,2},{3,19},{19,3},{4,20},{20... | collective-permute-start | bytes 835592 | tf_op jit(solution)/shard_map/ppermute | solution.py:25
  60.2 6.0 %collective-permute-start.12 = (f32[256,128]{1,0:T(8,128)S(1)}, f32[256,128]{1,0:T(8,128)S(1)}, u32[]{:S(2)}, u32[]{:S(2)}) collective-permute-start(f32[256,128]{1,0:T(8,128)S(1)} %get-tuple-element.40), channel_id=1, source_target_pairs={{0,32},{32,1},{1,33},{33,2},{2,34},{34,3},{3,35},{35,0},{4,36},{36... | collective-permute-start | bytes 393224 | tf_op jit(solution)/shard_map/ppermute | solution.py:34
  64.2 5.1 %collective-permute-start.16 = (f32[256,128]{1,0:T(8,128)S(1)}, f32[256,128]{1,0:T(8,128)S(1)}, u32[]{:S(2)}, u32[]{:S(2)}) collective-permute-start(f32[256,128]{1,0:T(8,128)S(1)} %ring_step.13), channel_id=1, source_target_pairs={{0,35},{32,0},{1,32},{33,1},{2,33},{34,2},{3,34},{35,3},{4,39},{36... | collective-permute-start | bytes 393224 | tf_op jit(solution)/shard_map/ppermute | solution.py:34
  69.2 5.9 %collective-permute-start.13 = (f32[256,128]{1,0:T(8,128)S(1)}, f32[256,128]{1,0:T(8,128)S(1)}, u32[]{:S(2)}, u32[]{:S(2)}) collective-permute-start(f32[256,128]{1,0:T(8,128)S(1)} %ring_step.10), channel_id=1, source_target_pairs={{0,32},{32,1},{1,33},{33,2},{2,34},{34,3},{3,35},{35,0},{4,36},{36... | collective-permute-start | bytes 393224 | tf_op jit(solution)/shard_map/ppermute | solution.py:34
  72.3 5.8 %collective-permute-start.17 = (f32[256,128]{1,0:T(8,128)S(1)}, f32[256,128]{1,0:T(8,128)S(1)}, u32[]{:S(2)}, u32[]{:S(2)}) collective-permute-start(f32[256,128]{1,0:T(8,128)S(1)} %ring_step.14), channel_id=1, source_target_pairs={{0,35},{32,0},{1,32},{33,1},{2,33},{34,2},{3,34},{35,3},{4,39},{36... | collective-permute-start | bytes 393224 | tf_op jit(solution)/shard_map/ppermute | solution.py:34
  78.1 5.8 %collective-permute-start.14 = (f32[256,128]{1,0:T(8,128)S(1)}, f32[256,128]{1,0:T(8,128)S(1)}, u32[]{:S(2)}, u32[]{:S(2)}) collective-permute-start(f32[256,128]{1,0:T(8,128)S(1)} %ring_step.11), channel_id=1, source_target_pairs={{0,32},{32,1},{1,33},{33,2},{2,34},{34,3},{3,35},{35,0},{4,36},{36... | collective-permute-start | bytes 393224 | tf_op jit(solution)/shard_map/ppermute | solution.py:34
  81.1 10.9 %collective-permute-start.18 = (f32[256,128]{1,0:T(8,128)S(1)}, f32[256,128]{1,0:T(8,128)S(1)}, u32[]{:S(2)}, u32[]{:S(2)}) collective-permute-start(f32[256,128]{1,0:T(8,128)S(1)} %ring_step.15), channel_id=1, source_target_pairs={{0,35},{32,0},{1,32},{33,1},{2,33},{34,2},{3,34},{35,3},{4,39},{36... | collective-permute-start | bytes 393224 | tf_op jit(solution)/shard_map/ppermute | solution.py:34
  86.9 5.3 %collective-permute-start.15 = (f32[256,128]{1,0:T(8,128)S(1)}, f32[256,128]{1,0:T(8,128)S(1)}, u32[]{:S(2)}, u32[]{:S(2)}) collective-permute-start(f32[256,128]{1,0:T(8,128)S(1)} %ring_step.12), channel_id=1, source_target_pairs={{0,32},{32,1},{1,33},{33,2},{2,34},{34,3},{3,35},{35,0},{4,36},{36... | collective-permute-start | bytes 393224 | tf_op jit(solution)/shard_map/ppermute | solution.py:34
  87.2 5.0 %copy-start.1 = (f32[128,256]{1,0:T(8,128)S(1)}, f32[128,256]{1,0:T(8,128)}, u32[]{:S(2)}) copy-start(f32[128,256]{1,0:T(8,128)} %direction_ref.3) | copy-start | bytes 393220
  87.2 5.0 %copy-start.2 = (f32[128,256]{1,0:T(8,128)S(1)}, f32[128,256]{1,0:T(8,128)}, u32[]{:S(2)}) copy-start(f32[128,256]{1,0:T(8,128)} %residual_ref.3) | copy-start | bytes 393220
  87.2 5.0 %copy-start.5 = (f32[256]{0:T(256)S(1)}, f32[256]{0:T(256)}, u32[]{:S(2)}) copy-start(f32[256]{0:T(256)} %param.6) | copy-start | bytes 3076
  87.2 32.9 %copy-start.3 = (f32[128,256]{1,0:T(8,128)S(1)}, f32[128,256]{1,0:T(8,128)}, u32[]{:S(2)}) copy-start(f32[128,256]{1,0:T(8,128)} %solution_ref.1) | copy-start | bytes 393220
  (2 other events, 1.6 us)

commit v7 on v6

--- a/solution.py
+++ b/solution.py
@@ -13,7 +13,7 @@
 RING = ("zl", "zh")
 PLANE = ("x", "c", "y")
 PART = 256
-LANES = 256
+LANES = 1024
 COORDS = 8
 KERNEL_VMEM = 10 * 2**20
 VMEM = pl.BlockSpec(memory_space=pltpu.VMEM)
@@ -63,17 +63,18 @@
 
     def make(place, tile):
         first, column = place
+        step = min(wide, LANES)
         for r in range(0, PART, 16):
-            here = [jnp.broadcast_to(columns[pl.ds(first + r, 16), i : i + 1], (16, LANES)) for i in range(3)]
-            for c in range(0, wide, LANES):
-                lanes = pl.ds(column + c, LANES)
+            here = [jnp.broadcast_to(columns[pl.ds(first + r, 16), i : i + 1], (16, step)) for i in range(3)]
+            for c in range(0, wide, step):
+                lanes = pl.ds(column + c, step)
                 far = [jnp.concatenate([rows[8 * i : 8 * i + 8, lanes]] * 2, axis=0) for i in range(3)]
                 dx, dy, dz = (far[i] - here[i] for i in range(3))
                 kernel = lax.rsqrt(dx * dx + dy * dy + (dz * dz + smoothing * smoothing))
                 high = kernel.astype(jnp.bfloat16)
                 low = (kernel - high.astype(jnp.float32)).astype(jnp.bfloat16)
-                tile[r : r + 16, c : c + LANES] = high
-                tile[PART + r : PART + r + 16, c : c + LANES] = low
+                tile[r : r + 16, c : c + step] = high
+                tile[PART + r : PART + r + 16, c : c + step] = low
 
     def multiply(place, tile):
         first, column = place
@@ -275,9 +276,9 @@
         compiler_params=small,
         name="pack",
     )(points, direction)
+    targets = lax.all_to_all(coords, RING, 0, 0)
     near = [shift(mine, "x", 1), shift(mine, "x", -1), shift(mine, "x", 2)]
-    coords, *near = lax.optimization_barrier((coords, *near))
-    targets = lax.all_to_all(coords, RING, 0, 0)
+    targets, *near[1:] = lax.optimization_barrier((targets, *near[1:]))
     line = jnp.stack([mine, *near])
     above, below = shift(line, "y", 1), shift(line, "y", -1)
     (sums,) = bulk(here, [line, shift(line, "c", 1)], targets, None, smoothing)

time: 121 us -> 119 us (0.983)
  blocking collectives: 27.7 us -> 39.1 us
  waiting for transfers between devices: 13.1 us -> 6.28 us
  starting transfers between devices: 29.9 us -> 23.9 us
    all_to_all x0 -> x1, blocking collectives: none -> 14.6 us  [on_device(): targets = lax.all_to_all(coords, RING, 0, 0)]
    all_to_all x1 -> x0, starting transfers between devices: 7.32 us -> none  [on_device(): targets = lax.all_to_all(coords, RING, 0, 0)]
    all_to_all x1 -> x0, waiting for transfers between devices: 4.02 us -> none  [on_device(): targets = lax.all_to_all(coords, RING, 0, 0)]
    ppermute x12, waiting for transfers between devices: 8.72 us -> 5.88 us  [shift(): lax.ppermute(value, axes, [(i, (i + by) % size) for i in range(size)])]
    all_to_all x1, blocking collectives: 16.9 us -> 15.3 us  [on_device(): lax.all_to_all(shares, PLANE, 0, 0)]
    all_to_all x1, blocking collectives: 10.7 us -> 9.21 us  [on_device(): lax.all_to_all(shares, RING, 0, 0)]
    ppermute x12, starting transfers between devices: 13.8 us -> 15.2 us  [shift(): lax.ppermute(value, axes, [(i, (i + by) % size) for i in range(size)])]
  transfers between devices with their start and end apart: 20 -> 19, of which waited for: 9 -> 6; matrix products, arithmetic and copies ran while one was open for 0% -> 0% of each run, Pallas kernels for 35% -> 36%
where the time goes in v7:
time: 119 us
  Pallas kernels  47.2 us (40%)
  blocking collectives  39.1 us (33%)
  starting transfers between devices  23.9 us (20%)
  waiting for transfers between devices  6.28 us (5%)
  local copies, waits for them, and re-layouts  1.65 us (1%)
    pallas_call x8, Pallas kernels, ring_step(): pl.pallas_call(functools.partial(step_kernel, smoothing, wide, offset % c...  26 us
    pallas_call x2, Pallas kernels, bulk(): pl.pallas_call(functools.partial(bulk_kernel, smoothing, wide, len(groups...  20.1 us
    all_to_all x1, blocking collectives, on_device(): lax.all_to_all(shares, PLANE, 0, 0)  15.3 us
    ppermute x12, starting transfers between devices, shift(): lax.ppermute(value, axes, [(i, (i + by) % size) for i in range(size)])  15.2 us
    all_to_all x1, blocking collectives, on_device(): targets = lax.all_to_all(coords, RING, 0, 0)  14.6 us
    all_to_all x1, blocking collectives, on_device(): lax.all_to_all(shares, RING, 0, 0)  9.21 us
    ppermute x7, starting transfers between devices, ring_shift(): lax.ppermute(value, RING, [(ring_index(z), ring_index((z + by) % size)) f...  8.75 us
    ppermute x12, waiting for transfers between devices, shift(): lax.ppermute(value, axes, [(i, (i + by) % size) for i in range(size)])  5.88 us
  transfers between devices with their start and end apart: 19, of which 6 were waited for; matrix products, arithmetic and copies ran while one was open for 0% of the time, Pallas kernels for 36%

profile of v7, /device:TPU:1, one launch (start us, length us, event | category | flops | bytes accessed | tf_op | source)
XLA Modules:
  0.0 119.0 jit_solution(15220466298486992971)
XLA Ops:
  2.2 3.7 %collective-permute-start.2 = (f32[136,256]{1,0:T(8,128)S(1)}, f32[136,256]{1,0:T(8,128)S(1)}, u32[]{:S(2)}, u32[]{:S(2)}) collective-permute-start(f32[136,256]{1,0:T(8,128)S(1)} %get-tuple-element.22), channel_id=1, source_target_pairs={{0,128},{64,192},{128,0},{192,64},{1,129},{65,193},{129,1},{193,65... | collective-permute-start | bytes 417800 | tf_op jit(solution)/shard_map/ppermute | solution.py:25
  7.4 14.6 %all_to_all.15.refs_2_.refs_6_.refs_4_ = f32[8,8,256]{2,1,0:T(8,128)S(1)} all-to-all(f32[8,8,256]{2,1,0:T(8,128)S(1)} %get-tuple-element.23), channel_id=1, replica_groups=mesh['x'=4,'zl'=2,'c'=2,'y'=4,'zh'=4] {'zl','zh'}, dimensions={0} | all-to-all | bytes 131072 | tf_op jit(solution)/shard_map/all_to_all | solution.py:279
  22.0 3.0 %collective-permute-start.3 = (f32[4,136,256]{2,1,0:T(8,128)S(1)}, f32[4,136,256]{2,1,0:T(8,128)S(1)}, u32[]{:S(2)}, u32[]{:S(2)}) collective-permute-start(f32[4,136,256]{2,1,0:T(8,128)S(1)} %pad_maximum_fusion.refs_0_), channel_id=1, source_target_pairs={{0,16},{16,0},{1,17},{17,1},{2,18},{18,2},{3,19},{19,3},{4,20},{20... | collective-permute-start | bytes 1671176 | tf_op jit(solution)/shard_map/ppermute | solution.py:25
  25.1 2.8 %collective-permute-start.5 = (f32[4,136,256]{2,1,0:T(8,128)S(1)}, f32[4,136,256]{2,1,0:T(8,128)S(1)}, u32[]{:S(2)}, u32[]{:S(2)}) collective-permute-start(f32[4,136,256]{2,1,0:T(8,128)S(1)} %pad_maximum_fusion.refs_0_), channel_id=1, source_target_pairs={{0,12},{4,0},{8,4},{12,8},{1,13},{5,1},{9,5},{13,9},{2,14},{6,2},{... | collective-permute-start | bytes 1671176 | tf_op jit(solution)/shard_map/ppermute | solution.py:25
  27.8 10.5 %bulk.2.refs_3_ = f32[2048,128]{1,0:T(8,128)S(1)} custom-call(s32[1]{0:T(128)} %bitcast.here, f32[4,136,256]{2,1,0:T(8,128)S(1)} %pad_maximum_fusion.refs_0_, f32[4,136,256]{2,1,0:T(8,128)S(1)} %collective-permute-done.3.refs_1_, f32[8,8,256]{2,1,0:T(8,128)S(1)} %all_to_all.15.refs_2_.refs_6_.refs_4_), custom_call_target="tpu_custom_call" | custom-call | flops 8589934592 | bytes 1048576 | tf_op jit(solution)/shard_map/bulk/pallas_call | solution.py:171
  38.3 1.5 %collective-permute-done.5.refs_1_ = f32[4,136,256]{2,1,0:T(8,128)S(1)} collective-permute-done((f32[4,136,256]{2,1,0:T(8,128)S(1)}, f32[4,136,256]{2,1,0:T(8,128)S(1)}, u32[]{:S(2)}, u32[]{:S(2)}) %collective-permute-start.5) | collective-permute-done | bytes 557088 | tf_op jit(solution)/shard_map/ppermute | solution.py:25
  39.8 3.1 %collective-permute-done.4.refs_0_ = f32[4,136,256]{2,1,0:T(8,128)S(1)} collective-permute-done((f32[4,136,256]{2,1,0:T(8,128)S(1)}, f32[4,136,256]{2,1,0:T(8,128)S(1)}, u32[]{:S(2)}, u32[]{:S(2)}) %collective-permute-start.4) | collective-permute-done | bytes 557088 | tf_op jit(solution)/shard_map/ppermute | solution.py:25
  42.9 1.3 %collective-permute-start.6 = (f32[4,136,256]{2,1,0:T(8,128)S(1)}, f32[4,136,256]{2,1,0:T(8,128)S(1)}, u32[]{:S(2)}, u32[]{:S(2)}) collective-permute-start(f32[4,136,256]{2,1,0:T(8,128)S(1)} %collective-permute-done.4.refs_0_), channel_id=1, source_target_pairs={{0,16},{16,0},{1,17},{17,1},{2,18},{18,2},{3,19},{19,3},{4,20},{20... | collective-permute-start | bytes 1671176 | tf_op jit(solution)/shard_map/ppermute | solution.py:25
  44.4 1.5 %collective-permute-start.8 = (f32[2,136,256]{2,1,0:T(8,128)S(1)}, f32[2,136,256]{2,1,0:T(8,128)S(1)}, u32[]{:S(2)}, u32[]{:S(2)}) collective-permute-start(f32[2,136,256]{2,1,0:T(8,128)S(1)} %slice.6), channel_id=1, source_target_pairs={{0,4},{4,8},{8,12},{12,0},{1,5},{5,9},{9,13},{13,1},{2,6},{6,10},{... | collective-permute-start | bytes 835592 | tf_op jit(solution)/shard_map/ppermute | solution.py:25
  45.8 9.6 %bulk.3 = (f32[2048,128]{1,0:T(8,128)S(1)}, bf16[256,2048]{1,0:T(8,128)(2,1)S(1)}, f32[24,2048]{1,0:T(8,128)S(1)}) custom-call(s32[1]{0:T(128)} %bitcast.here, f32[4,136,256]{2,1,0:T(8,128)S(1)} %collective-permute-done.4.refs_0_, f32[4,136,256]{2,1,0:T(8,128)S(1)} %collective-permute-done.5.refs_1_, f32[8,8,256]{2,1,0:T(8,128)S(1)} %all_to_all.15.refs_2_.refs_6_.refs_4_, ...), custom_call_target="tpu_custom_call" | custom-call | flops 8589934592 | bytes 1048576 | tf_op jit(solution)/shard_map/bulk/pallas_call | solution.py:171
  55.4 1.1 collective-permute-start.10
  58.1 3.3 %ring_step.8 = (f32[256,128]{1,0:T(8,128)S(1)}, bf16[256,4096]{1,0:T(8,128)(2,1)S(1)}, f32[24,4096]{1,0:T(8,128)S(1)}) custom-call(s32[1]{0:T(128)} %bitcast.here, f32[4,136,256]{2,1,0:T(8,128)S(1)} %collective-permute-done.6.refs_0_, f32[4,136,256]{2,1,0:T(8,128)S(1)} %collective-permute-done.7.refs_1_, f32[2,136,256]{2,1,0:T(8,128)S(1)} %collective-permute-done.8.refs_2_, ...), custom_call_target="tpu_custom_call" | custom-call | flops 2147483648 | bytes 131072 | tf_op jit(solution)/shard_map/ring_step/pallas_call | solution.py:197
  62.4 3.0 %ring_step.13 = f32[256,128]{1,0:T(8,128)S(1)} custom-call(s32[1]{0:T(128)} %bitcast.here, bf16[256,4096]{1,0:T(8,128)(2,1)S(1)} %get-tuple-element.36.refs_2_.refs_0_, f32[24,4096]{1,0:T(8,128)S(1)} %get-tuple-element.37.refs_3_.refs_1_, f32[8,8,256]{2,1,0:T(8,128)S(1)} %all_to_all.15.refs_2_.refs_6_.refs_4_, ...), custom_call_target="tpu_custom_call" | custom-call | flops 2147483648 | bytes 131072 | tf_op jit(solution)/shard_map/ring_step/pallas_call | solution.py:197
  65.4 1.9 %collective-permute-start.16 = (f32[256,128]{1,0:T(8,128)S(1)}, f32[256,128]{1,0:T(8,128)S(1)}, u32[]{:S(2)}, u32[]{:S(2)}) collective-permute-start(f32[256,128]{1,0:T(8,128)S(1)} %ring_step.13), channel_id=1, source_target_pairs={{0,35},{32,0},{1,32},{33,1},{2,33},{34,2},{3,34},{35,3},{4,39},{36... | collective-permute-start | bytes 393224 | tf_op jit(solution)/shard_map/ppermute | solution.py:34
  67.4 3.0 %ring_step.10 = f32[256,128]{1,0:T(8,128)S(1)} custom-call(s32[1]{0:T(128)} %bitcast.here, bf16[256,4096]{1,0:T(8,128)(2,1)S(1)} %get-tuple-element.36.refs_2_.refs_0_, f32[24,4096]{1,0:T(8,128)S(1)} %get-tuple-element.37.refs_3_.refs_1_, f32[8,8,256]{2,1,0:T(8,128)S(1)} %all_to_all.15.refs_2_.refs_6_.refs_4_, ...), custom_call_target="tpu_custom_call" | custom-call | flops 2147483648 | bytes 131072 | tf_op jit(solution)/shard_map/ring_step/pallas_call | solution.py:197
  70.5 3.0 %ring_step.14 = f32[256,128]{1,0:T(8,128)S(1)} custom-call(s32[1]{0:T(128)} %bitcast.here, bf16[256,4096]{1,0:T(8,128)(2,1)S(1)} %get-tuple-element.36.refs_2_.refs_0_, f32[24,4096]{1,0:T(8,128)S(1)} %get-tuple-element.37.refs_3_.refs_1_, f32[8,8,256]{2,1,0:T(8,128)S(1)} %all_to_all.15.refs_2_.refs_6_.refs_4_, ...), custom_call_target="tpu_custom_call" | custom-call | flops 2147483648 | bytes 131072 | tf_op jit(solution)/shard_map/ring_step/pallas_call | solution.py:197
  73.5 2.7 %collective-permute-start.17 = (f32[256,128]{1,0:T(8,128)S(1)}, f32[256,128]{1,0:T(8,128)S(1)}, u32[]{:S(2)}, u32[]{:S(2)}) collective-permute-start(f32[256,128]{1,0:T(8,128)S(1)} %ring_step.14), channel_id=1, source_target_pairs={{0,35},{32,0},{1,32},{33,1},{2,33},{34,2},{3,34},{35,3},{4,39},{36... | collective-permute-start | bytes 393224 | tf_op jit(solution)/shard_map/ppermute | solution.py:34
  76.3 3.0 %ring_step.11 = f32[256,128]{1,0:T(8,128)S(1)} custom-call(s32[1]{0:T(128)} %bitcast.here, bf16[256,4096]{1,0:T(8,128)(2,1)S(1)} %get-tuple-element.36.refs_2_.refs_0_, f32[24,4096]{1,0:T(8,128)S(1)} %get-tuple-element.37.refs_3_.refs_1_, f32[8,8,256]{2,1,0:T(8,128)S(1)} %all_to_all.15.refs_2_.refs_6_.refs_4_, ...), custom_call_target="tpu_custom_call" | custom-call | flops 2147483648 | bytes 131072 | tf_op jit(solution)/shard_map/ring_step/pallas_call | solution.py:197
  79.4 3.0 %ring_step.15 = f32[256,128]{1,0:T(8,128)S(1)} custom-call(s32[1]{0:T(128)} %bitcast.here, bf16[256,4096]{1,0:T(8,128)(2,1)S(1)} %get-tuple-element.36.refs_2_.refs_0_, f32[24,4096]{1,0:T(8,128)S(1)} %get-tuple-element.37.refs_3_.refs_1_, f32[8,8,256]{2,1,0:T(8,128)S(1)} %all_to_all.15.refs_2_.refs_6_.refs_4_, ...), custom_call_target="tpu_custom_call" | custom-call | flops 2147483648 | bytes 131072 | tf_op jit(solution)/shard_map/ring_step/pallas_call | solution.py:197
  82.3 2.7 %collective-permute-start.18 = (f32[256,128]{1,0:T(8,128)S(1)}, f32[256,128]{1,0:T(8,128)S(1)}, u32[]{:S(2)}, u32[]{:S(2)}) collective-permute-start(f32[256,128]{1,0:T(8,128)S(1)} %ring_step.15), channel_id=1, source_target_pairs={{0,35},{32,0},{1,32},{33,1},{2,33},{34,2},{3,34},{35,3},{4,39},{36... | collective-permute-start | bytes 393224 | tf_op jit(solution)/shard_map/ppermute | solution.py:34
  85.1 3.0 %ring_step.12 = f32[256,128]{1,0:T(8,128)S(1)} custom-call(s32[1]{0:T(128)} %bitcast.here, bf16[256,4096]{1,0:T(8,128)(2,1)S(1)} %get-tuple-element.36.refs_2_.refs_0_, f32[24,4096]{1,0:T(8,128)S(1)} %get-tuple-element.37.refs_3_.refs_1_, f32[8,8,256]{2,1,0:T(8,128)S(1)} %all_to_all.15.refs_2_.refs_6_.refs_4_, ...), custom_call_target="tpu_custom_call" | custom-call | flops 2147483648 | bytes 131072 | tf_op jit(solution)/shard_map/ring_step/pallas_call | solution.py:197
  88.4 4.7 %ring_step.9.own = f32[256,128]{1,0:T(8,128)S(1)} custom-call(s32[1]{0:T(128)} %bitcast.here, bf16[256,2048]{1,0:T(8,128)(2,1)S(1)} %get-tuple-element.30.refs_0_, f32[24,2048]{1,0:T(8,128)S(1)} %get-tuple-element.31.refs_1_, bf16[256,4096]{1,0:T(8,128)(2,1)S(1)} %get-tuple-element.36.refs_2_.refs_0_, f32[24,4096]{1,0:T(8,128)S(1)} %get-tuple-element.37.refs_3_.refs_1_, ...), custom_call_target="tpu_custom_call" | custom-call | flops 3221225472 | bytes 131072 | tf_op jit(solution)/shard_map/ring_step/pallas_call | solution.py:197
  93.6 15.3 %all_to_all.16.parts = f32[32,1,512]{2,1,0:T(1,128)S(1)} all-to-all(f32[32,1,512]{2,1,0:T(1,128)S(1)} %get-tuple-element.39), channel_id=1, replica_groups=mesh['x'=4,'zl'=2,'c'=2,'y'=4,'zh'=4] {'x','c','y'}, dimensions={0} | all-to-all | bytes 131072 | tf_op jit(solution)/shard_map/all_to_all | solution.py:322
  109.0 9.2 %all_to_all.17.sums_ref = f32[8,1,512]{2,1,0:T(1,128)S(1)} all-to-all(f32[8,1,512]{2,1,0:T(1,128)S(1)} %spread.1), channel_id=1, replica_groups=mesh['x'=4,'zl'=2,'c'=2,'y'=4,'zh'=4] {'zl','zh'}, dimensions={0} | all-to-all | bytes 32768 | tf_op jit(solution)/shard_map/all_to_all | solution.py:330
  (46 shorter events, 7.9 us)
Async XLA Ops:
  0.6 0.9 copy-start
  2.2 19.7 %collective-permute-start.2 = (f32[136,256]{1,0:T(8,128)S(1)}, f32[136,256]{1,0:T(8,128)S(1)}, u32[]{:S(2)}, u32[]{:S(2)}) collective-permute-start(f32[136,256]{1,0:T(8,128)S(1)} %get-tuple-element.22), channel_id=1, source_target_pairs={{0,128},{64,192},{128,0},{192,64},{1,129},{65,193},{129,1},{193,65... | collective-permute-start | bytes 417800 | tf_op jit(solution)/shard_map/ppermute | solution.py:25
  5.9 16.1 %collective-permute-start.1 = (f32[136,256]{1,0:T(8,128)S(1)}, f32[136,256]{1,0:T(8,128)S(1)}, u32[]{:S(2)}, u32[]{:S(2)}) collective-permute-start(f32[136,256]{1,0:T(8,128)S(1)} %get-tuple-element.22), channel_id=1, source_target_pairs={{0,192},{64,0},{128,64},{192,128},{1,193},{65,1},{129,65},{193,129... | collective-permute-start | bytes 417800 | tf_op jit(solution)/shard_map/ppermute | solution.py:25
  6.8 15.2 %collective-permute-start = (f32[136,256]{1,0:T(8,128)S(1)}, f32[136,256]{1,0:T(8,128)S(1)}, u32[]{:S(2)}, u32[]{:S(2)}) collective-permute-start(f32[136,256]{1,0:T(8,128)S(1)} %get-tuple-element.22), channel_id=1, source_target_pairs={{0,64},{64,128},{128,192},{192,0},{1,65},{65,129},{129,193},{193,1... | collective-permute-start | bytes 417800 | tf_op jit(solution)/shard_map/ppermute | solution.py:25
  22.0 5.8 %collective-permute-start.3 = (f32[4,136,256]{2,1,0:T(8,128)S(1)}, f32[4,136,256]{2,1,0:T(8,128)S(1)}, u32[]{:S(2)}, u32[]{:S(2)}) collective-permute-start(f32[4,136,256]{2,1,0:T(8,128)S(1)} %pad_maximum_fusion.refs_0_), channel_id=1, source_target_pairs={{0,16},{16,0},{1,17},{17,1},{2,18},{18,2},{3,19},{19,3},{4,20},{20... | collective-permute-start | bytes 1671176 | tf_op jit(solution)/shard_map/ppermute | solution.py:25
  25.1 14.7 %collective-permute-start.5 = (f32[4,136,256]{2,1,0:T(8,128)S(1)}, f32[4,136,256]{2,1,0:T(8,128)S(1)}, u32[]{:S(2)}, u32[]{:S(2)}) collective-permute-start(f32[4,136,256]{2,1,0:T(8,128)S(1)} %pad_maximum_fusion.refs_0_), channel_id=1, source_target_pairs={{0,12},{4,0},{8,4},{12,8},{1,13},{5,1},{9,5},{13,9},{2,14},{6,2},{... | collective-permute-start | bytes 1671176 | tf_op jit(solution)/shard_map/ppermute | solution.py:25
  27.8 15.1 %collective-permute-start.4 = (f32[4,136,256]{2,1,0:T(8,128)S(1)}, f32[4,136,256]{2,1,0:T(8,128)S(1)}, u32[]{:S(2)}, u32[]{:S(2)}) collective-permute-start(f32[4,136,256]{2,1,0:T(8,128)S(1)} %pad_maximum_fusion.refs_0_), channel_id=1, source_target_pairs={{0,4},{4,8},{8,12},{12,0},{1,5},{5,9},{9,13},{13,1},{2,6},{6,10},{... | collective-permute-start | bytes 1671176 | tf_op jit(solution)/shard_map/ppermute | solution.py:25
  42.9 13.9 %collective-permute-start.6 = (f32[4,136,256]{2,1,0:T(8,128)S(1)}, f32[4,136,256]{2,1,0:T(8,128)S(1)}, u32[]{:S(2)}, u32[]{:S(2)}) collective-permute-start(f32[4,136,256]{2,1,0:T(8,128)S(1)} %collective-permute-done.4.refs_0_), channel_id=1, source_target_pairs={{0,16},{16,0},{1,17},{17,1},{2,18},{18,2},{3,19},{19,3},{4,20},{20... | collective-permute-start | bytes 1671176 | tf_op jit(solution)/shard_map/ppermute | solution.py:25
  44.2 12.6 %collective-permute-start.7 = (f32[4,136,256]{2,1,0:T(8,128)S(1)}, f32[4,136,256]{2,1,0:T(8,128)S(1)}, u32[]{:S(2)}, u32[]{:S(2)}) collective-permute-start(f32[4,136,256]{2,1,0:T(8,128)S(1)} %collective-permute-done.5.refs_1_), channel_id=1, source_target_pairs={{0,16},{16,0},{1,17},{17,1},{2,18},{18,2},{3,19},{19,3},{4,20},{20... | collective-permute-start | bytes 1671176 | tf_op jit(solution)/shard_map/ppermute | solution.py:25
  44.3 11.1 %collective-permute-start.9 = (f32[2,136,256]{2,1,0:T(8,128)S(1)}, f32[2,136,256]{2,1,0:T(8,128)S(1)}, u32[]{:S(2)}, u32[]{:S(2)}) collective-permute-start(f32[2,136,256]{2,1,0:T(8,128)S(1)} %slice.7), channel_id=1, source_target_pairs={{0,12},{4,0},{8,4},{12,8},{1,13},{5,1},{9,5},{13,9},{2,14},{6,2},{... | collective-permute-start | bytes 835592 | tf_op jit(solution)/shard_map/ppermute | solution.py:25
  44.4 11.1 %collective-permute-start.8 = (f32[2,136,256]{2,1,0:T(8,128)S(1)}, f32[2,136,256]{2,1,0:T(8,128)S(1)}, u32[]{:S(2)}, u32[]{:S(2)}) collective-permute-start(f32[2,136,256]{2,1,0:T(8,128)S(1)} %slice.6), channel_id=1, source_target_pairs={{0,4},{4,8},{8,12},{12,0},{1,5},{5,9},{9,13},{13,1},{2,6},{6,10},{... | collective-permute-start | bytes 835592 | tf_op jit(solution)/shard_map/ppermute | solution.py:25
  55.4 2.3 %collective-permute-start.10 = (f32[2,136,256]{2,1,0:T(8,128)S(1)}, f32[2,136,256]{2,1,0:T(8,128)S(1)}, u32[]{:S(2)}, u32[]{:S(2)}) collective-permute-start(f32[2,136,256]{2,1,0:T(8,128)S(1)} %collective-permute-done.8.refs_2_), channel_id=1, source_target_pairs={{0,16},{16,0},{1,17},{17,1},{2,18},{18,2},{3,19},{19,3},{4,20},{20... | collective-permute-start | bytes 835592 | tf_op jit(solution)/shard_map/ppermute | solution.py:25
  56.5 1.6 %collective-permute-start.11 = (f32[2,136,256]{2,1,0:T(8,128)S(1)}, f32[2,136,256]{2,1,0:T(8,128)S(1)}, u32[]{:S(2)}, u32[]{:S(2)}) collective-permute-start(f32[2,136,256]{2,1,0:T(8,128)S(1)} %collective-permute-done.9.refs_3_), channel_id=1, source_target_pairs={{0,16},{16,0},{1,17},{17,1},{2,18},{18,2},{3,19},{19,3},{4,20},{20... | collective-permute-start | bytes 835592 | tf_op jit(solution)/shard_map/ppermute | solution.py:25
  61.4 6.0 %collective-permute-start.12 = (f32[256,128]{1,0:T(8,128)S(1)}, f32[256,128]{1,0:T(8,128)S(1)}, u32[]{:S(2)}, u32[]{:S(2)}) collective-permute-start(f32[256,128]{1,0:T(8,128)S(1)} %get-tuple-element.38), channel_id=1, source_target_pairs={{0,32},{32,1},{1,33},{33,2},{2,34},{34,3},{3,35},{35,0},{4,36},{36... | collective-permute-start | bytes 393224 | tf_op jit(solution)/shard_map/ppermute | solution.py:34
  65.4 5.1 %collective-permute-start.16 = (f32[256,128]{1,0:T(8,128)S(1)}, f32[256,128]{1,0:T(8,128)S(1)}, u32[]{:S(2)}, u32[]{:S(2)}) collective-permute-start(f32[256,128]{1,0:T(8,128)S(1)} %ring_step.13), channel_id=1, source_target_pairs={{0,35},{32,0},{1,32},{33,1},{2,33},{34,2},{3,34},{35,3},{4,39},{36... | collective-permute-start | bytes 393224 | tf_op jit(solution)/shard_map/ppermute | solution.py:34
  70.4 5.8 %collective-permute-start.13 = (f32[256,128]{1,0:T(8,128)S(1)}, f32[256,128]{1,0:T(8,128)S(1)}, u32[]{:S(2)}, u32[]{:S(2)}) collective-permute-start(f32[256,128]{1,0:T(8,128)S(1)} %ring_step.10), channel_id=1, source_target_pairs={{0,32},{32,1},{1,33},{33,2},{2,34},{34,3},{3,35},{35,0},{4,36},{36... | collective-permute-start | bytes 393224 | tf_op jit(solution)/shard_map/ppermute | solution.py:34
  73.5 5.8 %collective-permute-start.17 = (f32[256,128]{1,0:T(8,128)S(1)}, f32[256,128]{1,0:T(8,128)S(1)}, u32[]{:S(2)}, u32[]{:S(2)}) collective-permute-start(f32[256,128]{1,0:T(8,128)S(1)} %ring_step.14), channel_id=1, source_target_pairs={{0,35},{32,0},{1,32},{33,1},{2,33},{34,2},{3,34},{35,3},{4,39},{36... | collective-permute-start | bytes 393224 | tf_op jit(solution)/shard_map/ppermute | solution.py:34
  79.3 5.8 %collective-permute-start.14 = (f32[256,128]{1,0:T(8,128)S(1)}, f32[256,128]{1,0:T(8,128)S(1)}, u32[]{:S(2)}, u32[]{:S(2)}) collective-permute-start(f32[256,128]{1,0:T(8,128)S(1)} %ring_step.11), channel_id=1, source_target_pairs={{0,32},{32,1},{1,33},{33,2},{2,34},{34,3},{3,35},{35,0},{4,36},{36... | collective-permute-start | bytes 393224 | tf_op jit(solution)/shard_map/ppermute | solution.py:34
  82.3 10.8 %collective-permute-start.18 = (f32[256,128]{1,0:T(8,128)S(1)}, f32[256,128]{1,0:T(8,128)S(1)}, u32[]{:S(2)}, u32[]{:S(2)}) collective-permute-start(f32[256,128]{1,0:T(8,128)S(1)} %ring_step.15), channel_id=1, source_target_pairs={{0,35},{32,0},{1,32},{33,1},{2,33},{34,2},{3,34},{35,3},{4,39},{36... | collective-permute-start | bytes 393224 | tf_op jit(solution)/shard_map/ppermute | solution.py:34
  88.1 5.3 %collective-permute-start.15 = (f32[256,128]{1,0:T(8,128)S(1)}, f32[256,128]{1,0:T(8,128)S(1)}, u32[]{:S(2)}, u32[]{:S(2)}) collective-permute-start(f32[256,128]{1,0:T(8,128)S(1)} %ring_step.12), channel_id=1, source_target_pairs={{0,32},{32,1},{1,33},{33,2},{2,34},{34,3},{3,35},{35,0},{4,36},{36... | collective-permute-start | bytes 393224 | tf_op jit(solution)/shard_map/ppermute | solution.py:34
  88.4 5.0 %copy-start.1 = (f32[128,256]{1,0:T(8,128)S(1)}, f32[128,256]{1,0:T(8,128)}, u32[]{:S(2)}) copy-start(f32[128,256]{1,0:T(8,128)} %direction_ref.3) | copy-start | bytes 393220
  88.4 5.0 %copy-start.2 = (f32[128,256]{1,0:T(8,128)S(1)}, f32[128,256]{1,0:T(8,128)}, u32[]{:S(2)}) copy-start(f32[128,256]{1,0:T(8,128)} %residual_ref.3) | copy-start | bytes 393220
  88.4 5.0 %copy-start.5 = (f32[256]{0:T(256)S(1)}, f32[256]{0:T(256)}, u32[]{:S(2)}) copy-start(f32[256]{0:T(256)} %param.6) | copy-start | bytes 3076
  88.4 29.8 %copy-start.3 = (f32[128,256]{1,0:T(8,128)S(1)}, f32[128,256]{1,0:T(8,128)}, u32[]{:S(2)}) copy-start(f32[128,256]{1,0:T(8,128)} %solution_ref.1) | copy-start | bytes 393220
  (1 other events, 0.7 us)

commit v8 on v7

--- a/solution.py
+++ b/solution.py
@@ -25,13 +25,11 @@
     return lax.ppermute(value, axes, [(i, (i + by) % size) for i in range(size)])
 
 
-def ring_index(z):
-    return (z % 2) * SIZES[4] + z // 2
-
-
 def ring_shift(value, by):
-    size = lax.axis_size(RING)
-    return lax.ppermute(value, RING, [(ring_index(z), ring_index((z + by) % size)) for z in range(size)])
+    chips, half = lax.axis_size(RING), SIZES[4]
+    place = lambda z, core: (z % 2) * 2 * half + core * half + z // 2
+    hops = [(place(z, c), place((z + (1 - 2 * c) * by) % chips, c)) for z in range(chips) for c in range(2)]
+    return lax.ppermute(value, ("zl", "c", "zh"), hops)
 
 
 def pack_kernel(points, direction, mine, coords):
@@ -134,7 +132,7 @@
         prepare(groups, *prepared)
     columns, tile_a, tile_b = refs
     chips, _, block = target.shape
-    which = shard_at(here[0], offset, chips)
+    which = shard_at(here[0], here[1] * offset + chips, chips)
     columns[...] = jnp.transpose(target[which])
     earlier = before[pl.ds(pl.multiple_of(which * block, block), block), :]
     out[...] = earlier + came[...] if arrived else earlier
@@ -195,7 +193,7 @@
         outs += prepared_shapes(systems, sources)
     operands = [*groups, *prepared, targets, before, *came]
     return pl.pallas_call(
-        functools.partial(step_kernel, smoothing, wide, offset % chips, len(groups), len(prepared) // 2, bool(came)),
+        functools.partial(step_kernel, smoothing, wide, offset, len(groups), len(prepared) // 2, bool(came)),
         out_shape=outs,
         in_specs=[SMEM] + [VMEM] * len(operands),
         out_specs=[VMEM] * len(outs),
@@ -262,7 +260,7 @@
     total = block * math.prod(SIZES)
     smoothing = 1.0 / math.sqrt(total)
     ring = lax.axis_size(RING)
-    here = jnp.reshape(lax.axis_index("zh") * 2 + lax.axis_index("zl"), (1,))
+    here = jnp.stack([lax.axis_index("zh") * 2 + lax.axis_index("zl"), 1 - 2 * lax.axis_index("c")])
     small = pltpu.CompilerParams(vmem_limit_bytes=16 * 2**20)
 
     mine, coords = pl.pallas_call(

time: 119 us -> 124 us (1.042)
  Pallas kernels: 47.2 us -> 52.7 us
    pallas_call x8, Pallas kernels: 26 us -> 30.4 us  [ring_step(): pl.pallas_call(functools.partial(step_kernel, smoothing, wide, offset, le...]
  transfers between devices with their start and end apart: 19 -> 19, of which waited for: 6 -> 4; matrix products, arithmetic and copies ran while one was open for 0% -> 0% of each run, Pallas kernels for 36% -> 39%
where the time goes in v8:
time: 124 us
  Pallas kernels  52.7 us (42%)
  blocking collectives  38.4 us (31%)
  starting transfers between devices  24.5 us (20%)
  waiting for transfers between devices  5.41 us (4%)
  local copies, waits for them, and re-layouts  1.64 us (1%)
    pallas_call x8, Pallas kernels, ring_step(): pl.pallas_call(functools.partial(step_kernel, smoothing, wide, offset, le...  30.4 us
    pallas_call x2, Pallas kernels, bulk(): pl.pallas_call(functools.partial(bulk_kernel, smoothing, wide, len(groups...  21.1 us
    ppermute x12, starting transfers between devices, shift(): lax.ppermute(value, axes, [(i, (i + by) % size) for i in range(size)])  15.1 us
    all_to_all x1, blocking collectives, on_device(): targets = lax.all_to_all(coords, RING, 0, 0)  14.6 us
    all_to_all x1, blocking collectives, on_device(): lax.all_to_all(shares, PLANE, 0, 0)  14.1 us
    all_to_all x1, blocking collectives, on_device(): lax.all_to_all(shares, RING, 0, 0)  9.75 us
    ppermute x7, starting transfers between devices, ring_shift(): return lax.ppermute(value, ('zl', 'c', 'zh'), hops)  9.37 us
    ppermute x12, waiting for transfers between devices, shift(): lax.ppermute(value, axes, [(i, (i + by) % size) for i in range(size)])  5.39 us
  transfers between devices with their start and end apart: 19, of which 4 were waited for; matrix products, arithmetic and copies ran while one was open for 0% of the time, Pallas kernels for 39%

profile of v8, /device:TPU:1, one launch (start us, length us, event | category | flops | bytes accessed | tf_op | source)
XLA Modules:
  0.0 123.6 jit_solution(14776767802888051931)
XLA Ops:
  2.2 3.7 %collective-permute-start.2 = (f32[136,256]{1,0:T(8,128)S(1)}, f32[136,256]{1,0:T(8,128)S(1)}, u32[]{:S(2)}, u32[]{:S(2)}) collective-permute-start(f32[136,256]{1,0:T(8,128)S(1)} %get-tuple-element.22), channel_id=1, source_target_pairs={{0,128},{64,192},{128,0},{192,64},{1,129},{65,193},{129,1},{193,65... | collective-permute-start | bytes 417800 | tf_op jit(solution)/shard_map/ppermute | solution.py:25
  7.4 14.6 %all_to_all.15.refs_2_.refs_6_.refs_4_ = f32[8,8,256]{2,1,0:T(8,128)S(1)} all-to-all(f32[8,8,256]{2,1,0:T(8,128)S(1)} %get-tuple-element.23), channel_id=1, replica_groups=mesh['x'=4,'zl'=2,'c'=2,'y'=4,'zh'=4] {'zl','zh'}, dimensions={0} | all-to-all | bytes 131072 | tf_op jit(solution)/shard_map/all_to_all | solution.py:277
  22.0 3.0 %collective-permute-start.3 = (f32[4,136,256]{2,1,0:T(8,128)S(1)}, f32[4,136,256]{2,1,0:T(8,128)S(1)}, u32[]{:S(2)}, u32[]{:S(2)}) collective-permute-start(f32[4,136,256]{2,1,0:T(8,128)S(1)} %pad_maximum_fusion.refs_0_), channel_id=1, source_target_pairs={{0,16},{16,0},{1,17},{17,1},{2,18},{18,2},{3,19},{19,3},{4,20},{20... | collective-permute-start | bytes 1671176 | tf_op jit(solution)/shard_map/ppermute | solution.py:25
  25.1 2.7 %collective-permute-start.5 = (f32[4,136,256]{2,1,0:T(8,128)S(1)}, f32[4,136,256]{2,1,0:T(8,128)S(1)}, u32[]{:S(2)}, u32[]{:S(2)}) collective-permute-start(f32[4,136,256]{2,1,0:T(8,128)S(1)} %pad_maximum_fusion.refs_0_), channel_id=1, source_target_pairs={{0,12},{4,0},{8,4},{12,8},{1,13},{5,1},{9,5},{13,9},{2,14},{6,2},{... | collective-permute-start | bytes 1671176 | tf_op jit(solution)/shard_map/ppermute | solution.py:25
  27.9 11.0 %bulk.2.refs_3_ = f32[2048,128]{1,0:T(8,128)S(1)} custom-call(s32[2]{0:T(128)S(1)} %pad_add_fusion.here, f32[4,136,256]{2,1,0:T(8,128)S(1)} %pad_maximum_fusion.refs_0_, f32[4,136,256]{2,1,0:T(8,128)S(1)} %collective-permute-done.3.refs_1_, f32[8,8,256]{2,1,0:T(8,128)S(1)} %all_to_all.15.refs_2_.refs_6_.refs_4_), custom_call_target="tpu_custom_call" | custom-call | flops 8589934592 | bytes 1048576 | tf_op jit(solution)/shard_map/bulk/pallas_call | solution.py:169
  38.9 1.0 collective-permute-done.5.refs_1_
  39.9 3.1 %collective-permute-done.4.refs_0_ = f32[4,136,256]{2,1,0:T(8,128)S(1)} collective-permute-done((f32[4,136,256]{2,1,0:T(8,128)S(1)}, f32[4,136,256]{2,1,0:T(8,128)S(1)}, u32[]{:S(2)}, u32[]{:S(2)}) %collective-permute-start.4) | collective-permute-done | bytes 557088 | tf_op jit(solution)/shard_map/ppermute | solution.py:25
  43.0 1.2 collective-permute-start.6
  44.5 1.5 %collective-permute-start.8 = (f32[2,136,256]{2,1,0:T(8,128)S(1)}, f32[2,136,256]{2,1,0:T(8,128)S(1)}, u32[]{:S(2)}, u32[]{:S(2)}) collective-permute-start(f32[2,136,256]{2,1,0:T(8,128)S(1)} %slice.6), channel_id=1, source_target_pairs={{0,4},{4,8},{8,12},{12,0},{1,5},{5,9},{9,13},{13,1},{2,6},{6,10},{... | collective-permute-start | bytes 835592 | tf_op jit(solution)/shard_map/ppermute | solution.py:25
  45.9 10.1 %bulk.3 = (f32[2048,128]{1,0:T(8,128)S(1)}, bf16[256,2048]{1,0:T(8,128)(2,1)S(1)}, f32[24,2048]{1,0:T(8,128)S(1)}) custom-call(s32[2]{0:T(128)S(1)} %pad_add_fusion.here, f32[4,136,256]{2,1,0:T(8,128)S(1)} %collective-permute-done.4.refs_0_, f32[4,136,256]{2,1,0:T(8,128)S(1)} %collective-permute-done.5.refs_1_, ...), custom_call_target="tpu_custom_call" | custom-call | flops 8589934592 | bytes 1048576 | tf_op jit(solution)/shard_map/bulk/pallas_call | solution.py:169
  56.1 1.1 collective-permute-start.10
  58.7 3.9 %ring_step.8 = (f32[256,128]{1,0:T(8,128)S(1)}, bf16[256,4096]{1,0:T(8,128)(2,1)S(1)}, f32[24,4096]{1,0:T(8,128)S(1)}) custom-call(s32[2]{0:T(128)S(1)} %pad_add_fusion.here, f32[4,136,256]{2,1,0:T(8,128)S(1)} %collective-permute-done.6.refs_0_, f32[4,136,256]{2,1,0:T(8,128)S(1)} %collective-permute-done.7.refs_1_, ...), custom_call_target="tpu_custom_call" | custom-call | flops 2147483648 | bytes 131072 | tf_op jit(solution)/shard_map/ring_step/pallas_call | solution.py:195
  63.3 3.5 %ring_step.13 = f32[256,128]{1,0:T(8,128)S(1)} custom-call(s32[2]{0:T(128)S(1)} %pad_add_fusion.here, bf16[256,4096]{1,0:T(8,128)(2,1)S(1)} %get-tuple-element.36.refs_2_.refs_0_, f32[24,4096]{1,0:T(8,128)S(1)} %get-tuple-element.37.refs_3_.refs_1_, f32[8,8,256]{2,1,0:T(8,128)S(1)} %all_to_all.15.refs_2_.refs_6_.refs_4_, ...), custom_call_target="tpu_custom_call" | custom-call | flops 2147483648 | bytes 131072 | tf_op jit(solution)/shard_map/ring_step/pallas_call | solution.py:195
  67.8 3.5 %ring_step.10 = f32[256,128]{1,0:T(8,128)S(1)} custom-call(s32[2]{0:T(128)S(1)} %pad_add_fusion.here, bf16[256,4096]{1,0:T(8,128)(2,1)S(1)} %get-tuple-element.36.refs_2_.refs_0_, f32[24,4096]{1,0:T(8,128)S(1)} %get-tuple-element.37.refs_3_.refs_1_, f32[8,8,256]{2,1,0:T(8,128)S(1)} %all_to_all.15.refs_2_.refs_6_.refs_4_, ...), custom_call_target="tpu_custom_call" | custom-call | flops 2147483648 | bytes 131072 | tf_op jit(solution)/shard_map/ring_step/pallas_call | solution.py:195
  71.3 1.9 %collective-permute-start.13 = (f32[256,128]{1,0:T(8,128)S(1)}, f32[256,128]{1,0:T(8,128)S(1)}, u32[]{:S(2)}, u32[]{:S(2)}) collective-permute-start(f32[256,128]{1,0:T(8,128)S(1)} %ring_step.10), channel_id=1, source_target_pairs={{0,32},{16,51},{32,1},{48,16},{1,33},{17,48},{33,2},{49,17},{2,34}... | collective-permute-start | bytes 393224 | tf_op jit(solution)/shard_map/ppermute | solution.py:32
  73.2 3.5 %ring_step.14 = f32[256,128]{1,0:T(8,128)S(1)} custom-call(s32[2]{0:T(128)S(1)} %pad_add_fusion.here, bf16[256,4096]{1,0:T(8,128)(2,1)S(1)} %get-tuple-element.36.refs_2_.refs_0_, f32[24,4096]{1,0:T(8,128)S(1)} %get-tuple-element.37.refs_3_.refs_1_, f32[8,8,256]{2,1,0:T(8,128)S(1)} %all_to_all.15.refs_2_.refs_6_.refs_4_, ...), custom_call_target="tpu_custom_call" | custom-call | flops 2147483648 | bytes 131072 | tf_op jit(solution)/shard_map/ring_step/pallas_call | solution.py:195
  76.9 3.5 %ring_step.11 = f32[256,128]{1,0:T(8,128)S(1)} custom-call(s32[2]{0:T(128)S(1)} %pad_add_fusion.here, bf16[256,4096]{1,0:T(8,128)(2,1)S(1)} %get-tuple-element.36.refs_2_.refs_0_, f32[24,4096]{1,0:T(8,128)S(1)} %get-tuple-element.37.refs_3_.refs_1_, f32[8,8,256]{2,1,0:T(8,128)S(1)} %all_to_all.15.refs_2_.refs_6_.refs_4_, ...), custom_call_target="tpu_custom_call" | custom-call | flops 2147483648 | bytes 131072 | tf_op jit(solution)/shard_map/ring_step/pallas_call | solution.py:195
  80.4 2.7 %collective-permute-start.14 = (f32[256,128]{1,0:T(8,128)S(1)}, f32[256,128]{1,0:T(8,128)S(1)}, u32[]{:S(2)}, u32[]{:S(2)}) collective-permute-start(f32[256,128]{1,0:T(8,128)S(1)} %ring_step.11), channel_id=1, source_target_pairs={{0,32},{16,51},{32,1},{48,16},{1,33},{17,48},{33,2},{49,17},{2,34}... | collective-permute-start | bytes 393224 | tf_op jit(solution)/shard_map/ppermute | solution.py:32
  83.1 3.5 %ring_step.15 = f32[256,128]{1,0:T(8,128)S(1)} custom-call(s32[2]{0:T(128)S(1)} %pad_add_fusion.here, bf16[256,4096]{1,0:T(8,128)(2,1)S(1)} %get-tuple-element.36.refs_2_.refs_0_, f32[24,4096]{1,0:T(8,128)S(1)} %get-tuple-element.37.refs_3_.refs_1_, f32[8,8,256]{2,1,0:T(8,128)S(1)} %all_to_all.15.refs_2_.refs_6_.refs_4_, ...), custom_call_target="tpu_custom_call" | custom-call | flops 2147483648 | bytes 131072 | tf_op jit(solution)/shard_map/ring_step/pallas_call | solution.py:195
  86.8 3.5 %ring_step.12 = f32[256,128]{1,0:T(8,128)S(1)} custom-call(s32[2]{0:T(128)S(1)} %pad_add_fusion.here, bf16[256,4096]{1,0:T(8,128)(2,1)S(1)} %get-tuple-element.36.refs_2_.refs_0_, f32[24,4096]{1,0:T(8,128)S(1)} %get-tuple-element.37.refs_3_.refs_1_, f32[8,8,256]{2,1,0:T(8,128)S(1)} %all_to_all.15.refs_2_.refs_6_.refs_4_, ...), custom_call_target="tpu_custom_call" | custom-call | flops 2147483648 | bytes 131072 | tf_op jit(solution)/shard_map/ring_step/pallas_call | solution.py:195
  90.3 2.9 %collective-permute-start.15 = (f32[256,128]{1,0:T(8,128)S(1)}, f32[256,128]{1,0:T(8,128)S(1)}, u32[]{:S(2)}, u32[]{:S(2)}) collective-permute-start(f32[256,128]{1,0:T(8,128)S(1)} %ring_step.12), channel_id=1, source_target_pairs={{0,32},{16,51},{32,1},{48,16},{1,33},{17,48},{33,2},{49,17},{2,34}... | collective-permute-start | bytes 393224 | tf_op jit(solution)/shard_map/ppermute | solution.py:32
  93.3 5.3 %ring_step.9.own = f32[256,128]{1,0:T(8,128)S(1)} custom-call(s32[2]{0:T(128)S(1)} %pad_add_fusion.here, bf16[256,2048]{1,0:T(8,128)(2,1)S(1)} %get-tuple-element.30.refs_0_, f32[24,2048]{1,0:T(8,128)S(1)} %get-tuple-element.31.refs_1_, bf16[256,4096]{1,0:T(8,128)(2,1)S(1)} %get-tuple-element.36.refs_2_.refs_0_, ...), custom_call_target="tpu_custom_call" | custom-call | flops 3221225472 | bytes 131072 | tf_op jit(solution)/shard_map/ring_step/pallas_call | solution.py:195
  98.8 14.1 %all_to_all.16.parts = f32[32,1,512]{2,1,0:T(1,128)S(1)} all-to-all(f32[32,1,512]{2,1,0:T(1,128)S(1)} %get-tuple-element.39), channel_id=1, replica_groups=mesh['x'=4,'zl'=2,'c'=2,'y'=4,'zh'=4] {'x','c','y'}, dimensions={0} | all-to-all | bytes 131072 | tf_op jit(solution)/shard_map/all_to_all | solution.py:320
  112.9 9.8 %all_to_all.17.sums_ref = f32[8,1,512]{2,1,0:T(1,128)S(1)} all-to-all(f32[8,1,512]{2,1,0:T(1,128)S(1)} %spread.1), channel_id=1, replica_groups=mesh['x'=4,'zl'=2,'c'=2,'y'=4,'zh'=4] {'zl','zh'}, dimensions={0} | all-to-all | bytes 32768 | tf_op jit(solution)/shard_map/all_to_all | solution.py:328
  (47 shorter events, 8.0 us)
Async XLA Ops:
  0.6 0.9 copy-start
  2.2 19.7 %collective-permute-start.2 = (f32[136,256]{1,0:T(8,128)S(1)}, f32[136,256]{1,0:T(8,128)S(1)}, u32[]{:S(2)}, u32[]{:S(2)}) collective-permute-start(f32[136,256]{1,0:T(8,128)S(1)} %get-tuple-element.22), channel_id=1, source_target_pairs={{0,128},{64,192},{128,0},{192,64},{1,129},{65,193},{129,1},{193,65... | collective-permute-start | bytes 417800 | tf_op jit(solution)/shard_map/ppermute | solution.py:25
  5.9 16.1 %collective-permute-start.1 = (f32[136,256]{1,0:T(8,128)S(1)}, f32[136,256]{1,0:T(8,128)S(1)}, u32[]{:S(2)}, u32[]{:S(2)}) collective-permute-start(f32[136,256]{1,0:T(8,128)S(1)} %get-tuple-element.22), channel_id=1, source_target_pairs={{0,192},{64,0},{128,64},{192,128},{1,193},{65,1},{129,65},{193,129... | collective-permute-start | bytes 417800 | tf_op jit(solution)/shard_map/ppermute | solution.py:25
  6.8 15.2 %collective-permute-start = (f32[136,256]{1,0:T(8,128)S(1)}, f32[136,256]{1,0:T(8,128)S(1)}, u32[]{:S(2)}, u32[]{:S(2)}) collective-permute-start(f32[136,256]{1,0:T(8,128)S(1)} %get-tuple-element.22), channel_id=1, source_target_pairs={{0,64},{64,128},{128,192},{192,0},{1,65},{65,129},{129,193},{193,1... | collective-permute-start | bytes 417800 | tf_op jit(solution)/shard_map/ppermute | solution.py:25
  22.0 5.9 %collective-permute-start.3 = (f32[4,136,256]{2,1,0:T(8,128)S(1)}, f32[4,136,256]{2,1,0:T(8,128)S(1)}, u32[]{:S(2)}, u32[]{:S(2)}) collective-permute-start(f32[4,136,256]{2,1,0:T(8,128)S(1)} %pad_maximum_fusion.refs_0_), channel_id=1, source_target_pairs={{0,16},{16,0},{1,17},{17,1},{2,18},{18,2},{3,19},{19,3},{4,20},{20... | collective-permute-start | bytes 1671176 | tf_op jit(solution)/shard_map/ppermute | solution.py:25
  25.1 14.8 %collective-permute-start.5 = (f32[4,136,256]{2,1,0:T(8,128)S(1)}, f32[4,136,256]{2,1,0:T(8,128)S(1)}, u32[]{:S(2)}, u32[]{:S(2)}) collective-permute-start(f32[4,136,256]{2,1,0:T(8,128)S(1)} %pad_maximum_fusion.refs_0_), channel_id=1, source_target_pairs={{0,12},{4,0},{8,4},{12,8},{1,13},{5,1},{9,5},{13,9},{2,14},{6,2},{... | collective-permute-start | bytes 1671176 | tf_op jit(solution)/shard_map/ppermute | solution.py:25
  27.9 15.1 %collective-permute-start.4 = (f32[4,136,256]{2,1,0:T(8,128)S(1)}, f32[4,136,256]{2,1,0:T(8,128)S(1)}, u32[]{:S(2)}, u32[]{:S(2)}) collective-permute-start(f32[4,136,256]{2,1,0:T(8,128)S(1)} %pad_maximum_fusion.refs_0_), channel_id=1, source_target_pairs={{0,4},{4,8},{8,12},{12,0},{1,5},{5,9},{9,13},{13,1},{2,6},{6,10},{... | collective-permute-start | bytes 1671176 | tf_op jit(solution)/shard_map/ppermute | solution.py:25
  43.0 14.4 %collective-permute-start.6 = (f32[4,136,256]{2,1,0:T(8,128)S(1)}, f32[4,136,256]{2,1,0:T(8,128)S(1)}, u32[]{:S(2)}, u32[]{:S(2)}) collective-permute-start(f32[4,136,256]{2,1,0:T(8,128)S(1)} %collective-permute-done.4.refs_0_), channel_id=1, source_target_pairs={{0,16},{16,0},{1,17},{17,1},{2,18},{18,2},{3,19},{19,3},{4,20},{20... | collective-permute-start | bytes 1671176 | tf_op jit(solution)/shard_map/ppermute | solution.py:25
  44.3 13.1 %collective-permute-start.7 = (f32[4,136,256]{2,1,0:T(8,128)S(1)}, f32[4,136,256]{2,1,0:T(8,128)S(1)}, u32[]{:S(2)}, u32[]{:S(2)}) collective-permute-start(f32[4,136,256]{2,1,0:T(8,128)S(1)} %collective-permute-done.5.refs_1_), channel_id=1, source_target_pairs={{0,16},{16,0},{1,17},{17,1},{2,18},{18,2},{3,19},{19,3},{4,20},{20... | collective-permute-start | bytes 1671176 | tf_op jit(solution)/shard_map/ppermute | solution.py:25
  44.4 11.7 %collective-permute-start.9 = (f32[2,136,256]{2,1,0:T(8,128)S(1)}, f32[2,136,256]{2,1,0:T(8,128)S(1)}, u32[]{:S(2)}, u32[]{:S(2)}) collective-permute-start(f32[2,136,256]{2,1,0:T(8,128)S(1)} %slice.7), channel_id=1, source_target_pairs={{0,12},{4,0},{8,4},{12,8},{1,13},{5,1},{9,5},{13,9},{2,14},{6,2},{... | collective-permute-start | bytes 835592 | tf_op jit(solution)/shard_map/ppermute | solution.py:25
  44.5 11.6 %collective-permute-start.8 = (f32[2,136,256]{2,1,0:T(8,128)S(1)}, f32[2,136,256]{2,1,0:T(8,128)S(1)}, u32[]{:S(2)}, u32[]{:S(2)}) collective-permute-start(f32[2,136,256]{2,1,0:T(8,128)S(1)} %slice.6), channel_id=1, source_target_pairs={{0,4},{4,8},{8,12},{12,0},{1,5},{5,9},{9,13},{13,1},{2,6},{6,10},{... | collective-permute-start | bytes 835592 | tf_op jit(solution)/shard_map/ppermute | solution.py:25
  56.1 2.3 %collective-permute-start.10 = (f32[2,136,256]{2,1,0:T(8,128)S(1)}, f32[2,136,256]{2,1,0:T(8,128)S(1)}, u32[]{:S(2)}, u32[]{:S(2)}) collective-permute-start(f32[2,136,256]{2,1,0:T(8,128)S(1)} %collective-permute-done.8.refs_2_), channel_id=1, source_target_pairs={{0,16},{16,0},{1,17},{17,1},{2,18},{18,2},{3,19},{19,3},{4,20},{20... | collective-permute-start | bytes 835592 | tf_op jit(solution)/shard_map/ppermute | solution.py:25
  57.1 1.6 %collective-permute-start.11 = (f32[2,136,256]{2,1,0:T(8,128)S(1)}, f32[2,136,256]{2,1,0:T(8,128)S(1)}, u32[]{:S(2)}, u32[]{:S(2)}) collective-permute-start(f32[2,136,256]{2,1,0:T(8,128)S(1)} %collective-permute-done.9.refs_3_), channel_id=1, source_target_pairs={{0,16},{16,0},{1,17},{17,1},{2,18},{18,2},{3,19},{19,3},{4,20},{20... | collective-permute-start | bytes 835592 | tf_op jit(solution)/shard_map/ppermute | solution.py:25
  62.6 5.2 %collective-permute-start.12 = (f32[256,128]{1,0:T(8,128)S(1)}, f32[256,128]{1,0:T(8,128)S(1)}, u32[]{:S(2)}, u32[]{:S(2)}) collective-permute-start(f32[256,128]{1,0:T(8,128)S(1)} %get-tuple-element.38), channel_id=1, source_target_pairs={{0,32},{16,51},{32,1},{48,16},{1,33},{17,48},{33,2},{49,17},{2,34}... | collective-permute-start | bytes 393224 | tf_op jit(solution)/shard_map/ppermute | solution.py:32
  66.8 6.4 %collective-permute-start.16 = (f32[256,128]{1,0:T(8,128)S(1)}, f32[256,128]{1,0:T(8,128)S(1)}, u32[]{:S(2)}, u32[]{:S(2)}) collective-permute-start(f32[256,128]{1,0:T(8,128)S(1)} %ring_step.13), channel_id=1, source_target_pairs={{0,35},{16,48},{32,0},{48,17},{1,32},{17,49},{33,1},{49,18},{2,33}... | collective-permute-start | bytes 393224 | tf_op jit(solution)/shard_map/ppermute | solution.py:32
  71.3 5.5 %collective-permute-start.13 = (f32[256,128]{1,0:T(8,128)S(1)}, f32[256,128]{1,0:T(8,128)S(1)}, u32[]{:S(2)}, u32[]{:S(2)}) collective-permute-start(f32[256,128]{1,0:T(8,128)S(1)} %ring_step.10), channel_id=1, source_target_pairs={{0,32},{16,51},{32,1},{48,16},{1,33},{17,48},{33,2},{49,17},{2,34}... | collective-permute-start | bytes 393224 | tf_op jit(solution)/shard_map/ppermute | solution.py:32
  76.8 6.4 %collective-permute-start.17 = (f32[256,128]{1,0:T(8,128)S(1)}, f32[256,128]{1,0:T(8,128)S(1)}, u32[]{:S(2)}, u32[]{:S(2)}) collective-permute-start(f32[256,128]{1,0:T(8,128)S(1)} %ring_step.14), channel_id=1, source_target_pairs={{0,35},{16,48},{32,0},{48,17},{1,32},{17,49},{33,1},{49,18},{2,33}... | collective-permute-start | bytes 393224 | tf_op jit(solution)/shard_map/ppermute | solution.py:32
  80.4 6.3 %collective-permute-start.14 = (f32[256,128]{1,0:T(8,128)S(1)}, f32[256,128]{1,0:T(8,128)S(1)}, u32[]{:S(2)}, u32[]{:S(2)}) collective-permute-start(f32[256,128]{1,0:T(8,128)S(1)} %ring_step.11), channel_id=1, source_target_pairs={{0,32},{16,51},{32,1},{48,16},{1,33},{17,48},{33,2},{49,17},{2,34}... | collective-permute-start | bytes 393224 | tf_op jit(solution)/shard_map/ppermute | solution.py:32
  86.6 11.9 %collective-permute-start.18 = (f32[256,128]{1,0:T(8,128)S(1)}, f32[256,128]{1,0:T(8,128)S(1)}, u32[]{:S(2)}, u32[]{:S(2)}) collective-permute-start(f32[256,128]{1,0:T(8,128)S(1)} %ring_step.15), channel_id=1, source_target_pairs={{0,35},{16,48},{32,0},{48,17},{1,32},{17,49},{33,1},{49,18},{2,33}... | collective-permute-start | bytes 393224 | tf_op jit(solution)/shard_map/ppermute | solution.py:32
  90.3 8.3 %collective-permute-start.15 = (f32[256,128]{1,0:T(8,128)S(1)}, f32[256,128]{1,0:T(8,128)S(1)}, u32[]{:S(2)}, u32[]{:S(2)}) collective-permute-start(f32[256,128]{1,0:T(8,128)S(1)} %ring_step.12), channel_id=1, source_target_pairs={{0,32},{16,51},{32,1},{48,16},{1,33},{17,48},{33,2},{49,17},{2,34}... | collective-permute-start | bytes 393224 | tf_op jit(solution)/shard_map/ppermute | solution.py:32
  93.2 5.3 %copy-start.1 = (f32[128,256]{1,0:T(8,128)S(1)}, f32[128,256]{1,0:T(8,128)}, u32[]{:S(2)}) copy-start(f32[128,256]{1,0:T(8,128)} %direction_ref.3) | copy-start | bytes 393220
  93.2 5.3 %copy-start.2 = (f32[128,256]{1,0:T(8,128)S(1)}, f32[128,256]{1,0:T(8,128)}, u32[]{:S(2)}) copy-start(f32[128,256]{1,0:T(8,128)} %residual_ref.3) | copy-start | bytes 393220
  93.2 5.3 %copy-start.5 = (f32[256]{0:T(256)S(1)}, f32[256]{0:T(256)}, u32[]{:S(2)}) copy-start(f32[256]{0:T(256)} %param.6) | copy-start | bytes 3076
  93.3 29.4 %copy-start.3 = (f32[128,256]{1,0:T(8,128)S(1)}, f32[128,256]{1,0:T(8,128)}, u32[]{:S(2)}) copy-start(f32[128,256]{1,0:T(8,128)} %solution_ref.1) | copy-start | bytes 393220
  (1 other events, 0.7 us)

commit v9 on v7

--- a/solution.py
+++ b/solution.py
@@ -117,10 +117,11 @@
     out[...] = before[...] if started else jnp.zeros_like(out)
 
     def at(pair, half):
-        shard = shard_at(here[0], pair + 1, chips) if started else pair
-        return pl.multiple_of(shard * block, block), half * wide
-
-    accumulate(smoothing, wide, chips - started, at, weights, rows, columns, out, tile_a, tile_b)
+        if not started:
+            return pl.multiple_of((2 * pair + half) * block, block), 0
+        return pl.multiple_of(shard_at(here[0], pair + 1, chips) * block, block), half * wide
+
+    accumulate(smoothing, wide, chips - 1 if started else chips // 2, at, weights, rows, columns, out, tile_a, tile_b)
 
 
 def step_kernel(smoothing, wide, offset, count, sets, arrived, here, *refs):
@@ -165,8 +166,8 @@
     chips, coords, block = targets.shape
     systems = groups[0].shape[1] - coords
     sources = sum(g.shape[0] for g in groups) * block
-    wide = sources // 2
     started = before is not None
+    wide = sources // 2 if started else sources
     held = prepared_shapes(systems, sources)
     return pl.pallas_call(
         functools.partial(bulk_kernel, smoothing, wide, len(groups), started),

time: 119 us -> 119 us (level)
  no operation moved by 1% of the time
where the time goes in v9:
time: 119 us
  Pallas kernels  47.3 us (40%)
  blocking collectives  39.1 us (33%)
  starting transfers between devices  23.7 us (20%)
  waiting for transfers between devices  6.42 us (5%)
  local copies, waits for them, and re-layouts  1.65 us (1%)
    pallas_call x8, Pallas kernels, ring_step(): pl.pallas_call(functools.partial(step_kernel, smoothing, wide, offset % c...  26 us
    pallas_call x2, Pallas kernels, bulk(): pl.pallas_call(functools.partial(bulk_kernel, smoothing, wide, len(groups...  20.1 us
    all_to_all x1, blocking collectives, on_device(): lax.all_to_all(shares, PLANE, 0, 0)  15.3 us
    ppermute x12, starting transfers between devices, shift(): lax.ppermute(value, axes, [(i, (i + by) % size) for i in range(size)])  15 us
    all_to_all x1, blocking collectives, on_device(): targets = lax.all_to_all(coords, RING, 0, 0)  14.6 us
    all_to_all x1, blocking collectives, on_device(): lax.all_to_all(shares, RING, 0, 0)  9.21 us
    ppermute x7, starting transfers between devices, ring_shift(): lax.ppermute(value, RING, [(ring_index(z), ring_index((z + by) % size)) f...  8.75 us
    ppermute x12, waiting for transfers between devices, shift(): lax.ppermute(value, axes, [(i, (i + by) % size) for i in range(size)])  6.02 us
  transfers between devices with their start and end apart: 19, of which 6 were waited for; matrix products, arithmetic and copies ran while one was open for 0% of the time, Pallas kernels for 36%

profile of v9, /device:TPU:1, one launch (start us, length us, event | category | flops | bytes accessed | tf_op | source)
XLA Modules:
  0.0 119.0 jit_solution(8341480107417841728)
XLA Ops:
  2.2 3.7 %collective-permute-start.2 = (f32[136,256]{1,0:T(8,128)S(1)}, f32[136,256]{1,0:T(8,128)S(1)}, u32[]{:S(2)}, u32[]{:S(2)}) collective-permute-start(f32[136,256]{1,0:T(8,128)S(1)} %get-tuple-element.22), channel_id=1, source_target_pairs={{0,128},{64,192},{128,0},{192,64},{1,129},{65,193},{129,1},{193,65... | collective-permute-start | bytes 417800 | tf_op jit(solution)/shard_map/ppermute | solution.py:25
  7.4 14.6 %all_to_all.15.refs_2_.refs_6_.refs_4_ = f32[8,8,256]{2,1,0:T(8,128)S(1)} all-to-all(f32[8,8,256]{2,1,0:T(8,128)S(1)} %get-tuple-element.23), channel_id=1, replica_groups=mesh['x'=4,'zl'=2,'c'=2,'y'=4,'zh'=4] {'zl','zh'}, dimensions={0} | all-to-all | bytes 131072 | tf_op jit(solution)/shard_map/all_to_all | solution.py:280
  22.0 3.0 %collective-permute-start.3 = (f32[4,136,256]{2,1,0:T(8,128)S(1)}, f32[4,136,256]{2,1,0:T(8,128)S(1)}, u32[]{:S(2)}, u32[]{:S(2)}) collective-permute-start(f32[4,136,256]{2,1,0:T(8,128)S(1)} %pad_maximum_fusion.refs_0_), channel_id=1, source_target_pairs={{0,16},{16,0},{1,17},{17,1},{2,18},{18,2},{3,19},{19,3},{4,20},{20... | collective-permute-start | bytes 1671176 | tf_op jit(solution)/shard_map/ppermute | solution.py:25
  25.1 2.8 %collective-permute-start.5 = (f32[4,136,256]{2,1,0:T(8,128)S(1)}, f32[4,136,256]{2,1,0:T(8,128)S(1)}, u32[]{:S(2)}, u32[]{:S(2)}) collective-permute-start(f32[4,136,256]{2,1,0:T(8,128)S(1)} %pad_maximum_fusion.refs_0_), channel_id=1, source_target_pairs={{0,12},{4,0},{8,4},{12,8},{1,13},{5,1},{9,5},{13,9},{2,14},{6,2},{... | collective-permute-start | bytes 1671176 | tf_op jit(solution)/shard_map/ppermute | solution.py:25
  27.8 10.5 %bulk.2.refs_3_ = f32[2048,128]{1,0:T(8,128)S(1)} custom-call(s32[1]{0:T(128)} %bitcast.here, f32[4,136,256]{2,1,0:T(8,128)S(1)} %pad_maximum_fusion.refs_0_, f32[4,136,256]{2,1,0:T(8,128)S(1)} %collective-permute-done.3.refs_1_, f32[8,8,256]{2,1,0:T(8,128)S(1)} %all_to_all.15.refs_2_.refs_6_.refs_4_), custom_call_target="tpu_custom_call" | custom-call | flops 8589934592 | bytes 1048576 | tf_op jit(solution)/shard_map/bulk/pallas_call | solution.py:172
  38.3 1.4 %collective-permute-done.5.refs_1_ = f32[4,136,256]{2,1,0:T(8,128)S(1)} collective-permute-done((f32[4,136,256]{2,1,0:T(8,128)S(1)}, f32[4,136,256]{2,1,0:T(8,128)S(1)}, u32[]{:S(2)}, u32[]{:S(2)}) %collective-permute-start.5) | collective-permute-done | bytes 557088 | tf_op jit(solution)/shard_map/ppermute | solution.py:25
  39.8 3.1 %collective-permute-done.4.refs_0_ = f32[4,136,256]{2,1,0:T(8,128)S(1)} collective-permute-done((f32[4,136,256]{2,1,0:T(8,128)S(1)}, f32[4,136,256]{2,1,0:T(8,128)S(1)}, u32[]{:S(2)}, u32[]{:S(2)}) %collective-permute-start.4) | collective-permute-done | bytes 557088 | tf_op jit(solution)/shard_map/ppermute | solution.py:25
  42.9 1.3 %collective-permute-start.6 = (f32[4,136,256]{2,1,0:T(8,128)S(1)}, f32[4,136,256]{2,1,0:T(8,128)S(1)}, u32[]{:S(2)}, u32[]{:S(2)}) collective-permute-start(f32[4,136,256]{2,1,0:T(8,128)S(1)} %collective-permute-done.4.refs_0_), channel_id=1, source_target_pairs={{0,16},{16,0},{1,17},{17,1},{2,18},{18,2},{3,19},{19,3},{4,20},{20... | collective-permute-start | bytes 1671176 | tf_op jit(solution)/shard_map/ppermute | solution.py:25
  44.4 1.5 %collective-permute-start.8 = (f32[2,136,256]{2,1,0:T(8,128)S(1)}, f32[2,136,256]{2,1,0:T(8,128)S(1)}, u32[]{:S(2)}, u32[]{:S(2)}) collective-permute-start(f32[2,136,256]{2,1,0:T(8,128)S(1)} %slice.6), channel_id=1, source_target_pairs={{0,4},{4,8},{8,12},{12,0},{1,5},{5,9},{9,13},{13,1},{2,6},{6,10},{... | collective-permute-start | bytes 835592 | tf_op jit(solution)/shard_map/ppermute | solution.py:25
  45.8 9.6 %bulk.3 = (f32[2048,128]{1,0:T(8,128)S(1)}, bf16[256,2048]{1,0:T(8,128)(2,1)S(1)}, f32[24,2048]{1,0:T(8,128)S(1)}) custom-call(s32[1]{0:T(128)} %bitcast.here, f32[4,136,256]{2,1,0:T(8,128)S(1)} %collective-permute-done.4.refs_0_, f32[4,136,256]{2,1,0:T(8,128)S(1)} %collective-permute-done.5.refs_1_, f32[8,8,256]{2,1,0:T(8,128)S(1)} %all_to_all.15.refs_2_.refs_6_.refs_4_, ...), custom_call_target="tpu_custom_call" | custom-call | flops 8589934592 | bytes 1048576 | tf_op jit(solution)/shard_map/bulk/pallas_call | solution.py:172
  56.6 1.1 collective-permute-done.10.refs_4_
  58.1 3.3 %ring_step.8 = (f32[256,128]{1,0:T(8,128)S(1)}, bf16[256,4096]{1,0:T(8,128)(2,1)S(1)}, f32[24,4096]{1,0:T(8,128)S(1)}) custom-call(s32[1]{0:T(128)} %bitcast.here, f32[4,136,256]{2,1,0:T(8,128)S(1)} %collective-permute-done.6.refs_0_, f32[4,136,256]{2,1,0:T(8,128)S(1)} %collective-permute-done.7.refs_1_, f32[2,136,256]{2,1,0:T(8,128)S(1)} %collective-permute-done.8.refs_2_, ...), custom_call_target="tpu_custom_call" | custom-call | flops 2147483648 | bytes 131072 | tf_op jit(solution)/shard_map/ring_step/pallas_call | solution.py:198
  62.4 3.0 %ring_step.13 = f32[256,128]{1,0:T(8,128)S(1)} custom-call(s32[1]{0:T(128)} %bitcast.here, bf16[256,4096]{1,0:T(8,128)(2,1)S(1)} %get-tuple-element.36.refs_2_.refs_0_, f32[24,4096]{1,0:T(8,128)S(1)} %get-tuple-element.37.refs_3_.refs_1_, f32[8,8,256]{2,1,0:T(8,128)S(1)} %all_to_all.15.refs_2_.refs_6_.refs_4_, ...), custom_call_target="tpu_custom_call" | custom-call | flops 2147483648 | bytes 131072 | tf_op jit(solution)/shard_map/ring_step/pallas_call | solution.py:198
  65.4 1.9 %collective-permute-start.16 = (f32[256,128]{1,0:T(8,128)S(1)}, f32[256,128]{1,0:T(8,128)S(1)}, u32[]{:S(2)}, u32[]{:S(2)}) collective-permute-start(f32[256,128]{1,0:T(8,128)S(1)} %ring_step.13), channel_id=1, source_target_pairs={{0,35},{32,0},{1,32},{33,1},{2,33},{34,2},{3,34},{35,3},{4,39},{36... | collective-permute-start | bytes 393224 | tf_op jit(solution)/shard_map/ppermute | solution.py:34
  67.4 3.0 %ring_step.10 = f32[256,128]{1,0:T(8,128)S(1)} custom-call(s32[1]{0:T(128)} %bitcast.here, bf16[256,4096]{1,0:T(8,128)(2,1)S(1)} %get-tuple-element.36.refs_2_.refs_0_, f32[24,4096]{1,0:T(8,128)S(1)} %get-tuple-element.37.refs_3_.refs_1_, f32[8,8,256]{2,1,0:T(8,128)S(1)} %all_to_all.15.refs_2_.refs_6_.refs_4_, ...), custom_call_target="tpu_custom_call" | custom-call | flops 2147483648 | bytes 131072 | tf_op jit(solution)/shard_map/ring_step/pallas_call | solution.py:198
  70.5 3.0 %ring_step.14 = f32[256,128]{1,0:T(8,128)S(1)} custom-call(s32[1]{0:T(128)} %bitcast.here, bf16[256,4096]{1,0:T(8,128)(2,1)S(1)} %get-tuple-element.36.refs_2_.refs_0_, f32[24,4096]{1,0:T(8,128)S(1)} %get-tuple-element.37.refs_3_.refs_1_, f32[8,8,256]{2,1,0:T(8,128)S(1)} %all_to_all.15.refs_2_.refs_6_.refs_4_, ...), custom_call_target="tpu_custom_call" | custom-call | flops 2147483648 | bytes 131072 | tf_op jit(solution)/shard_map/ring_step/pallas_call | solution.py:198
  73.5 2.7 %collective-permute-start.17 = (f32[256,128]{1,0:T(8,128)S(1)}, f32[256,128]{1,0:T(8,128)S(1)}, u32[]{:S(2)}, u32[]{:S(2)}) collective-permute-start(f32[256,128]{1,0:T(8,128)S(1)} %ring_step.14), channel_id=1, source_target_pairs={{0,35},{32,0},{1,32},{33,1},{2,33},{34,2},{3,34},{35,3},{4,39},{36... | collective-permute-start | bytes 393224 | tf_op jit(solution)/shard_map/ppermute | solution.py:34
  76.3 3.0 %ring_step.11 = f32[256,128]{1,0:T(8,128)S(1)} custom-call(s32[1]{0:T(128)} %bitcast.here, bf16[256,4096]{1,0:T(8,128)(2,1)S(1)} %get-tuple-element.36.refs_2_.refs_0_, f32[24,4096]{1,0:T(8,128)S(1)} %get-tuple-element.37.refs_3_.refs_1_, f32[8,8,256]{2,1,0:T(8,128)S(1)} %all_to_all.15.refs_2_.refs_6_.refs_4_, ...), custom_call_target="tpu_custom_call" | custom-call | flops 2147483648 | bytes 131072 | tf_op jit(solution)/shard_map/ring_step/pallas_call | solution.py:198
  79.6 3.0 %ring_step.15 = f32[256,128]{1,0:T(8,128)S(1)} custom-call(s32[1]{0:T(128)} %bitcast.here, bf16[256,4096]{1,0:T(8,128)(2,1)S(1)} %get-tuple-element.36.refs_2_.refs_0_, f32[24,4096]{1,0:T(8,128)S(1)} %get-tuple-element.37.refs_3_.refs_1_, f32[8,8,256]{2,1,0:T(8,128)S(1)} %all_to_all.15.refs_2_.refs_6_.refs_4_, ...), custom_call_target="tpu_custom_call" | custom-call | flops 2147483648 | bytes 131072 | tf_op jit(solution)/shard_map/ring_step/pallas_call | solution.py:198
  82.6 2.7 %collective-permute-start.18 = (f32[256,128]{1,0:T(8,128)S(1)}, f32[256,128]{1,0:T(8,128)S(1)}, u32[]{:S(2)}, u32[]{:S(2)}) collective-permute-start(f32[256,128]{1,0:T(8,128)S(1)} %ring_step.15), channel_id=1, source_target_pairs={{0,35},{32,0},{1,32},{33,1},{2,33},{34,2},{3,34},{35,3},{4,39},{36... | collective-permute-start | bytes 393224 | tf_op jit(solution)/shard_map/ppermute | solution.py:34
  85.3 3.0 %ring_step.12 = f32[256,128]{1,0:T(8,128)S(1)} custom-call(s32[1]{0:T(128)} %bitcast.here, bf16[256,4096]{1,0:T(8,128)(2,1)S(1)} %get-tuple-element.36.refs_2_.refs_0_, f32[24,4096]{1,0:T(8,128)S(1)} %get-tuple-element.37.refs_3_.refs_1_, f32[8,8,256]{2,1,0:T(8,128)S(1)} %all_to_all.15.refs_2_.refs_6_.refs_4_, ...), custom_call_target="tpu_custom_call" | custom-call | flops 2147483648 | bytes 131072 | tf_op jit(solution)/shard_map/ring_step/pallas_call | solution.py:198
  88.4 4.7 %ring_step.9.own = f32[256,128]{1,0:T(8,128)S(1)} custom-call(s32[1]{0:T(128)} %bitcast.here, bf16[256,2048]{1,0:T(8,128)(2,1)S(1)} %get-tuple-element.30.refs_0_, f32[24,2048]{1,0:T(8,128)S(1)} %get-tuple-element.31.refs_1_, bf16[256,4096]{1,0:T(8,128)(2,1)S(1)} %get-tuple-element.36.refs_2_.refs_0_, f32[24,4096]{1,0:T(8,128)S(1)} %get-tuple-element.37.refs_3_.refs_1_, ...), custom_call_target="tpu_custom_call" | custom-call | flops 3221225472 | bytes 131072 | tf_op jit(solution)/shard_map/ring_step/pallas_call | solution.py:198
  93.6 15.3 %all_to_all.16.parts = f32[32,1,512]{2,1,0:T(1,128)S(1)} all-to-all(f32[32,1,512]{2,1,0:T(1,128)S(1)} %get-tuple-element.39), channel_id=1, replica_groups=mesh['x'=4,'zl'=2,'c'=2,'y'=4,'zh'=4] {'x','c','y'}, dimensions={0} | all-to-all | bytes 131072 | tf_op jit(solution)/shard_map/all_to_all | solution.py:323
  109.0 9.2 %all_to_all.17.sums_ref = f32[8,1,512]{2,1,0:T(1,128)S(1)} all-to-all(f32[8,1,512]{2,1,0:T(1,128)S(1)} %spread.1), channel_id=1, replica_groups=mesh['x'=4,'zl'=2,'c'=2,'y'=4,'zh'=4] {'zl','zh'}, dimensions={0} | all-to-all | bytes 32768 | tf_op jit(solution)/shard_map/all_to_all | solution.py:331
  (46 shorter events, 7.9 us)
Async XLA Ops:
  0.6 0.9 copy-start
  2.2 19.7 %collective-permute-start.2 = (f32[136,256]{1,0:T(8,128)S(1)}, f32[136,256]{1,0:T(8,128)S(1)}, u32[]{:S(2)}, u32[]{:S(2)}) collective-permute-start(f32[136,256]{1,0:T(8,128)S(1)} %get-tuple-element.22), channel_id=1, source_target_pairs={{0,128},{64,192},{128,0},{192,64},{1,129},{65,193},{129,1},{193,65... | collective-permute-start | bytes 417800 | tf_op jit(solution)/shard_map/ppermute | solution.py:25
  5.9 16.1 %collective-permute-start.1 = (f32[136,256]{1,0:T(8,128)S(1)}, f32[136,256]{1,0:T(8,128)S(1)}, u32[]{:S(2)}, u32[]{:S(2)}) collective-permute-start(f32[136,256]{1,0:T(8,128)S(1)} %get-tuple-element.22), channel_id=1, source_target_pairs={{0,192},{64,0},{128,64},{192,128},{1,193},{65,1},{129,65},{193,129... | collective-permute-start | bytes 417800 | tf_op jit(solution)/shard_map/ppermute | solution.py:25
  6.8 15.2 %collective-permute-start = (f32[136,256]{1,0:T(8,128)S(1)}, f32[136,256]{1,0:T(8,128)S(1)}, u32[]{:S(2)}, u32[]{:S(2)}) collective-permute-start(f32[136,256]{1,0:T(8,128)S(1)} %get-tuple-element.22), channel_id=1, source_target_pairs={{0,64},{64,128},{128,192},{192,0},{1,65},{65,129},{129,193},{193,1... | collective-permute-start | bytes 417800 | tf_op jit(solution)/shard_map/ppermute | solution.py:25
  22.0 5.8 %collective-permute-start.3 = (f32[4,136,256]{2,1,0:T(8,128)S(1)}, f32[4,136,256]{2,1,0:T(8,128)S(1)}, u32[]{:S(2)}, u32[]{:S(2)}) collective-permute-start(f32[4,136,256]{2,1,0:T(8,128)S(1)} %pad_maximum_fusion.refs_0_), channel_id=1, source_target_pairs={{0,16},{16,0},{1,17},{17,1},{2,18},{18,2},{3,19},{19,3},{4,20},{20... | collective-permute-start | bytes 1671176 | tf_op jit(solution)/shard_map/ppermute | solution.py:25
  25.1 14.7 %collective-permute-start.5 = (f32[4,136,256]{2,1,0:T(8,128)S(1)}, f32[4,136,256]{2,1,0:T(8,128)S(1)}, u32[]{:S(2)}, u32[]{:S(2)}) collective-permute-start(f32[4,136,256]{2,1,0:T(8,128)S(1)} %pad_maximum_fusion.refs_0_), channel_id=1, source_target_pairs={{0,12},{4,0},{8,4},{12,8},{1,13},{5,1},{9,5},{13,9},{2,14},{6,2},{... | collective-permute-start | bytes 1671176 | tf_op jit(solution)/shard_map/ppermute | solution.py:25
  27.8 15.1 %collective-permute-start.4 = (f32[4,136,256]{2,1,0:T(8,128)S(1)}, f32[4,136,256]{2,1,0:T(8,128)S(1)}, u32[]{:S(2)}, u32[]{:S(2)}) collective-permute-start(f32[4,136,256]{2,1,0:T(8,128)S(1)} %pad_maximum_fusion.refs_0_), channel_id=1, source_target_pairs={{0,4},{4,8},{8,12},{12,0},{1,5},{5,9},{9,13},{13,1},{2,6},{6,10},{... | collective-permute-start | bytes 1671176 | tf_op jit(solution)/shard_map/ppermute | solution.py:25
  42.9 13.7 %collective-permute-start.6 = (f32[4,136,256]{2,1,0:T(8,128)S(1)}, f32[4,136,256]{2,1,0:T(8,128)S(1)}, u32[]{:S(2)}, u32[]{:S(2)}) collective-permute-start(f32[4,136,256]{2,1,0:T(8,128)S(1)} %collective-permute-done.4.refs_0_), channel_id=1, source_target_pairs={{0,16},{16,0},{1,17},{17,1},{2,18},{18,2},{3,19},{19,3},{4,20},{20... | collective-permute-start | bytes 1671176 | tf_op jit(solution)/shard_map/ppermute | solution.py:25
  44.2 12.4 %collective-permute-start.7 = (f32[4,136,256]{2,1,0:T(8,128)S(1)}, f32[4,136,256]{2,1,0:T(8,128)S(1)}, u32[]{:S(2)}, u32[]{:S(2)}) collective-permute-start(f32[4,136,256]{2,1,0:T(8,128)S(1)} %collective-permute-done.5.refs_1_), channel_id=1, source_target_pairs={{0,16},{16,0},{1,17},{17,1},{2,18},{18,2},{3,19},{19,3},{4,20},{20... | collective-permute-start | bytes 1671176 | tf_op jit(solution)/shard_map/ppermute | solution.py:25
  44.3 11.1 %collective-permute-start.9 = (f32[2,136,256]{2,1,0:T(8,128)S(1)}, f32[2,136,256]{2,1,0:T(8,128)S(1)}, u32[]{:S(2)}, u32[]{:S(2)}) collective-permute-start(f32[2,136,256]{2,1,0:T(8,128)S(1)} %slice.7), channel_id=1, source_target_pairs={{0,12},{4,0},{8,4},{12,8},{1,13},{5,1},{9,5},{13,9},{2,14},{6,2},{... | collective-permute-start | bytes 835592 | tf_op jit(solution)/shard_map/ppermute | solution.py:25
  44.4 11.1 %collective-permute-start.8 = (f32[2,136,256]{2,1,0:T(8,128)S(1)}, f32[2,136,256]{2,1,0:T(8,128)S(1)}, u32[]{:S(2)}, u32[]{:S(2)}) collective-permute-start(f32[2,136,256]{2,1,0:T(8,128)S(1)} %slice.6), channel_id=1, source_target_pairs={{0,4},{4,8},{8,12},{12,0},{1,5},{5,9},{9,13},{13,1},{2,6},{6,10},{... | collective-permute-start | bytes 835592 | tf_op jit(solution)/shard_map/ppermute | solution.py:25
  55.4 2.3 %collective-permute-start.10 = (f32[2,136,256]{2,1,0:T(8,128)S(1)}, f32[2,136,256]{2,1,0:T(8,128)S(1)}, u32[]{:S(2)}, u32[]{:S(2)}) collective-permute-start(f32[2,136,256]{2,1,0:T(8,128)S(1)} %collective-permute-done.8.refs_2_), channel_id=1, source_target_pairs={{0,16},{16,0},{1,17},{17,1},{2,18},{18,2},{3,19},{19,3},{4,20},{20... | collective-permute-start | bytes 835592 | tf_op jit(solution)/shard_map/ppermute | solution.py:25
  56.5 1.6 %collective-permute-start.11 = (f32[2,136,256]{2,1,0:T(8,128)S(1)}, f32[2,136,256]{2,1,0:T(8,128)S(1)}, u32[]{:S(2)}, u32[]{:S(2)}) collective-permute-start(f32[2,136,256]{2,1,0:T(8,128)S(1)} %collective-permute-done.9.refs_3_), channel_id=1, source_target_pairs={{0,16},{16,0},{1,17},{17,1},{2,18},{18,2},{3,19},{19,3},{4,20},{20... | collective-permute-start | bytes 835592 | tf_op jit(solution)/shard_map/ppermute | solution.py:25
  61.4 6.0 %collective-permute-start.12 = (f32[256,128]{1,0:T(8,128)S(1)}, f32[256,128]{1,0:T(8,128)S(1)}, u32[]{:S(2)}, u32[]{:S(2)}) collective-permute-start(f32[256,128]{1,0:T(8,128)S(1)} %get-tuple-element.38), channel_id=1, source_target_pairs={{0,32},{32,1},{1,33},{33,2},{2,34},{34,3},{3,35},{35,0},{4,36},{36... | collective-permute-start | bytes 393224 | tf_op jit(solution)/shard_map/ppermute | solution.py:34
  65.4 5.1 %collective-permute-start.16 = (f32[256,128]{1,0:T(8,128)S(1)}, f32[256,128]{1,0:T(8,128)S(1)}, u32[]{:S(2)}, u32[]{:S(2)}) collective-permute-start(f32[256,128]{1,0:T(8,128)S(1)} %ring_step.13), channel_id=1, source_target_pairs={{0,35},{32,0},{1,32},{33,1},{2,33},{34,2},{3,34},{35,3},{4,39},{36... | collective-permute-start | bytes 393224 | tf_op jit(solution)/shard_map/ppermute | solution.py:34
  70.4 5.8 %collective-permute-start.13 = (f32[256,128]{1,0:T(8,128)S(1)}, f32[256,128]{1,0:T(8,128)S(1)}, u32[]{:S(2)}, u32[]{:S(2)}) collective-permute-start(f32[256,128]{1,0:T(8,128)S(1)} %ring_step.10), channel_id=1, source_target_pairs={{0,32},{32,1},{1,33},{33,2},{2,34},{34,3},{3,35},{35,0},{4,36},{36... | collective-permute-start | bytes 393224 | tf_op jit(solution)/shard_map/ppermute | solution.py:34
  73.5 6.0 %collective-permute-start.17 = (f32[256,128]{1,0:T(8,128)S(1)}, f32[256,128]{1,0:T(8,128)S(1)}, u32[]{:S(2)}, u32[]{:S(2)}) collective-permute-start(f32[256,128]{1,0:T(8,128)S(1)} %ring_step.14), channel_id=1, source_target_pairs={{0,35},{32,0},{1,32},{33,1},{2,33},{34,2},{3,34},{35,3},{4,39},{36... | collective-permute-start | bytes 393224 | tf_op jit(solution)/shard_map/ppermute | solution.py:34
  79.3 6.0 %collective-permute-start.14 = (f32[256,128]{1,0:T(8,128)S(1)}, f32[256,128]{1,0:T(8,128)S(1)}, u32[]{:S(2)}, u32[]{:S(2)}) collective-permute-start(f32[256,128]{1,0:T(8,128)S(1)} %ring_step.11), channel_id=1, source_target_pairs={{0,32},{32,1},{1,33},{33,2},{2,34},{34,3},{3,35},{35,0},{4,36},{36... | collective-permute-start | bytes 393224 | tf_op jit(solution)/shard_map/ppermute | solution.py:34
  82.6 10.6 %collective-permute-start.18 = (f32[256,128]{1,0:T(8,128)S(1)}, f32[256,128]{1,0:T(8,128)S(1)}, u32[]{:S(2)}, u32[]{:S(2)}) collective-permute-start(f32[256,128]{1,0:T(8,128)S(1)} %ring_step.15), channel_id=1, source_target_pairs={{0,35},{32,0},{1,32},{33,1},{2,33},{34,2},{3,34},{35,3},{4,39},{36... | collective-permute-start | bytes 393224 | tf_op jit(solution)/shard_map/ppermute | solution.py:34
  88.3 5.1 %collective-permute-start.15 = (f32[256,128]{1,0:T(8,128)S(1)}, f32[256,128]{1,0:T(8,128)S(1)}, u32[]{:S(2)}, u32[]{:S(2)}) collective-permute-start(f32[256,128]{1,0:T(8,128)S(1)} %ring_step.12), channel_id=1, source_target_pairs={{0,32},{32,1},{1,33},{33,2},{2,34},{34,3},{3,35},{35,0},{4,36},{36... | collective-permute-start | bytes 393224 | tf_op jit(solution)/shard_map/ppermute | solution.py:34
  88.4 5.0 %copy-start.1 = (f32[128,256]{1,0:T(8,128)S(1)}, f32[128,256]{1,0:T(8,128)}, u32[]{:S(2)}) copy-start(f32[128,256]{1,0:T(8,128)} %direction_ref.3) | copy-start | bytes 393220
  88.4 5.0 %copy-start.2 = (f32[128,256]{1,0:T(8,128)S(1)}, f32[128,256]{1,0:T(8,128)}, u32[]{:S(2)}) copy-start(f32[128,256]{1,0:T(8,128)} %residual_ref.3) | copy-start | bytes 393220
  88.4 5.0 %copy-start.5 = (f32[256]{0:T(256)S(1)}, f32[256]{0:T(256)}, u32[]{:S(2)}) copy-start(f32[256]{0:T(256)} %param.6) | copy-start | bytes 3076
  88.4 29.8 %copy-start.3 = (f32[128,256]{1,0:T(8,128)S(1)}, f32[128,256]{1,0:T(8,128)}, u32[]{:S(2)}) copy-start(f32[128,256]{1,0:T(8,128)} %solution_ref.1) | copy-start | bytes 393220
  (1 other events, 0.7 us)
